TPU v7x, 128 devices: a whole 4x4x4 slice. The times are simulated.
128 devices in a mesh: xy: 32 (over z, x, core), lev: 4 (over y).
Axes of the slice: x: 4, y: 4, z: 4, core: 2. Of those that a mesh axis runs over, the one named last changes fastest.
Arguments:
- euler_field: float32 [8, 128, 256, 256], P(None, 'lev', 'xy'), may hold values from 0.1 to 3
- parcel_mass: float32 [8, 524288], P(None, ('xy', 'lev')), may hold values from 0.05 to 2
- dest_device: int32 [524288, 1], P(('xy', 'lev')), may hold values from 0 to 31; in each aligned block of 4096 rows (0 to 4095, 4096 to 8191, ...) at most 256 rows name the same one
- dest_cell: int32 [524288], P(('xy', 'lev')), may hold values from 0 to 65535
- diffusivity: float32 [128, 256, 256], P('lev', 'xy'), may hold values from 0.02 to 0.12
- wind_speed: float32 [128, 256, 256], P('lev', 'xy'), may hold values from 0 to 0.3
- inverses: float32 [8, 8, 16, 16], P('lev'), may hold values from -0.15 to 1
- lower_coupling: float32 [8, 8], P('lev'), may hold values from 0.3 to 1.5
- upper_coupling: float32 [8, 8], P('lev'), may hold values from 0.3 to 1.5
Outputs:
- dust_field: float32 [8, 128, 256, 256], P(None, 'lev', 'xy')
Inputs may be any that keep to these rules, and one draw needn't show every extreme that they name: `dest_device`: in the rows of one device no tile is named more than 256 times, a bound that some block reaches.
All inputs are finite; a program needn't handle non-finite values.
Results may differ from a plain program's by a relative error of at most 0.0003.
Values sent between devices are 32-bit elements; how exact they have to be, the bound alone decides.
A program may use at most 512 MiB of HBM per device.

v0:
```python
import math

import jax
import jax.numpy as jnp
from jax import lax
from jax.sharding import PartitionSpec as P

PRECISE = lax.Precision.HIGHEST


def with_halo(shard, sides, width):
    for axis, dim in sides:
        peers, length = (lax.axis_size(axis), shard.shape[dim])
        up = [(i, (i + 1) % peers) for i in range(peers - 1)]
        down = [(j, i) for i, j in up]
        last = lax.slice_in_dim(shard, length - width, length, axis=dim)
        first = lax.slice_in_dim(shard, 0, width, axis=dim)
        before = lax.ppermute(last, axis, up)
        after = lax.ppermute(first, axis, down)
        shard = jnp.concatenate([before, shard, after], axis=dim)
    return shard


def passed_along(value, axis, steps):
    count = lax.axis_size(axis)
    first, last = (max(0, -steps), min(count, count - steps))
    return lax.ppermute(value, axis, [(source, source + steps) for source in range(first, last)])


def horizontal(grid_field, diffusivity, wind_speed):
    extended = with_halo(grid_field, (("xy", 2),), 1)
    padded = jnp.pad(extended, ((0, 0), (0, 0), (0, 0), (1, 1)))
    centre = padded[:, :, 1:-1, 1:-1]
    lower_row = padded[:, :, :-2, 1:-1]
    laplace = (
        padded[:, :, 2:, 1:-1]
        + lower_row
        + padded[:, :, 1:-1, 2:]
        + padded[:, :, 1:-1, :-2]
        - 4.0 * centre
    )
    return centre + diffusivity * laplace - wind_speed * (centre - lower_row)


def pass_down(factor, offset):
    incoming = jnp.zeros_like(offset)
    for step_id in range(lax.axis_size("lev") - 1):
        incoming = passed_along(factor * incoming + offset, "lev", 1)
    return incoming


def pass_up(factor, offset):
    incoming = jnp.zeros_like(offset)
    for step_id in range(lax.axis_size("lev") - 1):
        incoming = passed_along(factor * incoming + offset, "lev", -1)
    return incoming


def vertical(grid_field, inverses, lower_coupling, upper_coupling):
    extent = grid_field.shape
    groups = inverses.shape[0]
    block_size = inverses.shape[2]
    columns = extent[2] * extent[3]
    values = grid_field.reshape(extent[0], groups, block_size, columns)
    carried = jnp.zeros((extent[0], columns), jnp.float32)
    factor = jnp.ones((extent[0], 1), jnp.float32)
    downward = []
    for group_id in range(groups):
        matrix = inverses[group_id]
        current = jnp.einsum("bkj,bjh->bkh", matrix, values[:, group_id], precision=PRECISE)
        current = (
            current
            + lower_coupling[group_id][:, None, None]
            * matrix[:, :, 0][:, :, None]
            * carried[:, None, :]
        )
        downward.append(current)
        carried = current[:, block_size - 1]
        factor = factor * (lower_coupling[group_id] * matrix[:, block_size - 1, 0])[:, None]
    correction = pass_down(factor, carried)
    for group_id in range(groups):
        matrix = inverses[group_id]
        scaled = lower_coupling[group_id][:, None] * correction
        downward[group_id] = downward[group_id] + matrix[:, :, 0][:, :, None] * scaled[:, None, :]
        correction = scaled * matrix[:, block_size - 1, 0][:, None]
    carried = jnp.zeros((extent[0], columns), jnp.float32)
    factor = jnp.ones((extent[0], 1), jnp.float32)
    upward = list(downward)
    for group_id in range(groups - 1, -1, -1):
        matrix = inverses[group_id]
        current = (
            downward[group_id]
            + upper_coupling[group_id][:, None, None]
            * matrix[:, :, block_size - 1][:, :, None]
            * carried[:, None, :]
        )
        upward[group_id] = current
        carried = current[:, 0]
        factor = factor * (upper_coupling[group_id] * matrix[:, 0, block_size - 1])[:, None]
    correction = pass_up(factor, carried)
    for group_id in range(groups - 1, -1, -1):
        matrix = inverses[group_id]
        scaled = upper_coupling[group_id][:, None] * correction
        upward[group_id] = (
            upward[group_id] + matrix[:, :, block_size - 1][:, :, None] * scaled[:, None, :]
        )
        correction = scaled * matrix[:, 0, block_size - 1][:, None]
    return jnp.stack(upward, axis=1).reshape(extent)


def split_rows(mass_rows, cells):
    first_part = mass_rows.astype(jnp.bfloat16)
    remainder = mass_rows - first_part.astype(jnp.float32)
    second_part = remainder.astype(jnp.bfloat16)
    third_part = (remainder - second_part.astype(jnp.float32)).astype(jnp.bfloat16)
    present = (cells >= 0).astype(jnp.bfloat16)[None, :]
    return jnp.concatenate([first_part, second_part, third_part, present], axis=0)


def project_cells(split, cells, high_count, low_count):
    high_ids = cells // low_count
    low_ids = cells % low_count
    high_table = (high_ids[None, :] == lax.broadcasted_iota(jnp.int32, (high_count, 1), 0)).astype(
        jnp.bfloat16
    )
    low_table = (low_ids[:, None] == lax.broadcasted_iota(jnp.int32, (1, low_count), 1)).astype(
        jnp.bfloat16
    )
    weighted = split[:, None, :] * high_table[None, :, :]
    return jnp.einsum("qhs,sl->qhl", weighted, low_table, preferred_element_type=jnp.float32)


def project_blocked(split, cells, high_count, low_count):
    slot_total = cells.shape[0]
    block_len = math.gcd(slot_total, 4096)
    block_count = slot_total // block_len
    row_count = split.shape[0]
    split_blocks = split.reshape(row_count, block_count, block_len).transpose(1, 0, 2)
    cell_blocks = cells.reshape(block_count, block_len)

    def accumulate(total, pair):
        return (total + project_cells(pair[0], pair[1], high_count, low_count), None)

    start_total = jnp.zeros((row_count, high_count, low_count), jnp.float32)
    summed, unused = lax.scan(accumulate, start_total, (split_blocks, cell_blocks))
    return summed


def combine_parts(projected, bin_count):
    deposit = (
        projected[0:bin_count]
        + projected[bin_count : 2 * bin_count]
        + projected[2 * bin_count : 3 * bin_count]
    )
    return (deposit, projected[3 * bin_count])


def place_slots(parcel_mass, dest_device, dest_cell, owners):
    bin_count = parcel_mass.shape[0]
    parcel_total = parcel_mass.shape[1]
    capacity = 2 * parcel_total // owners
    target = dest_device[:, 0]
    owner_table = (target[:, None] == lax.broadcasted_iota(jnp.int32, (1, owners), 1)).astype(
        jnp.bfloat16
    )
    block_len = math.gcd(parcel_total, 512)
    block_count = parcel_total // block_len
    owner_blocks = owner_table.reshape(block_count, block_len, owners)
    strict_lower = (
        lax.broadcasted_iota(jnp.int32, (block_len, block_len), 1)
        < lax.broadcasted_iota(jnp.int32, (block_len, block_len), 0)
    ).astype(jnp.bfloat16)
    inside_rank = jnp.einsum(
        "ij,bjo->bio", strict_lower, owner_blocks, preferred_element_type=jnp.float32
    )
    block_totals = jnp.sum(owner_blocks.astype(jnp.float32), axis=1)
    block_before = jnp.cumsum(block_totals, axis=0) - block_totals
    rank_table = inside_rank + block_before[:, None, :]
    rank_value = jnp.sum(rank_table * owner_blocks.astype(jnp.float32), axis=2).reshape(
        parcel_total
    )
    slot_index = target * capacity + rank_value.astype(jnp.int32)
    source = (
        jnp.full((owners * capacity,), parcel_total, jnp.int32)
        .at[slot_index]
        .set(jnp.arange(parcel_total, dtype=jnp.int32))
    )
    mass_padded = jnp.concatenate([parcel_mass, jnp.zeros((bin_count, 1), jnp.float32)], axis=1)
    cell_padded = jnp.concatenate([dest_cell, jnp.full((1,), -1, jnp.int32)], axis=0)
    return (mass_padded[:, source], cell_padded[source], capacity)


def deposit_parcels(parcel_mass, dest_device, dest_cell, high_count, low_count):
    owners = lax.axis_size("xy")
    bin_count = parcel_mass.shape[0]
    cell_count = high_count * low_count
    send_mass, send_cell, capacity = place_slots(parcel_mass, dest_device, dest_cell, owners)
    received = (
        lax.all_to_all(
            send_mass.reshape(bin_count, owners, capacity),
            "xy",
            split_axis=1,
            concat_axis=1,
            tiled=True,
        ),
        lax.all_to_all(
            send_cell.reshape(1, owners, capacity), "xy", split_axis=1, concat_axis=1, tiled=True
        ),
    )
    mass_in = received[0].reshape(bin_count, owners * capacity)
    cell_in = received[1].reshape(owners * capacity)
    split = split_rows(mass_in, cell_in)
    projected = project_blocked(split, cell_in, high_count, low_count)
    deposit, counts = combine_parts(projected, bin_count)
    return (deposit.reshape(bin_count, cell_count), counts.reshape(cell_count))


def shards(
    euler_field,
    parcel_mass,
    dest_device,
    dest_cell,
    diffusivity,
    wind_speed,
    inverses,
    lower_coupling,
    upper_coupling,
):
    first_step = horizontal(euler_field, diffusivity, wind_speed)
    extent = euler_field.shape
    high_count = extent[1] * extent[2]
    low_count = extent[3]
    deposit, counts = deposit_parcels(parcel_mass, dest_device, dest_cell, high_count, low_count)
    deposit = deposit.reshape(extent)
    counts = counts.reshape(extent[1:])
    weight_share = counts / (counts + 2.0)
    blended = (1.0 - weight_share) * first_step + weight_share * deposit
    after_first = vertical(blended, inverses, lower_coupling, upper_coupling)
    second_step = horizontal(after_first, diffusivity, wind_speed)
    return vertical(second_step, inverses, lower_coupling, upper_coupling)


def solution(mesh):
    placed = (
        P(None, "lev", "xy", None),
        P(None, ("xy", "lev")),
        P(("xy", "lev"), None),
        P(("xy", "lev")),
        P("lev", "xy", None),
        P("lev", "xy", None),
        P("lev", None, None, None),
        P("lev", None),
        P("lev", None),
    )
    return jax.shard_map(
        shards, mesh=mesh, in_specs=placed, out_specs=P(None, "lev", "xy", None), check_vma=False
    )
```

profile of v0, /device:TPU:0, one launch (start us, length us, event | category | flops | bytes accessed | tf_op | source)
XLA Modules:
  0.0 330.3 jit_solution(1200197495628855616)
XLA Ops:
  0.5 1.4 reduce.28
  2.5 0.7 compare_select_fusion.3
  3.3 15.5 %scatter_custom_fusion = s32[8192]{0:T(1024)S(1)} fusion(s32[4096]{0:T(1024)S(1)} %bitcast.181, s32[4096]{0:T(1024)S(1)} %iota.46, s32[]{:T(128)} %constant.79.clone.1), kind=kCustom, calls=%fused_computation.138 | custom fusion | bytes 32772 | tf_op jit(solution)/shard_map/scatter | solution.py:186
  18.9 0.7 pad_add_fusion
  19.6 80.5 %gather_fusion.1 = s32[8192]{0:T(1024)} fusion(s32[4097]{0:T(1024)S(1)} %pad_add_fusion, s32[8192]{0:T(1024)S(1)} %fusion.45), kind=kCustom, calls=%fused_computation.1 | custom fusion | bytes 98304 | tf_op jit(solution)/shard_map/gather | solution.py:190
  100.1 8.2 %all-to-all-start.1 = ((s32[1,32,256]{2,0,1:T(1,128)}), s32[1,32,256]{2,0,1:T(1,128)S(1)}, u32[]{:S(2)}, u32[]{:S(2)}) async-start(s32[1,32,256]{2,0,1:T(1,128)} %bitcast.5), calls=%async_computation.1 | async-start | bytes 65536 | tf_op jit(solution)/shard_map/all_to_all | solution.py:206
  108.4 3.5 %fusion.50 = (f32[8,32,1,256]{3,2,1,0:T(1,128)}, f32[8,32,1,256]{3,2,1,0:T(1,128)}) fusion(f32[8,32,8,256]{3,2,1,0:T(8,128)} %param.11), kind=kLoop, calls=%fused_computation.153 | loop fusion | bytes 1048576 | tf_op jit(solution)/shard_map/slice | solution.py:16
  111.8 1.3 collective-permute-start
  113.1 3.7 %collective-permute-start.1 = (f32[8,32,1,256]{3,2,1,0:T(1,128)}, f32[8,32,1,256]{3,2,1,0:T(1,128)}, u32[]{:S(2)}, u32[]{:S(2)}) collective-permute-start(f32[8,32,1,256]{3,2,1,0:T(1,128)} %get-tuple-element.122), channel_id=1, source_target_pairs={{0,4},{4,8},{8,12},{12,16},{16,20},{20,24},{24,28},{28,32},{32,36}... | collective-permute-start | bytes 786440 | tf_op jit(solution)/shard_map/ppermute | solution.py:18
  117.0 0.9 slice_reduce_fusion
  117.9 0.8 slice_reduce_fusion.4
  118.7 1.9 copy.30
  120.6 1.7 concatenate.28
  122.4 27.8 %gather_fusion = f32[8192,8]{1,0:T(8,128)} fusion(f32[8,4097]{0,1:T(8,128)S(1)} %concatenate.28, s32[8192]{0:T(1024)S(1)} %fusion.45), kind=kCustom, calls=%fused_computation | custom fusion | bytes 557056 | tf_op jit(solution)/shard_map/gather | solution.py:190
  150.2 3.5 %copy.31 = f32[8,32,256]{2,0,1:T(8,128)} copy(f32[8,32,256]{0,2,1:T(8,128)} %bitcast.169) | data formatting | bytes 524288 | tf_op jit(solution)/shard_map/reshape | solution.py:200
  153.7 0.8 copy.45
  154.4 9.7 %all-to-all-start = ((f32[8,32,256]{2,0,1:T(8,128)}), f32[8,32,256]{2,0,1:T(8,128)S(1)}, u32[]{:S(2)}, u32[]{:S(2)}) async-start(f32[8,32,256]{2,0,1:T(8,128)} %copy.31), calls=%async_computation | async-start | bytes 524288 | tf_op jit(solution)/shard_map/all_to_all | solution.py:199
  165.0 7.9 %all-to-all-done = f32[8,32,256]{2,0,1:T(8,128)S(1)} async-done(((f32[8,32,256]{2,0,1:T(8,128)}), f32[8,32,256]{2,0,1:T(8,128)S(1)}, u32[]{:S(2)}, u32[]{:S(2)}) %all-to-all-start) | async-done | bytes 262176 | tf_op jit(solution)/shard_map/all_to_all | solution.py:199
  173.5 0.6 maximum_bitcast_fusion
  174.4 39.1 %while.13 = (s32[]{:T(128)}, f32[25,256,256]{2,1,0:T(8,128)}, bf16[2,25,4096]{2,1,0:T(8,128)(2,1)S(1)}, s32[2,4096]{1,0:T(2,128)S(1)}, s32[]{:T(128)}, /*index=5*/s32[]{:T(128)}) while((s32[]{:T(128)}, f32[25,256,256]{2,1,0:T(8,128)}, bf16[2,25,4096]{2,1,0:T(8,128)(2,1)S(1)}, s32[2,4096]{1,0:T(2,128)S(1)}, s32[]{:T(128)}, ...), condition=%wide.region_5.6_spmd.clone, body=%wide.region_4.5_spmd.clone.sunk | while | flops 13454516224 | bytes 18030680 | solution.py:145
  175.0 18.1 %select_add_fusion.2 = f32[25,256,256]{2,1,0:T(8,128)} fusion(f32[25,256,256]{2,1,0:T(8,128)} %get-tuple-element.176, pred[]{:T(512)S(6)} %compare.41, bf16[256,4096]{1,0:T(8,128)(2,1)S(1)} %fusion.57, bf16[25,4096]{1,0:T(8,128)(2,1)S(1)} %dynamic-slice_bitcast_fusion.2, s32[4096]{0:T(1024)S(1)} %add_select_fusion.2), kind=kOutput, calls=%fused_computation.7.clone.1 | convolution fusion | flops 13452312576 | bytes 15425537 | tf_op jit(solution)/shard_map/while/body/eval_jaxpr/qhs,sl->qhl/dot_general | solution.py:130
  193.7 19.7 %select_add_fusion.2 = f32[25,256,256]{2,1,0:T(8,128)} fusion(f32[25,256,256]{2,1,0:T(8,128)} %get-tuple-element.176, pred[]{:T(512)S(6)} %compare.41, bf16[256,4096]{1,0:T(8,128)(2,1)S(1)} %fusion.57, bf16[25,4096]{1,0:T(8,128)(2,1)S(1)} %dynamic-slice_bitcast_fusion.2, s32[4096]{0:T(1024)S(1)} %add_select_fusion.2), kind=kOutput, calls=%fused_computation.7.clone.1 | convolution fusion | flops 13452312576 | bytes 15425537 | tf_op jit(solution)/shard_map/while/body/eval_jaxpr/qhs,sl->qhl/dot_general | solution.py:130
  213.4 1.0 broadcast_subtract_fusion
  214.5 5.6 %select_maximum_fusion.2 = f32[8,32,10,258]{3,2,1,0:T(8,128)S(1)} fusion(f32[8,32,1,256]{3,2,1,0:T(1,128)} %collective-permute-done, f32[8,32,8,256]{3,2,1,0:T(8,128)} %param.11, f32[8,32,1,256]{3,2,1,0:T(1,128)} %collective-permute-done.1), kind=kLoop, calls=%fused_computation.27 | loop fusion | flops 5283840 | bytes 5263360 | tf_op jit(solution)/shard_map/concatenate | solution.py:20
  220.2 4.3 %fusion.29 = f32[8,32,8,256]{3,2,1,0:T(8,128)} fusion(f32[8,32,8,256]{3,2,1,0:T(8,128)S(1)} %copy-done, f32[8,32,10,258]{3,2,1,0:T(8,128)S(1)} %select_maximum_fusion.2, f32[8,32,1,256]{3,2,1,0:T(1,128)} %collective-permute-done.1, f32[8,32,1,256]{3,2,1,0:T(1,128)} %collective-permute-done, f32[25,256,256]{2,1,0:T(8,128)S(1)} %copy-done.1, ...), kind=kLoop, calls=%fused_computation.53 | loop fusion | flops 8912896 | bytes 16252928 | tf_op jit(solution)/shard_map/add | solution.py:237
  224.5 2.0 reshape.217
  226.5 1.0 fusion.36
  227.7 1.0 fusion.16
  229.5 3.5 %collective-permute-start.2 = (f32[8,2048]{1,0:T(8,128)S(1)}, f32[8,2048]{1,0:T(8,128)S(1)}, u32[]{:S(2)}, u32[]{:S(2)}) collective-permute-start(f32[8,2048]{1,0:T(8,128)S(1)} %fusion.44), channel_id=1, source_target_pairs={{0,1},{1,2},{2,3},{4,5},{5,6},{6,7},{8,9},{9,10},{10,11},{12,13},{... | collective-permute-start | bytes 196616 | tf_op jit(solution)/shard_map/ppermute | solution.py:27
  233.0 1.9 collective-permute-done.2
  235.0 4.3 %collective-permute-start.3 = (f32[8,2048]{1,0:T(8,128)S(1)}, f32[8,2048]{1,0:T(8,128)S(1)}, u32[]{:S(2)}, u32[]{:S(2)}) collective-permute-start(f32[8,2048]{1,0:T(8,128)S(1)} %multiply_add_fusion.5), channel_id=1, source_target_pairs={{0,1},{1,2},{2,3},{4,5},{5,6},{6,7},{8,9},{9,10},{10,11},{12,13},{... | collective-permute-start | bytes 196616 | tf_op jit(solution)/shard_map/ppermute | solution.py:27
  239.2 1.9 collective-permute-done.3
  241.2 4.3 %collective-permute-start.4 = (f32[8,2048]{1,0:T(8,128)S(1)}, f32[8,2048]{1,0:T(8,128)S(1)}, u32[]{:S(2)}, u32[]{:S(2)}) collective-permute-start(f32[8,2048]{1,0:T(8,128)S(1)} %multiply_add_fusion.4), channel_id=1, source_target_pairs={{0,1},{1,2},{2,3},{4,5},{5,6},{6,7},{8,9},{9,10},{10,11},{12,13},{... | collective-permute-start | bytes 196616 | tf_op jit(solution)/shard_map/ppermute | solution.py:27
  245.5 1.8 collective-permute-done.4
  247.5 0.6 fusion.37
  248.6 1.3 collective-permute-start.5
  249.9 5.2 %collective-permute-done.5 = f32[8,2048]{1,0:T(8,128)S(1)} collective-permute-done((f32[8,2048]{1,0:T(8,128)S(1)}, f32[8,2048]{1,0:T(8,128)S(1)}, u32[]{:S(2)}, u32[]{:S(2)}) %collective-permute-start.5) | collective-permute-done | bytes 65568 | tf_op jit(solution)/shard_map/ppermute | solution.py:27
  255.2 1.3 collective-permute-start.6
  256.5 5.2 %collective-permute-done.6 = f32[8,2048]{1,0:T(8,128)S(1)} collective-permute-done((f32[8,2048]{1,0:T(8,128)S(1)}, f32[8,2048]{1,0:T(8,128)S(1)}, u32[]{:S(2)}, u32[]{:S(2)}) %collective-permute-start.6) | collective-permute-done | bytes 65568 | tf_op jit(solution)/shard_map/ppermute | solution.py:27
  261.8 1.3 collective-permute-start.7
  263.1 5.1 %collective-permute-done.7 = f32[8,2048]{1,0:T(8,128)S(1)} collective-permute-done((f32[8,2048]{1,0:T(8,128)S(1)}, f32[8,2048]{1,0:T(8,128)S(1)}, u32[]{:S(2)}, u32[]{:S(2)}) %collective-permute-start.7) | collective-permute-done | bytes 65568 | tf_op jit(solution)/shard_map/ppermute | solution.py:27
  268.7 0.7 add_bitcast_fusion.2
  269.8 0.9 copy.58
  271.1 1.3 collective-permute-start.8
  272.4 3.0 collective-permute-start.9
  275.5 1.1 collective-permute-done.9
  276.6 4.3 %select_maximum_fusion = f32[8,32,10,258]{3,2,1,0:T(8,128)S(1)} fusion(f32[8,32,1,256]{3,2,1,0:T(1,128)S(1)} %collective-permute-done.8, f32[8,32,8,256]{3,2,1,0:T(8,128)S(1)} %bitcast.165, f32[8,32,1,256]{3,2,1,0:T(1,128)S(1)} %collective-permute-done.9), kind=kLoop, calls=%fused_computation.25 | loop fusion | flops 5283840 | bytes 5263360 | tf_op jit(solution)/shard_map/concatenate | solution.py:20
  280.9 2.8 fusion.20
  283.7 1.7 reshape.219
  285.4 1.0 fusion.15
  286.7 1.5 fusion.14
  288.4 3.9 %collective-permute-start.10 = (f32[8,2048]{1,0:T(8,128)S(1)}, f32[8,2048]{1,0:T(8,128)S(1)}, u32[]{:S(2)}, u32[]{:S(2)}) collective-permute-start(f32[8,2048]{1,0:T(8,128)S(1)} %bitcast_add_fusion.6), channel_id=1, source_target_pairs={{0,1},{1,2},{2,3},{4,5},{5,6},{6,7},{8,9},{9,10},{10,11},{12,13},{... | collective-permute-start | bytes 196616 | tf_op jit(solution)/shard_map/ppermute | solution.py:27
  292.3 1.9 collective-permute-done.10
  294.3 4.3 %collective-permute-start.11 = (f32[8,2048]{1,0:T(8,128)S(1)}, f32[8,2048]{1,0:T(8,128)S(1)}, u32[]{:S(2)}, u32[]{:S(2)}) collective-permute-start(f32[8,2048]{1,0:T(8,128)S(1)} %bitcast_add_fusion.5), channel_id=1, source_target_pairs={{0,1},{1,2},{2,3},{4,5},{5,6},{6,7},{8,9},{9,10},{10,11},{12,13},{... | collective-permute-start | bytes 196616 | tf_op jit(solution)/shard_map/ppermute | solution.py:27
  298.5 2.3 collective-permute-done.11
  300.9 4.4 %collective-permute-start.12 = (f32[8,2048]{1,0:T(8,128)S(1)}, f32[8,2048]{1,0:T(8,128)S(1)}, u32[]{:S(2)}, u32[]{:S(2)}) collective-permute-start(f32[8,2048]{1,0:T(8,128)S(1)} %bitcast_add_fusion.4), channel_id=1, source_target_pairs={{0,1},{1,2},{2,3},{4,5},{5,6},{6,7},{8,9},{9,10},{10,11},{12,13},{... | collective-permute-start | bytes 196616 | tf_op jit(solution)/shard_map/ppermute | solution.py:27
  305.2 1.9 collective-permute-done.12
  307.9 1.3 collective-permute-start.13
  309.2 5.2 %collective-permute-done.13 = f32[8,2048]{1,0:T(8,128)S(1)} collective-permute-done((f32[8,2048]{1,0:T(8,128)S(1)}, f32[8,2048]{1,0:T(8,128)S(1)}, u32[]{:S(2)}, u32[]{:S(2)}) %collective-permute-start.13) | collective-permute-done | bytes 65568 | tf_op jit(solution)/shard_map/ppermute | solution.py:27
  314.5 1.3 collective-permute-start.14
  315.8 4.9 %collective-permute-done.14 = f32[8,2048]{1,0:T(8,128)S(1)} collective-permute-done((f32[8,2048]{1,0:T(8,128)S(1)}, f32[8,2048]{1,0:T(8,128)S(1)}, u32[]{:S(2)}, u32[]{:S(2)}) %collective-permute-start.14) | collective-permute-done | bytes 65568 | tf_op jit(solution)/shard_map/ppermute | solution.py:27
  320.7 1.3 collective-permute-start.15
  322.0 4.9 %collective-permute-done.15 = f32[8,2048]{1,0:T(8,128)S(1)} collective-permute-done((f32[8,2048]{1,0:T(8,128)S(1)}, f32[8,2048]{1,0:T(8,128)S(1)}, u32[]{:S(2)}, u32[]{:S(2)}) %collective-permute-start.15) | collective-permute-done | bytes 65568 | tf_op jit(solution)/shard_map/ppermute | solution.py:27
  328.1 2.2 copy.59
  (140 shorter events, 9.4 us)
Async XLA Ops:
  19.6 97.3 %copy-start.29 = (f32[2,8]{1,0:T(2,128)S(1)}, f32[2,8]{1,0:T(2,128)}, u32[]{:S(2)}) copy-start(f32[2,8]{1,0:T(2,128)} %param.19) | copy-start | bytes 196
  19.6 97.3 %copy-start.28 = (f32[2,8]{1,0:T(2,128)S(1)}, f32[2,8]{1,0:T(2,128)}, u32[]{:S(2)}) copy-start(f32[2,8]{1,0:T(2,128)} %param.18) | copy-start | bytes 196
  19.6 97.3 %copy-start.2 = (f32[2,8,16,16]{3,2,1,0:T(8,128)S(1)}, f32[2,8,16,16]{3,2,1,0:T(8,128)}, u32[]{:S(2)}) copy-start(f32[2,8,16,16]{3,2,1,0:T(8,128)} %param.17) | copy-start | bytes 49156
  19.6 99.1 %copy-start.6 = (f32[8,4096]{1,0:T(8,128)S(1)}, f32[8,4096]{1,0:T(8,128)}, u32[]{:S(2)}) copy-start(f32[8,4096]{1,0:T(8,128)} %param.12) | copy-start | bytes 393220
  100.1 54.3 %all-to-all-start.1 = ((s32[1,32,256]{2,0,1:T(1,128)}), s32[1,32,256]{2,0,1:T(1,128)S(1)}, u32[]{:S(2)}, u32[]{:S(2)}) async-start(s32[1,32,256]{2,0,1:T(1,128)} %bitcast.5), calls=%async_computation.1 | async-start | bytes 65536 | tf_op jit(solution)/shard_map/all_to_all | solution.py:206
  111.8 102.7 %collective-permute-start = (f32[8,32,1,256]{3,2,1,0:T(1,128)}, f32[8,32,1,256]{3,2,1,0:T(1,128)}, u32[]{:S(2)}, u32[]{:S(2)}) collective-permute-start(f32[8,32,1,256]{3,2,1,0:T(1,128)} %get-tuple-element.123), channel_id=1, source_target_pairs={{4,0},{8,4},{12,8},{16,12},{20,16},{24,20},{28,24},{32,28},{36,32}... | collective-permute-start | bytes 786440 | tf_op jit(solution)/shard_map/ppermute | solution.py:19
  113.1 101.4 %collective-permute-start.1 = (f32[8,32,1,256]{3,2,1,0:T(1,128)}, f32[8,32,1,256]{3,2,1,0:T(1,128)}, u32[]{:S(2)}, u32[]{:S(2)}) collective-permute-start(f32[8,32,1,256]{3,2,1,0:T(1,128)} %get-tuple-element.122), channel_id=1, source_target_pairs={{0,4},{4,8},{8,12},{12,16},{16,20},{20,24},{24,28},{28,32},{32,36}... | collective-permute-start | bytes 786440 | tf_op jit(solution)/shard_map/ppermute | solution.py:18
  116.9 1.8 copy-start.16
  116.9 1.8 copy-start.18
  116.9 1.8 copy-start.20
  116.9 1.7 copy-start.22
  118.7 45.5 %copy-start.25 = (f32[8]{0:T(128)}, f32[8]{0:T(128)S(1)}, u32[]{:S(2)}) copy-start(f32[8]{0:T(128)S(1)} %get-tuple-element.95) | copy-start | bytes 100
  154.4 18.4 %all-to-all-start = ((f32[8,32,256]{2,0,1:T(8,128)}), f32[8,32,256]{2,0,1:T(8,128)S(1)}, u32[]{:S(2)}, u32[]{:S(2)}) async-start(f32[8,32,256]{2,0,1:T(8,128)} %copy.31), calls=%async_computation | async-start | bytes 524288 | tf_op jit(solution)/shard_map/all_to_all | solution.py:199
  213.4 6.7 %copy-start.5 = (f32[32,8,256]{2,1,0:T(8,128)S(1)}, f32[32,8,256]{2,1,0:T(8,128)}, u32[]{:S(2)}) copy-start(f32[32,8,256]{2,1,0:T(8,128)} %param.15) | copy-start | bytes 786436
  214.5 5.7 %copy-start = (f32[8,32,8,256]{3,2,1,0:T(8,128)S(1)}, f32[8,32,8,256]{3,2,1,0:T(8,128)}, u32[]{:S(2)}) copy-start(f32[8,32,8,256]{3,2,1,0:T(8,128)} %param.11) | copy-start | bytes 6291460
  214.5 5.7 %copy-start.4 = (f32[32,8,256]{2,1,0:T(8,128)S(1)}, f32[32,8,256]{2,1,0:T(8,128)}, u32[]{:S(2)}) copy-start(f32[32,8,256]{2,1,0:T(8,128)} %param.16) | copy-start | bytes 786436
  214.5 5.6 %copy-start.1 = (f32[25,256,256]{2,1,0:T(8,128)S(1)}, f32[25,256,256]{2,1,0:T(8,128)}, u32[]{:S(2)}) copy-start(f32[25,256,256]{2,1,0:T(8,128)} %get-tuple-element.61) | copy-start | bytes 19660804
  224.5 2.0 copy-start.3
  226.5 1.0 copy-start.14
  226.5 2.3 copy-start.11
  227.6 1.9 copy-start.27
  227.6 7.3 %copy-start.15 = (f32[8]{0:T(128)S(1)}, f32[8]{0:T(128)}, u32[]{:S(2)}) copy-start(f32[8]{0:T(128)} %get-tuple-element.117) | copy-start | bytes 100
  227.6 17.9 %copy-start.24 = (f32[8]{0:T(128)S(1)}, f32[8]{0:T(128)}, u32[]{:S(2)}) copy-start(f32[8]{0:T(128)} %get-tuple-element.139) | copy-start | bytes 100
  227.6 17.9 %copy-start.30 = (f32[2,8]{1,0:T(2,128)S(1)}, f32[2,8]{1,0:T(2,128)}, u32[]{:S(2)}) copy-start(f32[2,8]{1,0:T(2,128)} %param.19) | copy-start | bytes 196
  227.6 17.9 %copy-start.31 = (f32[8]{0:T(128)S(1)}, f32[8]{0:T(128)}, u32[]{:S(2)}) copy-start(f32[8]{0:T(128)} %get-tuple-element.94) | copy-start | bytes 100
  227.6 19.7 %copy-start.21 = (f32[8]{0:T(128)S(1)}, f32[8]{0:T(128)}, u32[]{:S(2)}) copy-start(f32[8]{0:T(128)} %copy-done.20) | copy-start | bytes 100
  227.6 19.7 %copy-start.23 = (f32[8]{0:T(128)S(1)}, f32[8]{0:T(128)}, u32[]{:S(2)}) copy-start(f32[8]{0:T(128)} %copy-done.22) | copy-start | bytes 100
  227.6 19.7 %copy-start.26 = (f32[8]{0:T(128)S(1)}, f32[8]{0:T(128)}, u32[]{:S(2)}) copy-start(f32[8]{0:T(128)} %copy-done.25) | copy-start | bytes 100
  228.7 18.8 %copy-start.7 = (f32[8,16]{1,0:T(8,128)S(1)}, f32[8,16]{1,0:T(8,128)}, u32[]{:S(2)}) copy-start(f32[8,16]{1,0:T(8,128)} %get-tuple-element.90) | copy-start | bytes 1540
  228.7 18.8 %copy-start.8 = (f32[8,16]{1,0:T(8,128)S(1)}, f32[8,16]{1,0:T(8,128)}, u32[]{:S(2)}) copy-start(f32[8,16]{1,0:T(8,128)} %get-tuple-element.91) | copy-start | bytes 1540
  229.4 18.8 %copy-start.9 = (f32[8,16]{1,0:T(8,128)S(1)}, f32[8,16]{1,0:T(8,128)}, u32[]{:S(2)}) copy-start(f32[8,16]{1,0:T(8,128)} %get-tuple-element.135) | copy-start | bytes 1540
  229.4 18.8 %copy-start.10 = (f32[8,16]{1,0:T(8,128)S(1)}, f32[8,16]{1,0:T(8,128)}, u32[]{:S(2)}) copy-start(f32[8,16]{1,0:T(8,128)} %get-tuple-element.136) | copy-start | bytes 1540
  229.5 5.4 %collective-permute-start.2 = (f32[8,2048]{1,0:T(8,128)S(1)}, f32[8,2048]{1,0:T(8,128)S(1)}, u32[]{:S(2)}, u32[]{:S(2)}) collective-permute-start(f32[8,2048]{1,0:T(8,128)S(1)} %fusion.44), channel_id=1, source_target_pairs={{0,1},{1,2},{2,3},{4,5},{5,6},{6,7},{8,9},{9,10},{10,11},{12,13},{... | collective-permute-start | bytes 196616 | tf_op jit(solution)/shard_map/ppermute | solution.py:27
  235.0 6.2 %collective-permute-start.3 = (f32[8,2048]{1,0:T(8,128)S(1)}, f32[8,2048]{1,0:T(8,128)S(1)}, u32[]{:S(2)}, u32[]{:S(2)}) collective-permute-start(f32[8,2048]{1,0:T(8,128)S(1)} %multiply_add_fusion.5), channel_id=1, source_target_pairs={{0,1},{1,2},{2,3},{4,5},{5,6},{6,7},{8,9},{9,10},{10,11},{12,13},{... | collective-permute-start | bytes 196616 | tf_op jit(solution)/shard_map/ppermute | solution.py:27
  241.2 6.1 %collective-permute-start.4 = (f32[8,2048]{1,0:T(8,128)S(1)}, f32[8,2048]{1,0:T(8,128)S(1)}, u32[]{:S(2)}, u32[]{:S(2)}) collective-permute-start(f32[8,2048]{1,0:T(8,128)S(1)} %multiply_add_fusion.4), channel_id=1, source_target_pairs={{0,1},{1,2},{2,3},{4,5},{5,6},{6,7},{8,9},{9,10},{10,11},{12,13},{... | collective-permute-start | bytes 196616 | tf_op jit(solution)/shard_map/ppermute | solution.py:27
  248.1 20.1 %copy-start.17 = (f32[8]{0:T(128)S(1)}, f32[8]{0:T(128)}, u32[]{:S(2)}) copy-start(f32[8]{0:T(128)} %copy-done.16) | copy-start | bytes 100
  248.1 20.1 %copy-start.19 = (f32[8]{0:T(128)S(1)}, f32[8]{0:T(128)}, u32[]{:S(2)}) copy-start(f32[8]{0:T(128)} %copy-done.18) | copy-start | bytes 100
  248.1 20.1 %copy-start.13 = (f32[8,16]{1,0:T(8,128)S(1)}, f32[8,16]{1,0:T(8,128)}, u32[]{:S(2)}) copy-start(f32[8,16]{1,0:T(8,128)} %get-tuple-element.137) | copy-start | bytes 1540
  248.5 20.1 %copy-start.12 = (f32[8,16]{1,0:T(8,128)S(1)}, f32[8,16]{1,0:T(8,128)}, u32[]{:S(2)}) copy-start(f32[8,16]{1,0:T(8,128)} %get-tuple-element.89) | copy-start | bytes 1540
  248.6 6.5 %collective-permute-start.5 = (f32[8,2048]{1,0:T(8,128)S(1)}, f32[8,2048]{1,0:T(8,128)S(1)}, u32[]{:S(2)}, u32[]{:S(2)}) collective-permute-start(f32[8,2048]{1,0:T(8,128)S(1)} %fusion.43), channel_id=1, source_target_pairs={{1,0},{2,1},{3,2},{5,4},{6,5},{7,6},{9,8},{10,9},{11,10},{13,12},{... | collective-permute-start | bytes 196616 | tf_op jit(solution)/shard_map/ppermute | solution.py:27
  255.2 6.5 %collective-permute-start.6 = (f32[8,2048]{1,0:T(8,128)S(1)}, f32[8,2048]{1,0:T(8,128)S(1)}, u32[]{:S(2)}, u32[]{:S(2)}) collective-permute-start(f32[8,2048]{1,0:T(8,128)S(1)} %multiply_add_fusion.3), channel_id=1, source_target_pairs={{1,0},{2,1},{3,2},{5,4},{6,5},{7,6},{9,8},{10,9},{11,10},{13,12},{... | collective-permute-start | bytes 196616 | tf_op jit(solution)/shard_map/ppermute | solution.py:27
  261.8 6.3 %collective-permute-start.7 = (f32[8,2048]{1,0:T(8,128)S(1)}, f32[8,2048]{1,0:T(8,128)S(1)}, u32[]{:S(2)}, u32[]{:S(2)}) collective-permute-start(f32[8,2048]{1,0:T(8,128)S(1)} %multiply_add_fusion.2), channel_id=1, source_target_pairs={{1,0},{2,1},{3,2},{5,4},{6,5},{7,6},{9,8},{10,9},{11,10},{13,12},{... | collective-permute-start | bytes 196616 | tf_op jit(solution)/shard_map/ppermute | solution.py:27
  271.1 4.4 %collective-permute-start.8 = (f32[8,32,1,256]{3,2,1,0:T(1,128)S(1)}, f32[8,32,1,256]{3,2,1,0:T(1,128)S(1)}, u32[]{:S(2)}, u32[]{:S(2)}) collective-permute-start(f32[8,32,1,256]{3,2,1,0:T(1,128)S(1)} %get-tuple-element.121), channel_id=1, source_target_pairs={{4,0},{8,4},{12,8},{16,12},{20,16},{24,20},{28,24},{32,28},{36,32}... | collective-permute-start | bytes 786440 | tf_op jit(solution)/shard_map/ppermute | solution.py:19
  272.4 4.2 %collective-permute-start.9 = (f32[8,32,1,256]{3,2,1,0:T(1,128)S(1)}, f32[8,32,1,256]{3,2,1,0:T(1,128)S(1)}, u32[]{:S(2)}, u32[]{:S(2)}) collective-permute-start(f32[8,32,1,256]{3,2,1,0:T(1,128)S(1)} %get-tuple-element.120), channel_id=1, source_target_pairs={{0,4},{4,8},{8,12},{12,16},{16,20},{20,24},{24,28},{28,32},{32,36}... | collective-permute-start | bytes 786440 | tf_op jit(solution)/shard_map/ppermute | solution.py:18
  288.4 5.8 %collective-permute-start.10 = (f32[8,2048]{1,0:T(8,128)S(1)}, f32[8,2048]{1,0:T(8,128)S(1)}, u32[]{:S(2)}, u32[]{:S(2)}) collective-permute-start(f32[8,2048]{1,0:T(8,128)S(1)} %bitcast_add_fusion.6), channel_id=1, source_target_pairs={{0,1},{1,2},{2,3},{4,5},{5,6},{6,7},{8,9},{9,10},{10,11},{12,13},{... | collective-permute-start | bytes 196616 | tf_op jit(solution)/shard_map/ppermute | solution.py:27
  294.3 6.5 %collective-permute-start.11 = (f32[8,2048]{1,0:T(8,128)S(1)}, f32[8,2048]{1,0:T(8,128)S(1)}, u32[]{:S(2)}, u32[]{:S(2)}) collective-permute-start(f32[8,2048]{1,0:T(8,128)S(1)} %bitcast_add_fusion.5), channel_id=1, source_target_pairs={{0,1},{1,2},{2,3},{4,5},{5,6},{6,7},{8,9},{9,10},{10,11},{12,13},{... | collective-permute-start | bytes 196616 | tf_op jit(solution)/shard_map/ppermute | solution.py:27
  300.9 6.3 %collective-permute-start.12 = (f32[8,2048]{1,0:T(8,128)S(1)}, f32[8,2048]{1,0:T(8,128)S(1)}, u32[]{:S(2)}, u32[]{:S(2)}) collective-permute-start(f32[8,2048]{1,0:T(8,128)S(1)} %bitcast_add_fusion.4), channel_id=1, source_target_pairs={{0,1},{1,2},{2,3},{4,5},{5,6},{6,7},{8,9},{9,10},{10,11},{12,13},{... | collective-permute-start | bytes 196616 | tf_op jit(solution)/shard_map/ppermute | solution.py:27
  307.9 6.5 %collective-permute-start.13 = (f32[8,2048]{1,0:T(8,128)S(1)}, f32[8,2048]{1,0:T(8,128)S(1)}, u32[]{:S(2)}, u32[]{:S(2)}) collective-permute-start(f32[8,2048]{1,0:T(8,128)S(1)} %bitcast_add_fusion.3), channel_id=1, source_target_pairs={{1,0},{2,1},{3,2},{5,4},{6,5},{7,6},{9,8},{10,9},{11,10},{13,12},{... | collective-permute-start | bytes 196616 | tf_op jit(solution)/shard_map/ppermute | solution.py:27
  314.5 6.1 %collective-permute-start.14 = (f32[8,2048]{1,0:T(8,128)S(1)}, f32[8,2048]{1,0:T(8,128)S(1)}, u32[]{:S(2)}, u32[]{:S(2)}) collective-permute-start(f32[8,2048]{1,0:T(8,128)S(1)} %bitcast_add_fusion.2), channel_id=1, source_target_pairs={{1,0},{2,1},{3,2},{5,4},{6,5},{7,6},{9,8},{10,9},{11,10},{13,12},{... | collective-permute-start | bytes 196616 | tf_op jit(solution)/shard_map/ppermute | solution.py:27
  320.7 6.1 %collective-permute-start.15 = (f32[8,2048]{1,0:T(8,128)S(1)}, f32[8,2048]{1,0:T(8,128)S(1)}, u32[]{:S(2)}, u32[]{:S(2)}) collective-permute-start(f32[8,2048]{1,0:T(8,128)S(1)} %bitcast_add_fusion.1), channel_id=1, source_target_pairs={{1,0},{2,1},{3,2},{5,4},{6,5},{7,6},{9,8},{10,9},{11,10},{13,12},{... | collective-permute-start | bytes 196616 | tf_op jit(solution)/shard_map/ppermute | solution.py:27
where the time goes:
time: 336 us; the launch traced here: 330 us
  local copies, waits for them, and re-layouts  145 us (43%)
  starting transfers between devices  59.5 us (18%)
  waiting for transfers between devices  51.1 us (15%)
  matrix products  42.8 us (13%)
  other arithmetic  30.4 us (9%)
    gather x2, local copies, waits for them, and re-layouts, place_slots(): return (mass_padded[:, source], cell_padded[source], capacity)  108 us
    ppermute x12, waiting for transfers between devices, passed_along(): lax.ppermute(value, axis, [(source, source + steps) for source in range(f...  42.1 us
    dot_general x2, matrix products, project_cells(): jnp.einsum('qhs,sl->qhl', weighted, low_table, preferred_element_type=jnp...  37.9 us
    ppermute x12, starting transfers between devices, passed_along(): lax.ppermute(value, axis, [(source, source + steps) for source in range(f...  32.2 us
    scatter x1, local copies, waits for them, and re-layouts, place_slots(): source = jnp.full((owners * capacity,), parcel_total, jnp.int32).at[slot_...  15.5 us
    concatenate x2, other arithmetic, with_halo(): shard = jnp.concatenate([before, shard, after], axis=dim)  9.86 us
    all_to_all x1, starting transfers between devices, deposit_parcels(): lax.all_to_all(send_mass.reshape(bin_count, owners, capacity), 'xy', spli...  9.71 us
    all_to_all x1, starting transfers between devices, deposit_parcels(): lax.all_to_all(send_cell.reshape(1, owners, capacity), 'xy', split_axis=1...  8.25 us
  transfers between devices with their start and end apart: 18, of which 14 were waited for; matrix products, arithmetic and copies ran while one was open for 25% of the time, Pallas kernels for 0%

commit v1 on v0

v1 whole, which is shorter than its diff:
```python
import functools

import jax
import jax.numpy as jnp
from jax import lax
from jax.experimental import pallas as pl
from jax.experimental.pallas import tpu as pltpu
from jax.sharding import PartitionSpec as P

F32, BF16, I32 = jnp.float32, jnp.bfloat16, jnp.int32
MESH = pl.DeviceIdType.MESH
N_XY, N_LEV, BINS, LEV, GX, GY = 32, 4, 8, 32, 8, 256
ROWS = BINS * LEV
PARC, CAP, BLK = 4096, 256, 256
BUCKETS = 16
NT = (((1,), (1,)), ((), ()))
LIMIT = 50 << 20


def iota(shape, dim, dtype=F32):
    return lax.broadcasted_iota(I32, shape, dim).astype(dtype)


def ranks(keys, count, lower):
    n = keys.shape[0]
    masks = [jnp.where(keys == k, 1.0, 0.0) for k in range(count)]
    stack = jnp.concatenate(masks, axis=0).astype(BF16)
    before = (iota((BLK, BLK), 0) < iota((BLK, BLK), 1)).astype(BF16)
    inside = jnp.dot(stack, before, preferred_element_type=F32)
    totals = jnp.dot(stack, jnp.ones((BLK, 128), BF16), preferred_element_type=F32)
    base = jnp.dot(lower, totals.astype(BF16), preferred_element_type=F32)
    wide = jnp.concatenate([base, base], axis=1)
    whole = inside + wide
    position = jnp.zeros(keys.shape, F32)
    for k in range(count):
        position += masks[k] * whole[k * n : (k + 1) * n]
    return position, base


def sort_block(values16, high_low, column, target, slot, out_rows, out_codes):
    chosen = jnp.broadcast_to(target, (16, BLK)).astype(BF16)
    zero = jnp.zeros((16, BLK), BF16)
    parts = [jnp.where(chosen == jnp.array(d, BF16), values16, zero) for d in range(32)]
    weighted = jnp.concatenate(parts, axis=0)
    mine = iota((32, BLK), 0) == target
    codes = jnp.concatenate(
        [jnp.where(mine, high_low, 0.0), jnp.where(mine, column, 0.0)], axis=0
    ).astype(BF16)
    spot = one_hot(slot)
    out_rows[...] += lax.dot_general(weighted, spot, NT, preferred_element_type=F32)
    out_codes[...] += lax.dot_general(codes, spot, NT, preferred_element_type=F32)


def one_hot(row):
    wide = jnp.broadcast_to(row, (BLK, BLK)).astype(BF16)
    ids = iota((BLK, BLK), 0, BF16)
    return jnp.where(ids == wide, jnp.ones((BLK, BLK), BF16), jnp.zeros((BLK, BLK), BF16))


def two_parts(values):
    high = values.astype(BF16).astype(F32)
    return jnp.concatenate([high, values - high], axis=0).astype(BF16)


def stencil(centre, before, after, diffusivity, wind):
    shape = (BINS, LEV, GY)
    lane = lax.broadcasted_iota(I32, (ROWS, GY), 1)
    left = jnp.where(lane == 0, 0.0, pltpu.roll(centre, 1, 1))
    right = jnp.where(lane == GY - 1, 0.0, pltpu.roll(centre, GY - 1, 1))
    laplace = (after + before + right + left - 4.0 * centre).reshape(shape)
    drift = (centre - before).reshape(shape)
    result = centre.reshape(shape) + diffusivity[None] * laplace - wind[None] * drift
    return result.reshape(ROWS, GY)


def plane_copies(source, target, sems, at=0):
    return [pltpu.make_async_copy(source.at[:, x, :], target.at[at + x], sems.at[x]) for x in range(GX)]


def remote(src, dst, send, recv, device):
    return pltpu.make_async_remote_copy(
        src_ref=src, dst_ref=dst, send_sem=send, recv_sem=recv, device_id=device, device_id_type=MESH
    )


def compose(inv, low, up, hi_ref, lo_ref, p_ref, e_ref):
    lane16 = lax.broadcasted_iota(I32, (16, ROWS), 1) % LEV
    row16 = lax.broadcasted_iota(I32, (16, ROWS), 0)
    own = lax.broadcasted_iota(I32, (BINS, 16, ROWS), 0) == (
        lax.broadcasted_iota(I32, (BINS, 16, ROWS), 2) // LEV
    )

    def spread(group):
        place = (lane16 == row16 + 16 * group).astype(F32)
        flat = inv[group].reshape(BINS * 16, 16)
        full = jnp.dot(flat, place, precision=lax.Precision.HIGHEST, preferred_element_type=F32)
        return jnp.where(own, full.reshape(BINS, 16, ROWS), 0.0)

    def per_bin(ref, group):
        wide = jnp.broadcast_to(ref[group : group + 1, :].reshape(1, 1, BINS), (BINS, 1, BINS))
        same = lax.broadcasted_iota(I32, (BINS, 1, BINS), 0) == lax.broadcasted_iota(
            I32, (BINS, 1, BINS), 2
        )
        return jnp.sum(jnp.where(same, wide, 0.0), axis=2, keepdims=True)

    t0, t1 = spread(0), spread(1)
    l0, l1, u0, u1 = per_bin(low, 0), per_bin(low, 1), per_bin(up, 0), per_bin(up, 1)
    m0, m1 = inv[0], inv[1]
    m0_first, m0_last = m0[:, :, 0:1], m0[:, :, 15:16]
    m1_first, m1_last = m1[:, :, 0:1], m1[:, :, 15:16]
    tail0 = t0[:, 15:16, :]
    link = (l1 * m1[:, 0:1, 0:1]) * tail0 + t1[:, 0:1, :]
    p0 = t0 + (u0 * m0_last) * link
    p1 = t1 + (l1 * m1_first) * tail0
    full = jnp.concatenate([p0, p1], axis=1).reshape(ROWS, ROWS)
    high = full.astype(BF16)
    hi_ref[...] = high
    lo_ref[...] = (full - high.astype(F32)).astype(BF16)
    passed = l1 * l0 * m0[:, 15:16, 0:1]
    c0 = l0 * m0_first + (u0 * m0_last) * (passed * m1[:, 0:1, 0:1])
    c1 = passed * m1_first
    d0 = (u0 * u1 * m1[:, 0:1, 15:16]) * m0_last
    d1 = u1 * m1_last
    p_ref[...] = jnp.broadcast_to(jnp.concatenate([c0, c1], axis=1), (BINS, LEV, 128)).reshape(ROWS, 128)
    e_ref[...] = jnp.broadcast_to(jnp.concatenate([d0, d1], axis=1), (BINS, LEV, 128)).reshape(ROWS, 128)


def carry_factors(level, all_ref, out_ref):
    alpha = [all_ref[f, 0] for f in range(N_LEV)]
    beta = [all_ref[f, 1] for f in range(N_LEV)]
    gamma = [all_ref[f, 2] for f in range(N_LEV)]
    zero, one = jnp.zeros((BINS, 128), F32), jnp.ones((BINS, 128), F32)
    for f in range(N_LEV):
        down, product = zero, one
        for i in range(f + 1, N_LEV):
            down = jnp.where(level == i, product, down)
            product = product * alpha[i]
        upward, product = zero, one
        for i in range(f - 1, -1, -1):
            upward = jnp.where(level == i, product, upward)
            product = product * beta[i]
        out_ref[f] = down
        out_ref[N_LEV + f] = upward
    sigma = [zero] * N_LEV
    for f in range(N_LEV - 1, 0, -1):
        sigma[f - 1] = gamma[f] + beta[f] * alpha[f] * sigma[f]

    def own(values):
        result = values[0]
        for f in range(1, N_LEV):
            result = jnp.where(level == f, values[f], result)
        return result

    out_ref[8] = own(sigma)
    out_ref[9] = own([sigma[f] * alpha[f] for f in range(N_LEV)])
    out_ref[10] = own([sigma[f] * beta[f] for f in range(N_LEV)])


def route_kernel(
    euler, mass, dest, cell, diffusivity, wind, inv, low, up,
    first, got_mass, got_code, p_high, p_low, p_col, e_col, factors,
    ext, diff_s, wind_s, rows_acc, codes_acc, send_mass, send_code, dest_s, slot_s, hl_s, col_s, links,
    load_sem, halo_send, halo_recv, mass_send, mass_recv, code_send, code_recv, link_send, link_recv,
):
    me, level = lax.axis_index("xy"), lax.axis_index("lev")
    barrier = pltpu.get_barrier_semaphore()

    def greet(k, unused):
        pl.semaphore_signal(
            barrier, inc=1, device_id={"xy": lax.rem(me + k, N_XY), "lev": level}, device_id_type=MESH
        )
        return unused

    lax.fori_loop(1, N_XY, greet, 0)
    for k in range(1, N_LEV):
        pl.semaphore_signal(
            barrier, inc=1, device_id={"xy": me, "lev": lax.rem(level + k, N_LEV)}, device_id_type=MESH
        )

    loads = plane_copies(euler, ext, load_sem.at[0], 1)
    loads += plane_copies(diffusivity, diff_s, load_sem.at[1]) + plane_copies(wind, wind_s, load_sem.at[2])
    for copy in loads:
        copy.start()

    def wide(ref):
        return jnp.concatenate([ref[pl.ds(0, 16, stride=2), :], ref[pl.ds(1, 16, stride=2), :]], axis=1)

    target = wide(dest).astype(F32)
    cells = wide(cell)
    levels = cells // (GX * GY)
    xs = (cells // GY) % GX
    bucket = xs * 2 + levels // 16
    dest_s[...] = target
    hl_s[...] = (bucket * 16 + levels % 16 + 1).astype(F32)
    col_s[...] = (cells % GY).astype(F32)
    r, c = (lax.broadcasted_iota(I32, (512, 512), d) for d in (0, 1))
    lower = jnp.where((c < r) & (c // 16 == r // 16), 1.0, 0.0).astype(BF16)
    slot, unused_base = ranks(target, N_XY, lower)
    slot_s[...] = slot

    for copy in loads:
        copy.wait()
    pl.semaphore_wait(barrier, N_XY - 1 + N_LEV - 1)
    above, below = lax.rem(me + 1, N_XY), lax.rem(me + N_XY - 1, N_XY)
    up_copy = remote(ext.at[GX], ext.at[0], halo_send.at[0], halo_recv.at[0], {"xy": above, "lev": level})
    down_copy = remote(ext.at[1], ext.at[GX + 1], halo_send.at[1], halo_recv.at[1], {"xy": below, "lev": level})
    up_copy.start()
    down_copy.start()

    rows_acc[...] = jnp.zeros_like(rows_acc)
    codes_acc[...] = jnp.zeros_like(codes_acc)

    def one_block(i, unused):
        lanes = pl.ds(pl.multiple_of(i * BLK, BLK), BLK)
        row = pl.ds(i, 1)
        sort_block(
            two_parts(mass[:, lanes]), hl_s[row, :], col_s[row, :], dest_s[row, :], slot_s[row, :],
            rows_acc, codes_acc,
        )
        return unused

    lax.fori_loop(0, PARC // BLK, one_block, 0)
    table = rows_acc[...].reshape(N_XY, 16, CAP)
    send_mass[...] = table[:, :8] + table[:, 8:]
    send_code[...] = codes_acc[0:32] * 256.0 + codes_acc[32:64]

    def copies(other, slot_id):
        device = {"xy": other, "lev": level}
        return (
            remote(send_mass.at[other], got_mass.at[slot_id], mass_send.at[other], mass_recv.at[slot_id], device),
            remote(
                send_code.at[pl.ds(other, 1)], got_code.at[pl.ds(slot_id, 1)],
                code_send.at[other], code_recv.at[slot_id], device,
            ),
        )

    def send(k, unused):
        for copy in copies(lax.rem(me + k, N_XY), me):
            copy.start()
        return unused

    lax.fori_loop(1, N_XY, send, 0)
    got_mass[me] = send_mass[me]
    got_code[pl.ds(me, 1), :] = send_code[pl.ds(me, 1), :]

    compose(inv, low, up, p_high, p_low, p_col, e_col)
    links[level, 0] = p_col[pl.ds(LEV - 1, BINS, stride=LEV), :]
    links[level, 1] = e_col[pl.ds(0, BINS, stride=LEV), :]
    links[level, 2] = p_col[pl.ds(0, BINS, stride=LEV), :]

    def link_copy(k, owner):
        peer = lax.rem(level + k, N_LEV)
        return remote(
            links.at[owner], links.at[owner], link_send.at[k], link_recv.at[k], {"xy": me, "lev": peer}
        )

    for k in range(1, N_LEV):
        link_copy(k, level).start()

    up_copy.wait()
    down_copy.wait()

    @pl.when(me == 0)
    def _():
        ext[0] = jnp.zeros((ROWS, GY), F32)

    @pl.when(me == N_XY - 1)
    def _():
        ext[GX + 1] = jnp.zeros((ROWS, GY), F32)

    def step(x, unused):
        first[x] = stencil(ext[x + 1], ext[x], ext[x + 2], diff_s[x], wind_s[x])
        return unused

    lax.fori_loop(0, GX, step, 0)

    for k in range(1, N_LEV):
        link_copy(k, lax.rem(level + N_LEV - k, N_LEV)).wait()
    carry_factors(level, links, factors)

    def finish(k, unused):
        for copy in copies(lax.rem(me + k, N_XY), me):
            copy.wait_send()
        for copy in copies(me, lax.rem(me + k, N_XY)):
            copy.wait_recv()
        return unused

    lax.fori_loop(1, N_XY, finish, 0)


def deposit_kernel(
    got_mass, got_code, first, blended,
    rows_acc, codes_acc, key_s, hp_s, lp_s, hl_s, col_s, total, starts_v, starts_s, sem,
):
    code = got_code[...].astype(I32)
    hl = code // 256
    col = code % 256
    valid = hl > 0
    key = jnp.where(valid, (hl - 1) // 16, -1).astype(F32)
    hl_s[...] = hl.astype(F32)
    col_s[...] = col.astype(F32)
    r, c = (lax.broadcasted_iota(I32, (512, 512), d) for d in (0, 1))
    lower = jnp.where(c < r, 1.0, 0.0).astype(BF16)
    position, base = ranks(key, BUCKETS, lower)
    place = position.astype(I32)
    hp_s[...] = jnp.where(valid, place // BLK, -1).astype(F32)
    lp_s[...] = (place % BLK).astype(F32)
    for k in range(BUCKETS):
        starts_v[k : k + 1, :] = base[32 * k : 32 * k + 1, :].astype(I32)
    count = jnp.sum(jnp.where(valid, 1.0, 0.0)).astype(I32)
    starts_v[BUCKETS:, :] = jnp.full((8, 128), count, I32)
    to_scalars = pltpu.make_async_copy(starts_v, starts_s, sem)
    to_scalars.start()

    rows_acc[...] = jnp.zeros_like(rows_acc)
    codes_acc[...] = jnp.zeros_like(codes_acc)
    total[...] = jnp.zeros_like(total)

    def one_block(i, unused):
        row = pl.ds(i, 1)
        sort_block(
            two_parts(got_mass[i]), hl_s[row, :], col_s[row, :], hp_s[row, :], lp_s[row, :],
            rows_acc, codes_acc,
        )
        return unused

    lax.fori_loop(0, N_XY, one_block, 0)
    to_scalars.wait()

    def one_bucket(k, unused):
        begin, end = starts_s[k, 0], starts_s[k + 1, 0]
        first_code = (k * 16 + 1).astype(F32)
        x, half = k // 2, k % 2

        def one_pair(j, unused):
            rows = rows_acc[pl.ds(pl.multiple_of(j * 16, 16), 16), :]
            hl_row = codes_acc[pl.ds(j, 1), :]
            col_row = codes_acc[pl.ds(j + 32, 1), :]
            mine = jnp.broadcast_to(hl_row, (16, BLK)) == iota((16, BLK), 0) + first_code
            spread = [
                jnp.where(mine, jnp.broadcast_to(rows[q : q + 1, :], (16, BLK)), 0.0) for q in range(16)
            ]
            high = jnp.concatenate(spread[:8] + [jnp.where(mine, 1.0, 0.0)], axis=0).astype(BF16)
            low = jnp.concatenate(spread[8:], axis=0).astype(BF16)
            spot = one_hot(col_row)
            big = lax.dot_general(high, spot, NT, preferred_element_type=F32).reshape(9, 16, GY)
            small = lax.dot_general(low, spot, NT, preferred_element_type=F32).reshape(8, 16, GY)
            levels = pl.ds(pl.multiple_of(half * 16, 16), 16)
            total[x, 0:8, levels, :] += big[0:8] + small
            total[x, 8, levels, :] += big[8]
            return unused

        @pl.when(end > begin)
        def _():
            lax.fori_loop(begin // BLK, (end + BLK - 1) // BLK, one_pair, 0)

        return unused

    lax.fori_loop(0, BUCKETS, one_bucket, 0)

    def blend(x, unused):
        counts = total[x, 8]
        share = counts / (counts + 2.0)
        old = first[x].reshape(BINS, LEV, GY)
        mixed = (1.0 - share)[None] * old + share[None] * total[x, 0:8]
        blended[x] = mixed.reshape(ROWS, GY)
        return unused

    lax.fori_loop(0, GX, blend, 0)


def solve_kernel(
    blended, diffusivity, wind, p_high, p_low, p_col, e_col, factors,
    out,
    ext, diff_s, wind_s, second, edge, seen, edge2, seen2,
    load_sem, store_sem, lev_send, lev_recv, diag_send, diag_recv, halo_send, halo_recv, lev2_send, lev2_recv,
):
    me, level = lax.axis_index("xy"), lax.axis_index("lev")
    above, below = lax.rem(me + 1, N_XY), lax.rem(me + N_XY - 1, N_XY)
    barrier = pltpu.get_barrier_semaphore()
    for k in range(N_LEV):
        peer = lax.rem(level + k, N_LEV)
        for where in ([me] if k else []) + [above, below]:
            pl.semaphore_signal(barrier, inc=1, device_id={"xy": where, "lev": peer}, device_id_type=MESH)

    loads = plane_copies(diffusivity, diff_s, load_sem.at[0]) + plane_copies(wind, wind_s, load_sem.at[1])
    for copy in loads:
        copy.start()

    def product(values):
        high = values.astype(BF16)
        low = (values - high.astype(F32)).astype(BF16)
        return (
            jnp.dot(p_high[...], high, preferred_element_type=F32)
            + jnp.dot(p_high[...], low, preferred_element_type=F32)
            + jnp.dot(p_low[...], high, preferred_element_type=F32)
        )

    def both(ref, i):
        return jnp.concatenate([ref[i], ref[i]], axis=1)

    def edges(values, target, x):
        blocks = values.reshape(BINS, LEV, GY)
        last, start = blocks[:, LEV - 1, :], blocks[:, 0, :]
        target[0, x] = last
        target[1, x] = start + both(factors, 10) * last

    def corrected(values, at, seen_ref):
        down = jnp.zeros((BINS, GY), F32)
        upward = jnp.zeros((BINS, GY), F32)
        for f in range(N_LEV):
            here = jnp.where(level == f, 0.0, seen_ref[f, at])
            down += both(factors, f) * here
            upward += both(factors, N_LEV + f) * here
        tail = values.reshape(BINS, LEV, GY)[:, LEV - 1, :]
        upward += both(factors, 8) * tail + both(factors, 9) * down
        shape = (BINS, LEV, GY)
        p_wide = jnp.concatenate([p_col[...], p_col[...]], axis=1).reshape(shape)
        e_wide = jnp.concatenate([e_col[...], e_col[...]], axis=1).reshape(shape)
        result = values.reshape(shape) + p_wide * down[:, None, :] + e_wide * upward[:, None, :]
        return result.reshape(ROWS, GY)

    def solve_plane(x, unused):
        solved = product(blended[x])
        ext[x + 1] = solved
        edges(solved, edge, x)
        return unused

    lax.fori_loop(0, 2, lambda i, u: solve_plane(i * (GX - 1), u), 0)
    pl.semaphore_wait(barrier, 3 * N_LEV - 1)
    up_copy = remote(ext.at[GX], ext.at[0], halo_send.at[0], halo_recv.at[0], {"xy": above, "lev": level})
    down_copy = remote(ext.at[1], ext.at[GX + 1], halo_send.at[1], halo_recv.at[1], {"xy": below, "lev": level})
    up_copy.start()
    down_copy.start()
    lax.fori_loop(1, GX - 1, solve_plane, 0)

    def lev_copies(k, owner, first_round):
        peer = lax.rem(level + k, N_LEV)
        kind = jnp.where(peer > level, 0, 1)
        if not first_round:
            return [
                remote(edge2.at[kind], seen2.at[owner], lev2_send.at[k], lev2_recv.at[k], {"xy": me, "lev": peer})
            ]
        return [
            remote(
                edge.at[kind], seen.at[owner, pl.ds(1, GX)], lev_send.at[k], lev_recv.at[k], {"xy": me, "lev": peer}
            ),
            remote(
                edge.at[kind, GX - 1], seen.at[owner, 0], diag_send.at[0, k], diag_recv.at[0, k],
                {"xy": above, "lev": peer},
            ),
            remote(
                edge.at[kind, 0], seen.at[owner, GX + 1], diag_send.at[1, k], diag_recv.at[1, k],
                {"xy": below, "lev": peer},
            ),
        ]

    for k in range(1, N_LEV):
        for copy in lev_copies(k, level, True):
            copy.start()
    for k in range(1, N_LEV):
        for copy in lev_copies(k, lax.rem(level + N_LEV - k, N_LEV), True):
            copy.wait()

    def correct_plane(at, unused):
        ext[at] = corrected(ext[at], at, seen)
        return unused

    up_copy.wait()
    down_copy.wait()
    lax.fori_loop(0, GX + 2, correct_plane, 0)

    @pl.when(me == 0)
    def _():
        ext[0] = jnp.zeros((ROWS, GY), F32)

    @pl.when(me == N_XY - 1)
    def _():
        ext[GX + 1] = jnp.zeros((ROWS, GY), F32)

    def second_plane(x, unused):
        stepped = stencil(ext[x + 1], ext[x], ext[x + 2], diff_s[x], wind_s[x])
        solved = product(stepped)
        second[x] = solved
        edges(solved, edge2, x)
        return unused

    for copy in loads:
        copy.wait()
    lax.fori_loop(0, GX, second_plane, 0)
    for k in range(1, N_LEV):
        for copy in lev_copies(k, level, False):
            copy.start()
    for k in range(1, N_LEV):
        for copy in lev_copies(k, lax.rem(level + N_LEV - k, N_LEV), False):
            copy.wait()

    def last_plane(x, unused):
        second[x] = corrected(second[x], x, seen2)
        pltpu.make_async_copy(second.at[x], out.at[:, x, :], store_sem.at[x]).start()
        return unused

    lax.fori_loop(0, GX, last_plane, 0)
    for x in range(GX):
        pltpu.make_async_copy(second.at[x], out.at[:, x, :], store_sem.at[x]).wait()


def vmem(*shape, dtype=F32):
    return pltpu.VMEM(shape, dtype)


def whole(count):
    return [pl.BlockSpec(memory_space=pltpu.VMEM)] * count


def somewhere(count):
    return [pl.BlockSpec(memory_space=pl.ANY)] * count


def shaped(*shape, dtype=F32):
    return jax.ShapeDtypeStruct(shape, dtype)


def shards(
    euler_field, parcel_mass, dest_device, dest_cell, diffusivity, wind_speed, inverses, lower_coupling, upper_coupling
):
    dma = pltpu.SemaphoreType.DMA
    routed = pl.pallas_call(
        route_kernel,
        name="route",
        out_shape=[
            shaped(GX, ROWS, GY), shaped(N_XY, BINS, CAP), shaped(N_XY, CAP),
            shaped(ROWS, ROWS, dtype=BF16), shaped(ROWS, ROWS, dtype=BF16),
            shaped(ROWS, 128), shaped(ROWS, 128), shaped(11, BINS, 128),
        ],
        in_specs=somewhere(1) + whole(3) + somewhere(2) + whole(3),
        out_specs=whole(8),
        scratch_shapes=[
            vmem(GX + 2, ROWS, GY), vmem(GX, LEV, GY), vmem(GX, LEV, GY), vmem(512, CAP), vmem(64, CAP),
            vmem(N_XY, BINS, CAP), vmem(N_XY, CAP),
            vmem(16, BLK), vmem(16, BLK), vmem(16, BLK), vmem(16, BLK), vmem(N_LEV, 3, BINS, 128),
            dma((3, GX)), dma((2,)), dma((2,)), dma((N_XY,)), dma((N_XY,)), dma((N_XY,)), dma((N_XY,)),
            dma((N_LEV,)), dma((N_LEV,)),
        ],
        compiler_params=pltpu.CompilerParams(collective_id=0, has_side_effects=True, vmem_limit_bytes=LIMIT),
    )(
        euler_field.reshape(ROWS, GX, GY), parcel_mass, dest_device.reshape(32, 128), dest_cell.reshape(32, 128),
        diffusivity, wind_speed, inverses, lower_coupling, upper_coupling,
    )
    first, got_mass, got_code, p_high, p_low, p_col, e_col, factors = routed
    blended = pl.pallas_call(
        deposit_kernel,
        name="deposit",
        out_shape=shaped(GX, ROWS, GY),
        in_specs=whole(3),
        out_specs=pl.BlockSpec(memory_space=pltpu.VMEM),
        scratch_shapes=[
            vmem(512, BLK), vmem(64, BLK),
            vmem(N_XY, BLK), vmem(N_XY, BLK), vmem(N_XY, BLK), vmem(N_XY, BLK), vmem(N_XY, BLK),
            vmem(GX, BINS + 1, LEV, GY), vmem(BUCKETS + 8, 128, dtype=I32),
            pltpu.SMEM((BUCKETS + 8, 128), I32), dma,
        ],
        compiler_params=pltpu.CompilerParams(vmem_limit_bytes=LIMIT),
    )(got_mass, got_code, first)
    result = pl.pallas_call(
        solve_kernel,
        name="solve",
        out_shape=shaped(ROWS, GX, GY),
        in_specs=whole(1) + somewhere(2) + whole(5),
        out_specs=pl.BlockSpec(memory_space=pl.ANY),
        scratch_shapes=[
            vmem(GX + 2, ROWS, GY), vmem(GX, LEV, GY), vmem(GX, LEV, GY), vmem(GX, ROWS, GY),
            vmem(2, GX, BINS, GY), vmem(N_LEV, GX + 2, BINS, GY),
            vmem(2, GX, BINS, GY), vmem(N_LEV, GX, BINS, GY),
            dma((2, GX)), dma((GX,)), dma((N_LEV,)), dma((N_LEV,)), dma((2, N_LEV)), dma((2, N_LEV)), dma((2,)), dma((2,)),
            dma((N_LEV,)), dma((N_LEV,)),
        ],
        compiler_params=pltpu.CompilerParams(collective_id=1, has_side_effects=True, vmem_limit_bytes=LIMIT),
    )(blended, diffusivity, wind_speed, p_high, p_low, p_col, e_col, factors)
    return result.reshape(BINS, LEV, GX, GY)


def solution(mesh):
    placed = (
        P(None, "lev", "xy", None),
        P(None, ("xy", "lev")),
        P(("xy", "lev"), None),
        P(("xy", "lev")),
        P("lev", "xy", None),
        P("lev", "xy", None),
        P("lev", None, None, None),
        P("lev", None),
        P("lev", None),
    )
    return jax.shard_map(
        shards, mesh=mesh, in_specs=placed, out_specs=P(None, "lev", "xy", None), check_vma=False
    )
```

time: 336 us -> 81.2 us (0.24); the launches traced: 330 us -> 80.8 us
  local copies, waits for them, and re-layouts: 145 us -> 10.5 us
  Pallas kernels: 0 us -> 70.3 us
  starting transfers between devices: 59.5 us -> 0 us
  waiting for transfers between devices: 51.1 us -> 0 us
  matrix products: 42.8 us -> 0 us
  other arithmetic: 30.4 us -> 0 us
    gather x2 -> x0, local copies, waits for them, and re-layouts: 108 us -> none  [place_slots(): return (mass_padded[:, source], cell_padded[source], capacity)]
    pallas_call x0 -> x3, Pallas kernels: none -> 70.3 us  [the longest x1 26 us: shards(): pl.pallas_call(solve_kernel, name='solve', out_shape=shaped(ROWS, GX, GY)...]
    ppermute x16 -> x0, waiting for transfers between devices: 43.2 us -> none  [the longest x12 42.1 us: passed_along(): lax.ppermute(value, axis, [(source, source + steps) for source in range(f...]
    dot_general x7 -> x0, matrix products: 42.8 us -> none  [the longest x2 37.9 us: project_cells(): jnp.einsum('qhs,sl->qhl', weighted, low_table, preferred_element_type=jnp...]
    ppermute x16 -> x0, starting transfers between devices: 41.6 us -> none  [the longest x12 32.2 us: passed_along(): lax.ppermute(value, axis, [(source, source + steps) for source in range(f...]
    all_to_all x2 -> x0, starting transfers between devices: 18 us -> none  [the longest x1 9.71 us: deposit_parcels(): lax.all_to_all(send_mass.reshape(bin_count, owners, capacity), 'xy', spli...]
    scatter x1 -> x0, local copies, waits for them, and re-layouts: 15.5 us -> none  [place_slots(): source = jnp.full((owners * capacity,), parcel_total, jnp.int32).at[slot_...]
    concatenate x3 -> x0, other arithmetic: 10.6 us -> none  [the longest x2 9.86 us: with_halo(): shard = jnp.concatenate([before, shard, after], axis=dim)]
  transfers between devices with their start and end apart: 18 -> 0, of which waited for: 14 -> 0; matrix products, arithmetic and copies ran while one was open for 25% -> 0% of each run, Pallas kernels for 0% -> 0%
where the time goes in v1:
time: 81.2 us; the launch traced here: 80.8 us
  Pallas kernels  70.3 us (87%)
  local copies, waits for them, and re-layouts  10.5 us (13%)
    pallas_call x1, Pallas kernels, shards(): pl.pallas_call(solve_kernel, name='solve', out_shape=shaped(ROWS, GX, GY)...  26 us
    pallas_call x1, Pallas kernels, shards(): pl.pallas_call(deposit_kernel, name='deposit', out_shape=shaped(GX, ROWS,...  24.3 us
    pallas_call x1, Pallas kernels, shards(): pl.pallas_call(route_kernel, name='route', out_shape=[shaped(GX, ROWS, GY...  19.9 us
    unnamed x25, local copies, waits for them, and re-layouts  10.5 us

profile of v1, /device:TPU:0, one launch (start us, length us, event | category | flops | bytes accessed | tf_op | source)
XLA Modules:
  0.0 80.8 jit_solution(11980128581067878416)
XLA Ops:
  0.0 0.0 copy-start.2
  0.0 0.9 %copy-done.2 = f32[32,8,256]{2,1,0:T(8,128)S(1)} copy-done((f32[32,8,256]{2,1,0:T(8,128)S(1)}, f32[32,8,256]{2,1,0:T(8,128)}, u32[]{:S(2)}) %copy-start.2) | copy-done | bytes 262168
  1.0 0.0 copy-start.4
  1.0 0.9 %copy-done.4 = f32[32,8,256]{2,1,0:T(8,128)S(1)} copy-done((f32[32,8,256]{2,1,0:T(8,128)S(1)}, f32[32,8,256]{2,1,0:T(8,128)}, u32[]{:S(2)}) %copy-start.4) | copy-done | bytes 262168
  1.9 0.0 copy-start.6
  1.9 0.9 %copy-done.6 = f32[8,4096]{1,0:T(8,128)S(1)} copy-done((f32[8,4096]{1,0:T(8,128)S(1)}, f32[8,4096]{1,0:T(8,128)}, u32[]{:S(2)}) %copy-start.6) | copy-done | bytes 131096
  2.8 0.0 copy-start.7
  2.8 0.9 %copy-done.7 = f32[2,8,16,16]{3,2,1,0:T(8,128)S(1)} copy-done((f32[2,8,16,16]{3,2,1,0:T(8,128)S(1)}, f32[2,8,16,16]{3,2,1,0:T(8,128)}, u32[]{:S(2)}) %copy-start.7) | copy-done | bytes 16408
  3.7 0.0 copy-start.8
  3.7 0.7 copy-done.8
  4.4 0.0 copy-start.9
  4.4 0.7 copy-done.9
  5.1 0.0 copy-start.10
  5.1 0.7 copy-done.10
  5.8 0.0 copy-start.11
  5.8 0.7 copy-done.11
  6.5 19.9 %route.1 = (f32[8,256,256]{2,1,0:T(8,128)S(1)}, f32[32,8,256]{2,1,0:T(8,128)S(1)}, f32[32,256]{1,0:T(8,128)S(1)}, bf16[256,256]{1,0:T(8,128)(2,1)S(1)}, bf16[256...) custom-call(f32[256,8,256]{2,1,0:T(8,128)} %bitcast.7, ...), custom_call_target="tpu_custom_call" | custom-call | tf_op jit(solution)/shard_map/route/pallas_call | solution.py:528
  26.5 0.0 copy-start.1
  26.5 1.3 %copy-done.1 = f32[8,256,256]{2,1,0:T(8,128)} copy-done((f32[8,256,256]{2,1,0:T(8,128)}, f32[8,256,256]{2,1,0:T(8,128)S(1)}, u32[]{:S(2)}) %copy-start.1) | copy-done | bytes 2097176
  27.8 0.0 copy-start.3
  27.8 0.0 copy-start.5
  27.8 24.3 %deposit.1.blended = f32[8,256,256]{2,1,0:T(8,128)S(1)} custom-call(f32[32,8,256]{2,1,0:T(8,128)S(1)} %get-tuple-element.13.got_mass, f32[32,256]{1,0:T(8,128)S(1)} %get-tuple-element.14.got_code, f32[8,256,256]{2,1,0:T(8,128)} %copy-done.1), custom_call_target="tpu_custom_call" | custom-call | tf_op jit(solution)/shard_map/deposit/pallas_call | solution.py:551
  52.1 0.0 copy-start
  52.1 1.3 %copy-done = f32[8,256,256]{2,1,0:T(8,128)} copy-done((f32[8,256,256]{2,1,0:T(8,128)}, f32[8,256,256]{2,1,0:T(8,128)S(1)}, u32[]{:S(2)}) %copy-start) | copy-done | bytes 2097176
  53.4 0.0 copy-done.3
  53.4 0.0 copy-done.5
  53.4 26.0 %solve.1 = f32[256,8,256]{2,1,0:T(8,128)S(1)} custom-call(f32[8,256,256]{2,1,0:T(8,128)} %copy-done, f32[32,8,256]{2,1,0:T(8,128)S(1)} %copy-done.3, f32[32,8,256]{2,1,0:T(8,128)S(1)} %copy-done.5, bf16[256,256]{1,0:T(8,128)(2,1)S(1)} %get-tuple-element.16.p_high, bf16[256,256]{1,0:T(8,128)(2,1)S(1)} %get-tuple-element.17.p_low, ...), custom_call_target="tpu_custom_call" | custom-call | tf_op jit(solution)/shard_map/solve/pallas_call | solution.py:565
  79.4 1.3 %copy.11 = f32[8,32,8,256]{3,2,1,0:T(8,128)} copy(f32[8,32,8,256]{3,2,1,0:T(8,128)S(1)} %bitcast.4) | data formatting | bytes 4194304
Async XLA Ops:
  0.0 0.9 %copy-start.2 = (f32[32,8,256]{2,1,0:T(8,128)S(1)}, f32[32,8,256]{2,1,0:T(8,128)}, u32[]{:S(2)}) copy-start(f32[32,8,256]{2,1,0:T(8,128)} %diffusivity.3) | copy-start | bytes 786436
  1.0 0.9 %copy-start.4 = (f32[32,8,256]{2,1,0:T(8,128)S(1)}, f32[32,8,256]{2,1,0:T(8,128)}, u32[]{:S(2)}) copy-start(f32[32,8,256]{2,1,0:T(8,128)} %wind.3) | copy-start | bytes 786436
  1.9 0.9 %copy-start.6 = (f32[8,4096]{1,0:T(8,128)S(1)}, f32[8,4096]{1,0:T(8,128)}, u32[]{:S(2)}) copy-start(f32[8,4096]{1,0:T(8,128)} %mass.1) | copy-start | bytes 393220
  2.8 0.9 %copy-start.7 = (f32[2,8,16,16]{3,2,1,0:T(8,128)S(1)}, f32[2,8,16,16]{3,2,1,0:T(8,128)}, u32[]{:S(2)}) copy-start(f32[2,8,16,16]{3,2,1,0:T(8,128)} %inv.1) | copy-start | bytes 49156
  3.7 0.7 copy-start.8
  4.4 0.7 copy-start.9
  5.1 0.7 copy-start.10
  5.8 0.7 copy-start.11
  26.5 1.3 %copy-start.1 = (f32[8,256,256]{2,1,0:T(8,128)}, f32[8,256,256]{2,1,0:T(8,128)S(1)}, u32[]{:S(2)}) copy-start(f32[8,256,256]{2,1,0:T(8,128)S(1)} %get-tuple-element.15.first) | copy-start | bytes 6291460
  27.8 25.6 %copy-start.3 = (f32[32,8,256]{2,1,0:T(8,128)S(1)}, f32[32,8,256]{2,1,0:T(8,128)}, u32[]{:S(2)}) copy-start(f32[32,8,256]{2,1,0:T(8,128)} %diffusivity.3) | copy-start | bytes 786436
  27.8 25.6 %copy-start.5 = (f32[32,8,256]{2,1,0:T(8,128)S(1)}, f32[32,8,256]{2,1,0:T(8,128)}, u32[]{:S(2)}) copy-start(f32[32,8,256]{2,1,0:T(8,128)} %wind.3) | copy-start | bytes 786436
  52.1 1.3 %copy-start = (f32[8,256,256]{2,1,0:T(8,128)}, f32[8,256,256]{2,1,0:T(8,128)S(1)}, u32[]{:S(2)}) copy-start(f32[8,256,256]{2,1,0:T(8,128)S(1)} %deposit.1.blended) | copy-start | bytes 6291460

commit v2 on v1

v2 whole, which is shorter than its diff:
```python
import functools

import jax
import jax.numpy as jnp
from jax import lax
from jax.experimental import pallas as pl
from jax.experimental.pallas import tpu as pltpu
from jax.sharding import PartitionSpec as P

F32, BF16, I32 = jnp.float32, jnp.bfloat16, jnp.int32
MESH = pl.DeviceIdType.MESH
N_XY, N_LEV, BINS, LEV, GX, GY = 32, 4, 8, 32, 8, 256
ROWS = BINS * LEV
PARC, CAP, BLK = 4096, 256, 256
BUCKETS = 16
NT = (((1,), (1,)), ((), ()))
LIMIT = 24 << 20
SETS = 2
SRC = N_XY // SETS
SPAN = SRC * CAP
UNITS = SPAN // 128
WIN = 4


def iota(shape, dim, dtype=F32):
    return lax.broadcasted_iota(I32, shape, dim).astype(dtype)


def ranks(keys, count, lower):
    n = keys.shape[0]
    masks = [jnp.where(keys == k, 1.0, 0.0) for k in range(count)]
    stack = jnp.concatenate(masks, axis=0).astype(BF16)
    before = (iota((BLK, BLK), 0) < iota((BLK, BLK), 1)).astype(BF16)
    inside = jnp.dot(stack, before, preferred_element_type=F32)
    totals = jnp.dot(stack, jnp.ones((BLK, 128), BF16), preferred_element_type=F32)
    base = jnp.dot(lower, totals.astype(BF16), preferred_element_type=F32)
    wide = jnp.concatenate([base, base], axis=1)
    whole = inside + wide[: inside.shape[0]]
    position = jnp.zeros(keys.shape, F32)
    for k in range(count):
        position += masks[k] * whole[k * n : (k + 1) * n]
    return position, base


def lanes(pieces):
    return jnp.concatenate(pieces, axis=1)


def one_hot(row):
    width = row.shape[1]
    wide = jnp.broadcast_to(row, (BLK, width)).astype(BF16)
    ids = iota((BLK, width), 0, BF16)
    return jnp.where(ids == wide, jnp.ones((BLK, width), BF16), jnp.zeros((BLK, width), BF16))


def sort_slots(values16, high_low, column, target, slot, count):
    width = target.shape[1]
    chosen = jnp.broadcast_to(target, (16, width)).astype(BF16)
    zero = jnp.zeros((16, width), BF16)
    parts = [jnp.where(chosen == jnp.array(d, BF16), values16, zero) for d in range(count)]
    mine = iota((count, width), 0) == target
    codes = jnp.concatenate([jnp.where(mine, high_low, 0.0), jnp.where(mine, column, 0.0)], axis=0)
    weighted = jnp.concatenate(parts + [codes.astype(BF16)], axis=0)
    return lax.dot_general(weighted, one_hot(slot), NT, preferred_element_type=F32)


def two_parts(values):
    high = values.astype(BF16).astype(F32)
    return jnp.concatenate([high, values - high], axis=0).astype(BF16)


def stencil(centre, before, after, diffusivity, wind):
    shape = (BINS, LEV, GY)
    lane = lax.broadcasted_iota(I32, (ROWS, GY), 1)
    left = jnp.where(lane == 0, 0.0, pltpu.roll(centre, 1, 1))
    right = jnp.where(lane == GY - 1, 0.0, pltpu.roll(centre, GY - 1, 1))
    laplace = (after + before + right + left - 4.0 * centre).reshape(shape)
    drift = (centre - before).reshape(shape)
    result = centre.reshape(shape) + diffusivity[None] * laplace - wind[None] * drift
    return result.reshape(ROWS, GY)


def plane_copies(source, target, sems, at=0):
    return [pltpu.make_async_copy(source.at[:, x, :], target.at[at + x], sems.at[x]) for x in range(GX)]


def remote(src, dst, send, recv, device):
    return pltpu.make_async_remote_copy(
        src_ref=src, dst_ref=dst, send_sem=send, recv_sem=recv, device_id=device, device_id_type=MESH
    )


def compose(inv, low, up, hi_ref, lo_ref, p_ref, e_ref):
    lane16 = lax.broadcasted_iota(I32, (16, ROWS), 1) % LEV
    row16 = lax.broadcasted_iota(I32, (16, ROWS), 0)
    own = lax.broadcasted_iota(I32, (BINS, 16, ROWS), 0) == (
        lax.broadcasted_iota(I32, (BINS, 16, ROWS), 2) // LEV
    )

    def spread(group):
        place = (lane16 == row16 + 16 * group).astype(F32)
        flat = inv[group].reshape(BINS * 16, 16)
        full = jnp.dot(flat, place, precision=lax.Precision.HIGHEST, preferred_element_type=F32)
        return jnp.where(own, full.reshape(BINS, 16, ROWS), 0.0)

    def per_bin(ref, group):
        wide = jnp.broadcast_to(ref[group : group + 1, :].reshape(1, 1, BINS), (BINS, 1, BINS))
        same = lax.broadcasted_iota(I32, (BINS, 1, BINS), 0) == lax.broadcasted_iota(
            I32, (BINS, 1, BINS), 2
        )
        return jnp.sum(jnp.where(same, wide, 0.0), axis=2, keepdims=True)

    t0, t1 = spread(0), spread(1)
    l0, l1, u0, u1 = per_bin(low, 0), per_bin(low, 1), per_bin(up, 0), per_bin(up, 1)
    m0, m1 = inv[0], inv[1]
    m0_first, m0_last = m0[:, :, 0:1], m0[:, :, 15:16]
    m1_first, m1_last = m1[:, :, 0:1], m1[:, :, 15:16]
    tail0 = t0[:, 15:16, :]
    link = (l1 * m1[:, 0:1, 0:1]) * tail0 + t1[:, 0:1, :]
    p0 = t0 + (u0 * m0_last) * link
    p1 = t1 + (l1 * m1_first) * tail0
    full = jnp.concatenate([p0, p1], axis=1).reshape(ROWS, ROWS)
    high = full.astype(BF16)
    hi_ref[...] = high
    lo_ref[...] = (full - high.astype(F32)).astype(BF16)
    passed = l1 * l0 * m0[:, 15:16, 0:1]
    c0 = l0 * m0_first + (u0 * m0_last) * (passed * m1[:, 0:1, 0:1])
    c1 = passed * m1_first
    d0 = (u0 * u1 * m1[:, 0:1, 15:16]) * m0_last
    d1 = u1 * m1_last
    p_ref[...] = jnp.broadcast_to(jnp.concatenate([c0, c1], axis=1), (BINS, LEV, 128)).reshape(ROWS, 128)
    e_ref[...] = jnp.broadcast_to(jnp.concatenate([d0, d1], axis=1), (BINS, LEV, 128)).reshape(ROWS, 128)


def carry_factors(level, all_ref, out_ref):
    alpha = [all_ref[f, 0] for f in range(N_LEV)]
    beta = [all_ref[f, 1] for f in range(N_LEV)]
    gamma = [all_ref[f, 2] for f in range(N_LEV)]
    zero, one = jnp.zeros((BINS, 128), F32), jnp.ones((BINS, 128), F32)
    for f in range(N_LEV):
        down, product = zero, one
        for i in range(f + 1, N_LEV):
            down = jnp.where(level == i, product, down)
            product = product * alpha[i]
        upward, product = zero, one
        for i in range(f - 1, -1, -1):
            upward = jnp.where(level == i, product, upward)
            product = product * beta[i]
        out_ref[f] = down
        out_ref[N_LEV + f] = upward
    sigma = [zero] * N_LEV
    for f in range(N_LEV - 1, 0, -1):
        sigma[f - 1] = gamma[f] + beta[f] * alpha[f] * sigma[f]

    def own(values):
        result = values[0]
        for f in range(1, N_LEV):
            result = jnp.where(level == f, values[f], result)
        return result

    out_ref[8] = own(sigma)
    out_ref[9] = own([sigma[f] * alpha[f] for f in range(N_LEV)])
    out_ref[10] = own([sigma[f] * beta[f] for f in range(N_LEV)])


def route_kernel(
    euler, mass, dest, cell, diffusivity, wind, inv, low, up,
    first, got_mass, got_code, p_high, p_low, p_col, e_col, factors,
    ext, diff_s, wind_s, mass_s, dest_in, cell_in, inv_s, low_s, up_s, table_s,
    send_mass, send_code, dest_s, slot_s, hl_s, col_s, links,
    load_sem, small_sem, halo_send, halo_recv, mass_send, mass_recv, code_send, code_recv, link_send, link_recv,
):
    me, level = lax.axis_index("xy"), lax.axis_index("lev")
    barrier = pltpu.get_barrier_semaphore()

    def greet(k, unused):
        pl.semaphore_signal(
            barrier, inc=1, device_id={"xy": lax.rem(me + k, N_XY), "lev": level}, device_id_type=MESH
        )
        return unused

    lax.fori_loop(1, N_XY, greet, 0)
    for k in range(1, N_LEV):
        pl.semaphore_signal(
            barrier, inc=1, device_id={"xy": me, "lev": lax.rem(level + k, N_LEV)}, device_id_type=MESH
        )

    small = [
        pltpu.make_async_copy(source, target, small_sem.at[i])
        for i, (source, target) in enumerate(
            [(dest, dest_in), (cell, cell_in), (mass, mass_s), (inv, inv_s), (low, low_s), (up, up_s)]
        )
    ]
    field = plane_copies(euler, ext, load_sem.at[0], 1)
    coefficients = plane_copies(diffusivity, diff_s, load_sem.at[1]) + plane_copies(wind, wind_s, load_sem.at[2])
    for copy in small + field + coefficients:
        copy.start()

    def wide(ref):
        return jnp.concatenate([ref[pl.ds(0, 16, stride=2), :], ref[pl.ds(1, 16, stride=2), :]], axis=1)

    for copy in small[:2]:
        copy.wait()
    target = wide(dest_in).astype(F32)
    cells = wide(cell_in)
    levels = cells // (GX * GY)
    xs = (cells // GY) % GX
    bucket = xs * 2 + levels // 16
    dest_s[...] = target
    hl_s[...] = (bucket * 16 + levels % 16 + 1).astype(F32)
    col_s[...] = (cells % GY).astype(F32)
    r, c = (lax.broadcasted_iota(I32, (512, 512), d) for d in (0, 1))
    lower = jnp.where((c < r) & (c // 16 == r // 16), 1.0, 0.0).astype(BF16)
    slot, unused_base = ranks(target, N_XY, lower)
    slot_s[...] = slot

    for copy in field:
        copy.wait()
    pl.semaphore_wait(barrier, N_XY - 1 + N_LEV - 1)
    above, below = lax.rem(me + 1, N_XY), lax.rem(me + N_XY - 1, N_XY)
    up_copy = remote(ext.at[GX], ext.at[0], halo_send.at[0], halo_recv.at[0], {"xy": above, "lev": level})
    down_copy = remote(ext.at[1], ext.at[GX + 1], halo_send.at[1], halo_recv.at[1], {"xy": below, "lev": level})
    up_copy.start()
    down_copy.start()

    small[2].wait()
    table_s[...] = jnp.zeros_like(table_s)

    def some_blocks(i, unused):
        block = pl.ds(pl.multiple_of(i * (PARC // 2), PARC // 2), PARC // 2)
        take = lambda ref: lanes([ref[pl.ds(i * 8 + j, 1), :] for j in range(8)])
        table_s[...] += sort_slots(
            two_parts(mass_s[:, block]), take(hl_s), take(col_s), take(dest_s), take(slot_s), N_XY
        )
        return unused

    lax.fori_loop(0, 2, some_blocks, 0)
    table = table_s[0 : 16 * N_XY].reshape(N_XY, 16, CAP)
    send_mass[...] = table[:, :8] + table[:, 8:]
    send_code[...] = table_s[16 * N_XY : 17 * N_XY] * 256.0 + table_s[17 * N_XY :]

    def copies(other, slot_id):
        device = {"xy": other, "lev": level}
        return (
            remote(send_mass.at[other], got_mass.at[slot_id], mass_send.at[other], mass_recv.at[slot_id], device),
            remote(
                send_code.at[pl.ds(other, 1)], got_code.at[pl.ds(slot_id, 1)],
                code_send.at[other], code_recv.at[slot_id], device,
            ),
        )

    def send(k, unused):
        for copy in copies(lax.rem(me + k, N_XY), me):
            copy.start()
        return unused

    lax.fori_loop(1, N_XY, send, 0)
    got_mass[me] = send_mass[me]
    got_code[pl.ds(me, 1), :] = send_code[pl.ds(me, 1), :]

    for copy in small[3:]:
        copy.wait()
    compose(inv_s, low_s, up_s, p_high, p_low, p_col, e_col)
    links[level, 0] = p_col[pl.ds(LEV - 1, BINS, stride=LEV), :]
    links[level, 1] = e_col[pl.ds(0, BINS, stride=LEV), :]
    links[level, 2] = p_col[pl.ds(0, BINS, stride=LEV), :]

    def link_copy(k, owner):
        peer = lax.rem(level + k, N_LEV)
        return remote(
            links.at[owner], links.at[owner], link_send.at[k], link_recv.at[k], {"xy": me, "lev": peer}
        )

    for k in range(1, N_LEV):
        link_copy(k, level).start()

    for copy in coefficients:
        copy.wait()
    up_copy.wait()
    down_copy.wait()

    @pl.when(me == 0)
    def _():
        ext[0] = jnp.zeros((ROWS, GY), F32)

    @pl.when(me == N_XY - 1)
    def _():
        ext[GX + 1] = jnp.zeros((ROWS, GY), F32)

    def step(x, unused):
        first[x] = stencil(ext[x + 1], ext[x], ext[x + 2], diff_s[x], wind_s[x])
        return unused

    lax.fori_loop(0, GX, step, 0)

    for k in range(1, N_LEV):
        link_copy(k, lax.rem(level + N_LEV - k, N_LEV)).wait()
    carry_factors(level, links, factors)

    def finish(k, unused):
        for copy in copies(lax.rem(me + k, N_XY), me):
            copy.wait_send()
        for copy in copies(me, lax.rem(me + k, N_XY)):
            copy.wait_recv()
        return unused

    lax.fori_loop(1, N_XY, finish, 0)


def deposit_kernel(
    got_mass, got_code, first, blended,
    rows_u, hl_u, col_u, hp_s, lp_s, hl_s, col_s, total, starts_v, starts_s, sem,
):
    code = got_code[...].astype(I32)
    hl = code // 256
    col = code % 256
    valid = hl > 0
    key = jnp.where(valid, (hl - 1) // 16, -1).astype(F32)
    hl_s[...] = hl.astype(F32)
    col_s[...] = col.astype(F32)
    r, c = (lax.broadcasted_iota(I32, (N_XY * (BUCKETS + 1), 512), d) for d in (0, 1))
    lower = jnp.where((c < r) & ((c % N_XY) // SRC == (r % N_XY) // SRC), 1.0, 0.0).astype(BF16)
    position, base = ranks(key, BUCKETS, lower)
    place = position.astype(I32)
    hp_s[...] = jnp.where(valid, place // BLK, -1).astype(F32)
    lp_s[...] = (place % BLK).astype(F32)
    lane = lax.broadcasted_iota(I32, (1, 128), 1)
    longest = jnp.zeros((1, 128), I32)
    before = None
    for k in range(BUCKETS + 1):
        start = jnp.zeros((1, 128), F32)
        for g in range(SETS):
            at = N_XY * k + SRC * g
            start = jnp.where(lane == g, base[at : at + 1, :], start)
        start = start.astype(I32)
        starts_v[k : k + 1, :] = start
        if k:
            longest = jnp.maximum(longest, start - before // 128 * 128)
        before = start
    starts_v[BUCKETS + 1 : BUCKETS + 2, :] = longest
    to_scalars = pltpu.make_async_copy(starts_v, starts_s, sem)
    to_scalars.start()

    def one_set(g, unused):
        take = lambda ref: lanes([ref[pl.ds(g * SRC + i, 1), :] for i in range(SRC)])
        values = lanes([two_parts(got_mass[g * SRC + i]) for i in range(SRC)])
        table = sort_slots(values, take(hl_s), take(col_s), take(hp_s), take(lp_s), SRC)
        for half in range(2):
            side = slice(128 * half, 128 * half + 128)
            for d in range(SRC):
                rows_u[g, 2 * d + half] = table[16 * d : 16 * d + 16, side]
            hl_u[g, pl.ds(half, SRC, stride=2), :] = table[16 * SRC : 17 * SRC, side]
            col_u[g, pl.ds(half, SRC, stride=2), :] = table[17 * SRC : 18 * SRC, side]
        rows_u[g, UNITS:] = jnp.zeros((WIN, 16, 128), F32)
        hl_u[g, UNITS:, :] = jnp.zeros((8, 128), F32)
        col_u[g, UNITS:, :] = jnp.zeros((8, 128), F32)
        return unused

    lax.fori_loop(0, SETS, one_set, 0)
    to_scalars.wait()

    def place_of(k):
        return k // 2, pl.ds(pl.multiple_of((k % 2) * 16, 16), 16)

    def window(k, t):
        first_code = (k * 16 + 1).astype(F32)
        at = [jnp.minimum(starts_s[k, g] // 128 + WIN * t, UNITS) for g in range(SETS)]
        units = [(g, at[g] + i) for g in range(SETS) for i in range(WIN)]
        hl_row = lanes([hl_u[g, pl.ds(u, 1), :] for g, u in units])
        col_row = lanes([col_u[g, pl.ds(u, 1), :] for g, u in units])
        rows = lanes([rows_u[g, u] for g, u in units])
        width = 128 * WIN * SETS
        mine = jnp.broadcast_to(hl_row, (16, width)) == iota((16, width), 0) + first_code
        spread = [jnp.where(mine, jnp.broadcast_to(rows[q : q + 1, :], (16, width)), 0.0) for q in range(16)]
        spread.insert(8, jnp.where(mine, 1.0, 0.0))
        weighted = jnp.concatenate(spread, axis=0).astype(BF16)
        table = lax.dot_general(weighted, one_hot(col_row), NT, preferred_element_type=F32)
        table = table.reshape(17, 16, GY)
        return jnp.concatenate([table[:8] + table[9:], table[8:9]], axis=0)

    def one_bucket(k, unused):
        x, levels = place_of(k)
        total[x, :, levels, :] = window(k, 0)
        return unused

    lax.fori_loop(0, BUCKETS, one_bucket, 0, unroll=4)

    def rest(k, unused):
        x, levels = place_of(k)
        rounds = jnp.int32(1)
        for g in range(SETS):
            span = starts_s[k + 1, g] - starts_s[k, g] // 128 * 128
            rounds = jnp.maximum(rounds, (span + 128 * WIN - 1) // (128 * WIN))

        def again(t, unused):
            total[x, :, levels, :] += window(k, t)
            return unused

        lax.fori_loop(1, rounds, again, 0)
        return unused

    most = starts_s[BUCKETS + 1, 0]
    for g in range(1, SETS):
        most = jnp.maximum(most, starts_s[BUCKETS + 1, g])

    @pl.when(most > 128 * WIN)
    def _():
        lax.fori_loop(0, BUCKETS, rest, 0)

    def blend(x, unused):
        counts = total[x, 8]
        share = counts / (counts + 2.0)
        old = first[x].reshape(BINS, LEV, GY)
        mixed = (1.0 - share)[None] * old + share[None] * total[x, 0:8]
        blended[x] = mixed.reshape(ROWS, GY)
        return unused

    lax.fori_loop(0, GX, blend, 0)


def correction(values, down, upward, p_col, e_col):
    shape = (BINS, LEV, GY)
    p_wide = lanes([p_col[...], p_col[...]]).reshape(shape)
    e_wide = lanes([e_col[...], e_col[...]]).reshape(shape)
    result = values.reshape(shape) + p_wide * down[:, None, :] + e_wide * upward[:, None, :]
    return result.reshape(ROWS, GY)


def solve_kernel(
    blended, diffusivity, wind, p_high, p_low, p_col, e_col, factors,
    second, down_out, up_out,
    ext, fixed, triple, diff_s, wind_s, edge, seen, edge2, seen2,
    load_sem, lev_send, lev_recv, diag_send, diag_recv, halo_send, halo_recv, lev2_send, lev2_recv,
):
    me, level = lax.axis_index("xy"), lax.axis_index("lev")
    above, below = lax.rem(me + 1, N_XY), lax.rem(me + N_XY - 1, N_XY)
    barrier = pltpu.get_barrier_semaphore()
    for k in range(N_LEV):
        peer = lax.rem(level + k, N_LEV)
        for where in ([me] if k else []) + [above, below]:
            pl.semaphore_signal(barrier, inc=1, device_id={"xy": where, "lev": peer}, device_id_type=MESH)
    loads = plane_copies(diffusivity, diff_s, load_sem.at[0]) + plane_copies(wind, wind_s, load_sem.at[1])
    for copy in loads:
        copy.start()
    triple[:, 0:ROWS] = p_high[...]
    triple[:, ROWS : 2 * ROWS] = p_high[...]
    triple[:, 2 * ROWS :] = p_low[...]

    def product(values):
        high = values.astype(BF16)
        low = (values - high.astype(F32)).astype(BF16)
        return jnp.dot(triple[...], jnp.concatenate([high, low, high], axis=0), preferred_element_type=F32)

    def both(i):
        return lanes([factors[i], factors[i]])

    def edges(values, target, at):
        blocks = values.reshape(BINS, LEV, GY)
        last, start = blocks[:, LEV - 1, :], blocks[:, 0, :]
        target[0, at] = last
        target[1, at] = start + both(10) * last

    def carries(values, at, seen_ref):
        down = jnp.zeros((BINS, GY), F32)
        upward = jnp.zeros((BINS, GY), F32)
        for f in range(N_LEV):
            here = jnp.where(level == f, 0.0, seen_ref[f, at])
            down += both(f) * here
            upward += both(N_LEV + f) * here
        tail = values.reshape(BINS, LEV, GY)[:, LEV - 1, :]
        return down, upward + both(8) * tail + both(9) * down

    def solve_plane(x, unused):
        solved = product(blended[x])
        ext[x + 1] = solved
        edges(solved, edge, x)
        return unused

    lax.fori_loop(0, 2, lambda i, u: solve_plane(i * (GX - 1), u), 0, unroll=2)
    pl.semaphore_wait(barrier, 3 * N_LEV - 1)
    up_copy = remote(ext.at[GX], ext.at[0], halo_send.at[0], halo_recv.at[0], {"xy": above, "lev": level})
    down_copy = remote(ext.at[1], ext.at[GX + 1], halo_send.at[1], halo_recv.at[1], {"xy": below, "lev": level})
    up_copy.start()
    down_copy.start()
    lax.fori_loop(1, GX - 1, solve_plane, 0, unroll=3)

    def lev_copies(k, owner):
        peer = lax.rem(level + k, N_LEV)
        kind = jnp.where(peer > level, 0, 1)
        return [
            remote(
                edge.at[kind], seen.at[owner, pl.ds(1, GX)], lev_send.at[k], lev_recv.at[k], {"xy": me, "lev": peer}
            ),
            remote(
                edge.at[kind, GX - 1], seen.at[owner, 0], diag_send.at[0, k], diag_recv.at[0, k],
                {"xy": above, "lev": peer},
            ),
            remote(
                edge.at[kind, 0], seen.at[owner, GX + 1], diag_send.at[1, k], diag_recv.at[1, k],
                {"xy": below, "lev": peer},
            ),
        ]

    def back(k):
        return lax.rem(level + N_LEV - k, N_LEV)

    out_going = [lev_copies(k, level) for k in range(1, N_LEV)]
    in_coming = [lev_copies(k, back(k)) for k in range(1, N_LEV)]
    for i in range(3):
        for group in out_going:
            group[i].start()
    for group in in_coming:
        group[0].wait()

    def correct_plane(at, unused):
        down, upward = carries(ext[at], at, seen)
        fixed[at] = correction(ext[at], down, upward, p_col, e_col)
        return unused

    lax.fori_loop(1, GX + 1, correct_plane, 0, unroll=2)

    def second_plane(x, at):
        stepped = stencil(fixed[x + 1], fixed[x], fixed[x + 2], diff_s[x], wind_s[x])
        solved = product(stepped)
        second[x] = solved
        edges(solved, edge2, at)

    for copy in loads:
        copy.wait()

    parts = ((0, 3), (3, 3), (6, 2))

    def lev2_copies(part, k, owner):
        peer = lax.rem(level + k, N_LEV)
        kind = jnp.where(peer > level, 0, 1)
        begin, size = parts[part]
        return remote(
            edge2.at[kind, pl.ds(begin, size)], seen2.at[owner, pl.ds(begin, size)],
            lev2_send.at[part, k], lev2_recv.at[part, k], {"xy": me, "lev": peer},
        )

    def inner(at, unused):
        second_plane(at + 1, at)
        return unused

    for part in range(2):
        begin, size = parts[part]
        lax.fori_loop(begin, begin + size, inner, 0)
        for k in range(1, N_LEV):
            lev2_copies(part, k, level).start()

    up_copy.wait()
    down_copy.wait()
    for group in in_coming:
        for copy in group[1:]:
            copy.wait()
    correct_plane(0, 0)
    correct_plane(GX + 1, 0)

    @pl.when(me == 0)
    def _():
        fixed[0] = jnp.zeros((ROWS, GY), F32)

    @pl.when(me == N_XY - 1)
    def _():
        fixed[GX + 1] = jnp.zeros((ROWS, GY), F32)

    def outer(i, unused):
        second_plane(i * (GX - 1), i + 6)
        return unused

    lax.fori_loop(0, 2, outer, 0)
    for k in range(1, N_LEV):
        lev2_copies(2, k, level).start()
    for part in range(3):
        for k in range(1, N_LEV):
            lev2_copies(part, k, back(k)).wait()

    def last_carries(at, unused):
        x = jnp.where(at < 6, at + 1, (at - 6) * (GX - 1))
        down, upward = carries(second[x], at, seen2)
        down_out[x] = down
        up_out[x] = upward
        return unused

    lax.fori_loop(0, GX, last_carries, 0, unroll=2)


def finish_kernel(second, down, upward, p_col, e_col, out, planes, sem):
    def copy(x):
        return pltpu.make_async_copy(planes.at[x], out.at[:, x, :], sem.at[x])

    def one(x, unused):
        planes[x] = correction(second[x], down[x], upward[x], p_col, e_col)
        copy(x).start()
        return unused

    lax.fori_loop(0, GX, one, 0)
    for x in range(GX):
        copy(x).wait()


def vmem(*shape, dtype=F32):
    return pltpu.VMEM(shape, dtype)


def whole(count):
    return [pl.BlockSpec(memory_space=pltpu.VMEM)] * count


def somewhere(count):
    return [pl.BlockSpec(memory_space=pltpu.HBM)] * count


def shaped(*shape, dtype=F32):
    return jax.ShapeDtypeStruct(shape, dtype)


def shards(
    euler_field, parcel_mass, dest_device, dest_cell, diffusivity, wind_speed, inverses, lower_coupling, upper_coupling
):
    dma = pltpu.SemaphoreType.DMA
    euler, mass, dest, cell, diffusivity, wind, inv, low, up = [
        pltpu.with_memory_space_constraint(array, pltpu.HBM)
        for array in (
            euler_field.reshape(ROWS, GX, GY), parcel_mass, dest_device.reshape(32, 128), dest_cell.reshape(32, 128),
            diffusivity, wind_speed, inverses, lower_coupling, upper_coupling,
        )
    ]
    routed = pl.pallas_call(
        route_kernel,
        name="route",
        out_shape=[
            shaped(GX, ROWS, GY), shaped(N_XY, BINS, CAP), shaped(N_XY, CAP),
            shaped(ROWS, ROWS, dtype=BF16), shaped(ROWS, ROWS, dtype=BF16),
            shaped(ROWS, 128), shaped(ROWS, 128), shaped(11, BINS, 128),
        ],
        in_specs=somewhere(9),
        out_specs=whole(8),
        scratch_shapes=[
            vmem(GX + 2, ROWS, GY), vmem(GX, LEV, GY), vmem(GX, LEV, GY),
            vmem(BINS, PARC), vmem(32, 128, dtype=I32), vmem(32, 128, dtype=I32),
            vmem(2, BINS, 16, 16), vmem(2, BINS), vmem(2, BINS), vmem(18 * N_XY, CAP),
            vmem(N_XY, BINS, CAP), vmem(N_XY, CAP),
            vmem(16, BLK), vmem(16, BLK), vmem(16, BLK), vmem(16, BLK), vmem(N_LEV, 3, BINS, 128),
            dma((3, GX)), dma((6,)), dma((2,)), dma((2,)), dma((N_XY,)), dma((N_XY,)), dma((N_XY,)), dma((N_XY,)),
            dma((N_LEV,)), dma((N_LEV,)),
        ],
        compiler_params=pltpu.CompilerParams(collective_id=0, has_side_effects=True, vmem_limit_bytes=LIMIT),
    )(euler, mass, dest, cell, diffusivity, wind, inv, low, up)
    first, got_mass, got_code, p_high, p_low, p_col, e_col, factors = routed
    blended = pl.pallas_call(
        deposit_kernel,
        name="deposit",
        out_shape=shaped(GX, ROWS, GY),
        in_specs=whole(3),
        out_specs=pl.BlockSpec(memory_space=pltpu.VMEM),
        scratch_shapes=[
            vmem(SETS, UNITS + WIN, 16, 128), vmem(SETS, UNITS + 8, 128), vmem(SETS, UNITS + 8, 128),
            vmem(N_XY, BLK), vmem(N_XY, BLK), vmem(N_XY, BLK), vmem(N_XY, BLK),
            vmem(GX, BINS + 1, LEV, GY), vmem(BUCKETS + 8, 128, dtype=I32),
            pltpu.SMEM((BUCKETS + 8, 128), I32), dma,
        ],
        compiler_params=pltpu.CompilerParams(vmem_limit_bytes=LIMIT),
    )(got_mass, got_code, first)
    second, down, upward = pl.pallas_call(
        solve_kernel,
        name="solve",
        out_shape=[shaped(GX, ROWS, GY), shaped(GX, BINS, GY), shaped(GX, BINS, GY)],
        in_specs=whole(1) + somewhere(2) + whole(5),
        out_specs=whole(3),
        scratch_shapes=[
            vmem(GX + 2, ROWS, GY), vmem(GX + 2, ROWS, GY), vmem(ROWS, 3 * ROWS, dtype=BF16), vmem(GX, LEV, GY), vmem(GX, LEV, GY),
            vmem(2, GX, BINS, GY), vmem(N_LEV, GX + 2, BINS, GY),
            vmem(2, GX, BINS, GY), vmem(N_LEV, GX, BINS, GY),
            dma((2, GX)), dma((N_LEV,)), dma((N_LEV,)), dma((2, N_LEV)), dma((2, N_LEV)), dma((2,)), dma((2,)),
            dma((3, N_LEV)), dma((3, N_LEV)),
        ],
        compiler_params=pltpu.CompilerParams(collective_id=1, has_side_effects=True, vmem_limit_bytes=LIMIT),
    )(blended, diffusivity, wind, p_high, p_low, p_col, e_col, factors)
    result = pl.pallas_call(
        finish_kernel,
        name="finish",
        out_shape=shaped(ROWS, GX, GY),
        in_specs=whole(5),
        out_specs=pl.BlockSpec(memory_space=pltpu.HBM),
        scratch_shapes=[vmem(GX, ROWS, GY), dma((GX,))],
        compiler_params=pltpu.CompilerParams(vmem_limit_bytes=LIMIT),
    )(second, down, upward, p_col, e_col)
    return result.reshape(BINS, LEV, GX, GY)


def solution(mesh):
    placed = (
        P(None, "lev", "xy", None),
        P(None, ("xy", "lev")),
        P(("xy", "lev"), None),
        P(("xy", "lev")),
        P("lev", "xy", None),
        P("lev", "xy", None),
        P("lev", None, None, None),
        P("lev", None),
        P("lev", None),
    )
    return jax.shard_map(
        shards, mesh=mesh, in_specs=placed, out_specs=P(None, "lev", "xy", None), check_vma=False
    )
```

time: 81.2 us -> 47.2 us (0.58)
  Pallas kernels: 70.3 us -> 47 us
  local copies, waits for them, and re-layouts: 10.5 us -> 0 us
    pallas_call x1, Pallas kernels: 24.3 us -> 5.85 us  [shards(): pl.pallas_call(deposit_kernel, name='deposit', out_shape=shaped(GX, ROWS,...]
    unnamed x25 -> x0, local copies, waits for them, and re-layouts: 10.5 us -> none
    pallas_call x1 -> x2, Pallas kernels: 26 us -> 23.5 us  [the longest x1 22 us: shards(): pl.pallas_call(solve_kernel, name='solve', out_shape=[shaped(GX, ROWS, GY...]
    pallas_call x1, Pallas kernels: 19.9 us -> 17.7 us  [shards(): pl.pallas_call(route_kernel, name='route', out_shape=[shaped(GX, ROWS, GY...]
where the time goes in v2:
time: 47.2 us; the launch traced here: 47.1 us
  Pallas kernels  47 us (100%)
    pallas_call x1, Pallas kernels, shards(): pl.pallas_call(solve_kernel, name='solve', out_shape=[shaped(GX, ROWS, GY...  22 us
    pallas_call x1, Pallas kernels, shards(): pl.pallas_call(route_kernel, name='route', out_shape=[shaped(GX, ROWS, GY...  17.7 us
    pallas_call x1, Pallas kernels, shards(): pl.pallas_call(deposit_kernel, name='deposit', out_shape=shaped(GX, ROWS,...  5.85 us
    pallas_call x1, Pallas kernels, shards(): pl.pallas_call(finish_kernel, name='finish', out_shape=shaped(ROWS, GX, G...  1.43 us

profile of v2, /device:TPU:0, one launch (start us, length us, event | category | flops | bytes accessed | tf_op | source)
XLA Modules:
  0.0 47.1 jit_solution(5108568514171782653)
XLA Ops:
  0.0 17.7 %route.1 = (f32[8,256,256]{2,1,0:T(8,128)S(1)}, f32[32,8,256]{2,1,0:T(8,128)S(1)}, f32[32,256]{1,0:T(8,128)S(1)}, bf16[256,256]{1,0:T(8,128)(2,1)S(1)}, bf16[256...) custom-call(f32[256,8,256]{2,1,0:T(8,128)} %bitcast.4, ...), custom_call_target="tpu_custom_call" | custom-call | tf_op jit(solution)/shard_map/route/pallas_call | solution.py:630
  17.7 5.8 %deposit.1.blended = f32[8,256,256]{2,1,0:T(8,128)S(1)} custom-call(f32[32,8,256]{2,1,0:T(8,128)S(1)} %get-tuple-element.16.got_mass, f32[32,256]{1,0:T(8,128)S(1)} %get-tuple-element.17.got_code, f32[8,256,256]{2,1,0:T(8,128)S(1)} %get-tuple-element.18.first), custom_call_target="tpu_custom_call" | custom-call | tf_op jit(solution)/shard_map/deposit/pallas_call | solution.py:652
  23.6 22.0 %solve.1 = (f32[8,256,256]{2,1,0:T(8,128)S(1)}, f32[8,8,256]{2,1,0:T(8,128)S(1)}, f32[8,8,256]{2,1,0:T(8,128)S(1)}) custom-call(f32[8,256,256]{2,1,0:T(8,128)S(1)} %deposit.1.blended, f32[32,8,256]{2,1,0:T(8,128)} %diffusivity.3, f32[32,8,256]{2,1,0:T(8,128)} %wind.3, bf16[256,256]{1,0:T(8,128)(2,1)S(1)} %get-tuple-element.19.p_high, ...), custom_call_target="tpu_custom_call" | custom-call | tf_op jit(solution)/shard_map/solve/pallas_call | solution.py:666
  45.6 1.4 %finish.1 = f32[256,8,256]{2,1,0:T(8,128)} custom-call(f32[8,256,256]{2,1,0:T(8,128)S(1)} %get-tuple-element.24.second, f32[8,8,256]{2,1,0:T(8,128)S(1)} %get-tuple-element.25.down, f32[8,8,256]{2,1,0:T(8,128)S(1)} %get-tuple-element.26.upward, f32[256,128]{1,0:T(8,128)S(1)} %get-tuple-element.21.p_col, f32[256,128]{1,0:T(8,128)S(1)} %get-tuple-element.22.e_col), custom_call_target="tpu_custom_call" | custom-call | tf_op jit(solution)/shard_map/finish/pallas_call | solution.py:681

commit v3 on v2

--- a/solution.py
+++ b/solution.py
@@ -53,15 +53,15 @@
     return jnp.where(ids == wide, jnp.ones((BLK, width), BF16), jnp.zeros((BLK, width), BF16))
 
 
-def sort_slots(values16, high_low, column, target, slot, count):
+def sort_slots(values16, high_low, column, target, spot, first, count):
     width = target.shape[1]
     chosen = jnp.broadcast_to(target, (16, width)).astype(BF16)
     zero = jnp.zeros((16, width), BF16)
-    parts = [jnp.where(chosen == jnp.array(d, BF16), values16, zero) for d in range(count)]
-    mine = iota((count, width), 0) == target
+    parts = [jnp.where(chosen == jnp.array(first + d, BF16), values16, zero) for d in range(count)]
+    mine = iota((count, width), 0) + float(first) == target
     codes = jnp.concatenate([jnp.where(mine, high_low, 0.0), jnp.where(mine, column, 0.0)], axis=0)
     weighted = jnp.concatenate(parts + [codes.astype(BF16)], axis=0)
-    return lax.dot_general(weighted, one_hot(slot), NT, preferred_element_type=F32)
+    return lax.dot_general(weighted, spot, NT, preferred_element_type=F32)
 
 
 def two_parts(values):
@@ -166,8 +166,8 @@
 def route_kernel(
     euler, mass, dest, cell, diffusivity, wind, inv, low, up,
     first, got_mass, got_code, p_high, p_low, p_col, e_col, factors,
-    ext, diff_s, wind_s, mass_s, dest_in, cell_in, inv_s, low_s, up_s, table_s,
-    send_mass, send_code, dest_s, slot_s, hl_s, col_s, links,
+    ext, diff_s, wind_s, mass_s, dest_in, cell_in, inv_s, low_s, up_s,
+    send_mass, send_code, spot_s, links,
     load_sem, small_sem, halo_send, halo_recv, mass_send, mass_recv, code_send, code_recv, link_send, link_recv,
 ):
     me, level = lax.axis_index("xy"), lax.axis_index("lev")
@@ -196,48 +196,35 @@
     for copy in small + field + coefficients:
         copy.start()
 
+    above, below = lax.rem(me + 1, N_XY), lax.rem(me + N_XY - 1, N_XY)
+    up_copy = remote(ext.at[GX], ext.at[0], halo_send.at[0], halo_recv.at[0], {"xy": above, "lev": level})
+    down_copy = remote(ext.at[1], ext.at[GX + 1], halo_send.at[1], halo_recv.at[1], {"xy": below, "lev": level})
+    field[0].wait()
+    field[GX - 1].wait()
+    pl.semaphore_wait(barrier, N_XY - 1 + N_LEV - 1)
+    up_copy.start()
+    down_copy.start()
+
     def wide(ref):
-        return jnp.concatenate([ref[pl.ds(0, 16, stride=2), :], ref[pl.ds(1, 16, stride=2), :]], axis=1)
-
-    for copy in small[:2]:
+        return lanes([ref[pl.ds(0, 16, stride=2), :], ref[pl.ds(1, 16, stride=2), :]])
+
+    def flat(rows):
+        return lanes([rows[i : i + 1] for i in range(16)])
+
+    for copy in small[:3]:
         copy.wait()
     target = wide(dest_in).astype(F32)
     cells = wide(cell_in)
     levels = cells // (GX * GY)
-    xs = (cells // GY) % GX
-    bucket = xs * 2 + levels // 16
-    dest_s[...] = target
-    hl_s[...] = (bucket * 16 + levels % 16 + 1).astype(F32)
-    col_s[...] = (cells % GY).astype(F32)
+    bucket = (cells // GY) % GX * 2 + levels // 16
+    high_low = flat((bucket * 16 + levels % 16 + 1).astype(F32))
+    column = flat((cells % GY).astype(F32))
     r, c = (lax.broadcasted_iota(I32, (512, 512), d) for d in (0, 1))
     lower = jnp.where((c < r) & (c // 16 == r // 16), 1.0, 0.0).astype(BF16)
     slot, unused_base = ranks(target, N_XY, lower)
-    slot_s[...] = slot
-
-    for copy in field:
-        copy.wait()
-    pl.semaphore_wait(barrier, N_XY - 1 + N_LEV - 1)
-    above, below = lax.rem(me + 1, N_XY), lax.rem(me + N_XY - 1, N_XY)
-    up_copy = remote(ext.at[GX], ext.at[0], halo_send.at[0], halo_recv.at[0], {"xy": above, "lev": level})
-    down_copy = remote(ext.at[1], ext.at[GX + 1], halo_send.at[1], halo_recv.at[1], {"xy": below, "lev": level})
-    up_copy.start()
-    down_copy.start()
-
-    small[2].wait()
-    table_s[...] = jnp.zeros_like(table_s)
-
-    def some_blocks(i, unused):
-        block = pl.ds(pl.multiple_of(i * (PARC // 2), PARC // 2), PARC // 2)
-        take = lambda ref: lanes([ref[pl.ds(i * 8 + j, 1), :] for j in range(8)])
-        table_s[...] += sort_slots(
-            two_parts(mass_s[:, block]), take(hl_s), take(col_s), take(dest_s), take(slot_s), N_XY
-        )
-        return unused
-
-    lax.fori_loop(0, 2, some_blocks, 0)
-    table = table_s[0 : 16 * N_XY].reshape(N_XY, 16, CAP)
-    send_mass[...] = table[:, :8] + table[:, 8:]
-    send_code[...] = table_s[16 * N_XY : 17 * N_XY] * 256.0 + table_s[17 * N_XY :]
+    spot_s[...] = one_hot(flat(slot))
+    values = two_parts(mass_s[...])
+    flat_target = flat(target)
 
     def copies(other, slot_id):
         device = {"xy": other, "lev": level}
@@ -249,12 +236,24 @@
             ),
         )
 
-    def send(k, unused):
-        for copy in copies(lax.rem(me + k, N_XY), me):
-            copy.start()
-        return unused
-
-    lax.fori_loop(1, N_XY, send, 0)
+    half = N_XY // 2
+    for begin in (0, half):
+        table = sort_slots(values, high_low, column, flat_target, spot_s[...], begin, half)
+        masses = table[: 16 * half].reshape(half, 16, CAP)
+        send_mass[begin : begin + half] = masses[:, :8] + masses[:, 8:]
+        send_code[begin : begin + half] = table[16 * half : 17 * half] * 256.0 + table[17 * half :]
+
+        def send(k, unused):
+            other = begin + lax.rem(me + k, half)
+
+            @pl.when(other != me)
+            def _():
+                for copy in copies(other, me):
+                    copy.start()
+
+            return unused
+
+        lax.fori_loop(0, half, send, 0)
     got_mass[me] = send_mass[me]
     got_code[pl.ds(me, 1), :] = send_code[pl.ds(me, 1), :]
 
@@ -274,8 +273,14 @@
     for k in range(1, N_LEV):
         link_copy(k, level).start()
 
-    for copy in coefficients:
+    for copy in field[1 : GX - 1] + coefficients:
         copy.wait()
+
+    def step(x, unused):
+        first[x] = stencil(ext[x + 1], ext[x], ext[x + 2], diff_s[x], wind_s[x])
+        return unused
+
+    lax.fori_loop(1, GX - 1, step, 0)
     up_copy.wait()
     down_copy.wait()
 
@@ -287,11 +292,7 @@
     def _():
         ext[GX + 1] = jnp.zeros((ROWS, GY), F32)
 
-    def step(x, unused):
-        first[x] = stencil(ext[x + 1], ext[x], ext[x + 2], diff_s[x], wind_s[x])
-        return unused
-
-    lax.fori_loop(0, GX, step, 0)
+    lax.fori_loop(0, 2, lambda i, u: step(i * (GX - 1), u), 0)
 
     for k in range(1, N_LEV):
         link_copy(k, lax.rem(level + N_LEV - k, N_LEV)).wait()
@@ -344,7 +345,7 @@
     def one_set(g, unused):
         take = lambda ref: lanes([ref[pl.ds(g * SRC + i, 1), :] for i in range(SRC)])
         values = lanes([two_parts(got_mass[g * SRC + i]) for i in range(SRC)])
-        table = sort_slots(values, take(hl_s), take(col_s), take(hp_s), take(lp_s), SRC)
+        table = sort_slots(values, take(hl_s), take(col_s), take(hp_s), one_hot(take(lp_s)), 0, SRC)
         for half in range(2):
             side = slice(128 * half, 128 * half + 128)
             for d in range(SRC):
@@ -383,7 +384,7 @@
         total[x, :, levels, :] = window(k, 0)
         return unused
 
-    lax.fori_loop(0, BUCKETS, one_bucket, 0, unroll=4)
+    lax.fori_loop(0, BUCKETS, one_bucket, 0, unroll=16)
 
     def rest(k, unused):
         x, levels = place_of(k)
@@ -426,11 +427,14 @@
     return result.reshape(ROWS, GY)
 
 
+PARTS = ((0, 2), (2, 3), (5, 3))
+
+
 def solve_kernel(
     blended, diffusivity, wind, p_high, p_low, p_col, e_col, factors,
     second, down_out, up_out,
-    ext, fixed, triple, diff_s, wind_s, edge, seen, edge2, seen2,
-    load_sem, lev_send, lev_recv, diag_send, diag_recv, halo_send, halo_recv, lev2_send, lev2_recv,
+    ext, fixed, triple, diff_s, wind_s, edge, seen, seen_halo, edge2, seen2,
+    load_sem, lev_send, lev_recv, diag_send, diag_recv, halo_send, halo_recv,
 ):
     me, level = lax.axis_index("xy"), lax.axis_index("lev")
     above, below = lax.rem(me + 1, N_XY), lax.rem(me + N_XY - 1, N_XY)
@@ -454,108 +458,118 @@
     def both(i):
         return lanes([factors[i], factors[i]])
 
-    def edges(values, target, at):
+    def edges(values, target, place):
         blocks = values.reshape(BINS, LEV, GY)
         last, start = blocks[:, LEV - 1, :], blocks[:, 0, :]
-        target[0, at] = last
-        target[1, at] = start + both(10) * last
-
-    def carries(values, at, seen_ref):
+        target[0, place] = last
+        target[1, place] = start + both(10) * last
+
+    def carries(values, seen_at):
         down = jnp.zeros((BINS, GY), F32)
         upward = jnp.zeros((BINS, GY), F32)
         for f in range(N_LEV):
-            here = jnp.where(level == f, 0.0, seen_ref[f, at])
+            here = jnp.where(level == f, 0.0, seen_at(f))
             down += both(f) * here
             upward += both(N_LEV + f) * here
         tail = values.reshape(BINS, LEV, GY)[:, LEV - 1, :]
         return down, upward + both(8) * tail + both(9) * down
 
-    def solve_plane(x, unused):
+    def peer_of(k):
+        return lax.rem(level + k, N_LEV)
+
+    def back(k):
+        return lax.rem(level + N_LEV - k, N_LEV)
+
+    def kind(k):
+        return jnp.where(peer_of(k) > level, 0, 1)
+
+    def lev_copies(turn, part, own):
+        source, target = ((edge, seen), (edge2, seen2))[turn]
+        span = pl.ds(*PARTS[part])
+        return [
+            remote(
+                source.at[kind(k), span], target.at[level if own else back(k), span],
+                lev_send.at[turn, part, k], lev_recv.at[turn, part, k], {"xy": me, "lev": peer_of(k)},
+            )
+            for k in range(1, N_LEV)
+        ]
+
+    def diag_copies(own):
+        return [
+            remote(
+                edge.at[kind(k), 1 - side], seen_halo.at[side, level if own else back(k)],
+                diag_send.at[side, k], diag_recv.at[side, k], {"xy": where, "lev": peer_of(k)},
+            )
+            for side, where in enumerate((above, below))
+            for k in range(1, N_LEV)
+        ]
+
+    def start(copies):
+        for copy in copies:
+            copy.start()
+
+    def wait(copies):
+        for copy in copies:
+            copy.wait()
+
+    def solve_plane(x, place):
         solved = product(blended[x])
         ext[x + 1] = solved
-        edges(solved, edge, x)
-        return unused
-
-    lax.fori_loop(0, 2, lambda i, u: solve_plane(i * (GX - 1), u), 0, unroll=2)
+        edges(solved, edge, place)
+
+    def some(function, begin, count, shift):
+        def one(i, unused):
+            function(i, i + shift)
+            return unused
+
+        lax.fori_loop(begin, begin + count, one, 0, unroll=count)
+
+    solve_plane(0, 0)
+    solve_plane(GX - 1, 1)
     pl.semaphore_wait(barrier, 3 * N_LEV - 1)
-    up_copy = remote(ext.at[GX], ext.at[0], halo_send.at[0], halo_recv.at[0], {"xy": above, "lev": level})
-    down_copy = remote(ext.at[1], ext.at[GX + 1], halo_send.at[1], halo_recv.at[1], {"xy": below, "lev": level})
-    up_copy.start()
-    down_copy.start()
-    lax.fori_loop(1, GX - 1, solve_plane, 0, unroll=3)
-
-    def lev_copies(k, owner):
-        peer = lax.rem(level + k, N_LEV)
-        kind = jnp.where(peer > level, 0, 1)
-        return [
-            remote(
-                edge.at[kind], seen.at[owner, pl.ds(1, GX)], lev_send.at[k], lev_recv.at[k], {"xy": me, "lev": peer}
-            ),
-            remote(
-                edge.at[kind, GX - 1], seen.at[owner, 0], diag_send.at[0, k], diag_recv.at[0, k],
-                {"xy": above, "lev": peer},
-            ),
-            remote(
-                edge.at[kind, 0], seen.at[owner, GX + 1], diag_send.at[1, k], diag_recv.at[1, k],
-                {"xy": below, "lev": peer},
-            ),
-        ]
-
-    def back(k):
-        return lax.rem(level + N_LEV - k, N_LEV)
-
-    out_going = [lev_copies(k, level) for k in range(1, N_LEV)]
-    in_coming = [lev_copies(k, back(k)) for k in range(1, N_LEV)]
-    for i in range(3):
-        for group in out_going:
-            group[i].start()
-    for group in in_coming:
-        group[0].wait()
-
-    def correct_plane(at, unused):
-        down, upward = carries(ext[at], at, seen)
+    halos = [
+        remote(ext.at[GX], ext.at[0], halo_send.at[0], halo_recv.at[0], {"xy": above, "lev": level}),
+        remote(ext.at[1], ext.at[GX + 1], halo_send.at[1], halo_recv.at[1], {"xy": below, "lev": level}),
+    ]
+    start(diag_copies(True) + lev_copies(0, 0, True) + halos)
+    some(solve_plane, 1, 3, 1)
+    start(lev_copies(0, 1, True))
+    some(solve_plane, 4, 3, 1)
+    start(lev_copies(0, 2, True))
+
+    def correct_plane(x, place):
+        down, upward = carries(ext[x + 1], lambda f: seen[f, place])
+        fixed[x + 1] = correction(ext[x + 1], down, upward, p_col, e_col)
+
+    def correct_halo(at, side):
+        down, upward = carries(ext[at], lambda f: seen_halo[side, f])
         fixed[at] = correction(ext[at], down, upward, p_col, e_col)
-        return unused
-
-    lax.fori_loop(1, GX + 1, correct_plane, 0, unroll=2)
-
-    def second_plane(x, at):
+
+    def second_plane(x, place):
         stepped = stencil(fixed[x + 1], fixed[x], fixed[x + 2], diff_s[x], wind_s[x])
         solved = product(stepped)
         second[x] = solved
-        edges(solved, edge2, at)
-
-    for copy in loads:
-        copy.wait()
-
-    parts = ((0, 3), (3, 3), (6, 2))
-
-    def lev2_copies(part, k, owner):
-        peer = lax.rem(level + k, N_LEV)
-        kind = jnp.where(peer > level, 0, 1)
-        begin, size = parts[part]
-        return remote(
-            edge2.at[kind, pl.ds(begin, size)], seen2.at[owner, pl.ds(begin, size)],
-            lev2_send.at[part, k], lev2_recv.at[part, k], {"xy": me, "lev": peer},
-        )
-
-    def inner(at, unused):
-        second_plane(at + 1, at)
-        return unused
-
-    for part in range(2):
-        begin, size = parts[part]
-        lax.fori_loop(begin, begin + size, inner, 0)
-        for k in range(1, N_LEV):
-            lev2_copies(part, k, level).start()
-
-    up_copy.wait()
-    down_copy.wait()
-    for group in in_coming:
-        for copy in group[1:]:
-            copy.wait()
+        edges(solved, edge2, place)
+
+    def last_plane(x, place):
+        down, upward = carries(second[x], lambda f: seen2[f, place])
+        second[x] = correction(second[x], down, upward, p_col, e_col)
+
+    wait(loads)
+    wait(lev_copies(0, 0, False) + lev_copies(0, 1, False))
     correct_plane(0, 0)
-    correct_plane(GX + 1, 0)
+    correct_plane(GX - 1, 1)
+    some(correct_plane, 1, 3, 1)
+    some(second_plane, 1, 2, 1)
+    wait(lev_copies(0, 2, False))
+    some(correct_plane, 4, 3, 1)
+    second_plane(3, 4)
+    start(lev_copies(1, 1, True))
+    some(second_plane, 4, 3, 1)
+    start(lev_copies(1, 2, True))
+    wait(halos + diag_copies(False))
+    correct_halo(0, 0)
+    correct_halo(GX + 1, 1)
 
     @pl.when(me == 0)
     def _():
@@ -565,39 +579,31 @@
     def _():
         fixed[GX + 1] = jnp.zeros((ROWS, GY), F32)
 
-    def outer(i, unused):
-        second_plane(i * (GX - 1), i + 6)
-        return unused
-
-    lax.fori_loop(0, 2, outer, 0)
-    for k in range(1, N_LEV):
-        lev2_copies(2, k, level).start()
-    for part in range(3):
-        for k in range(1, N_LEV):
-            lev2_copies(part, k, back(k)).wait()
-
-    def last_carries(at, unused):
-        x = jnp.where(at < 6, at + 1, (at - 6) * (GX - 1))
-        down, upward = carries(second[x], at, seen2)
-        down_out[x] = down
-        up_out[x] = upward
-        return unused
-
-    lax.fori_loop(0, GX, last_carries, 0, unroll=2)
-
-
-def finish_kernel(second, down, upward, p_col, e_col, out, planes, sem):
-    def copy(x):
-        return pltpu.make_async_copy(planes.at[x], out.at[:, x, :], sem.at[x])
-
-    def one(x, unused):
-        planes[x] = correction(second[x], down[x], upward[x], p_col, e_col)
-        copy(x).start()
-        return unused
-
-    lax.fori_loop(0, GX, one, 0)
-    for x in range(GX):
-        copy(x).wait()
+    second_plane(0, 0)
+    second_plane(GX - 1, 1)
+    start(lev_copies(1, 0, True))
+    for part in (1, 2):
+        wait(lev_copies(1, part, False))
+        some(last_plane, 3 * part - 2, 3, 1)
+    wait(lev_copies(1, 0, False))
+    for side in range(2):
+        down, upward = carries(second[side * (GX - 1)], lambda f: seen2[f, side])
+        down_out[side] = down
+        up_out[side] = upward
+
+
+def finish_kernel(second, down, upward, p_col, e_col, out, outer, sem):
+    inner = [pltpu.make_async_copy(second.at[x], out.at[:, x, :], sem.at[x]) for x in range(1, GX - 1)]
+    for copy in inner:
+        copy.start()
+    last = []
+    for side in range(2):
+        x = side * (GX - 1)
+        outer[side] = correction(second[x], down[side], upward[side], p_col, e_col)
+        last.append(pltpu.make_async_copy(outer.at[side], out.at[:, x, :], sem.at[x]))
+        last[side].start()
+    for copy in inner + last:
+        copy.wait()
 
 
 def vmem(*shape, dtype=F32):
@@ -640,9 +646,8 @@
         scratch_shapes=[
             vmem(GX + 2, ROWS, GY), vmem(GX, LEV, GY), vmem(GX, LEV, GY),
             vmem(BINS, PARC), vmem(32, 128, dtype=I32), vmem(32, 128, dtype=I32),
-            vmem(2, BINS, 16, 16), vmem(2, BINS), vmem(2, BINS), vmem(18 * N_XY, CAP),
-            vmem(N_XY, BINS, CAP), vmem(N_XY, CAP),
-            vmem(16, BLK), vmem(16, BLK), vmem(16, BLK), vmem(16, BLK), vmem(N_LEV, 3, BINS, 128),
+            vmem(2, BINS, 16, 16), vmem(2, BINS), vmem(2, BINS),
+            vmem(N_XY, BINS, CAP), vmem(N_XY, CAP), vmem(CAP, PARC, dtype=BF16), vmem(N_LEV, 3, BINS, 128),
             dma((3, GX)), dma((6,)), dma((2,)), dma((2,)), dma((N_XY,)), dma((N_XY,)), dma((N_XY,)), dma((N_XY,)),
             dma((N_LEV,)), dma((N_LEV,)),
         ],
@@ -666,15 +671,15 @@
     second, down, upward = pl.pallas_call(
         solve_kernel,
         name="solve",
-        out_shape=[shaped(GX, ROWS, GY), shaped(GX, BINS, GY), shaped(GX, BINS, GY)],
+        out_shape=[shaped(GX, ROWS, GY), shaped(2, BINS, GY), shaped(2, BINS, GY)],
         in_specs=whole(1) + somewhere(2) + whole(5),
         out_specs=whole(3),
         scratch_shapes=[
-            vmem(GX + 2, ROWS, GY), vmem(GX + 2, ROWS, GY), vmem(ROWS, 3 * ROWS, dtype=BF16), vmem(GX, LEV, GY), vmem(GX, LEV, GY),
-            vmem(2, GX, BINS, GY), vmem(N_LEV, GX + 2, BINS, GY),
+            vmem(GX + 2, ROWS, GY), vmem(GX + 2, ROWS, GY), vmem(ROWS, 3 * ROWS, dtype=BF16),
+            vmem(GX, LEV, GY), vmem(GX, LEV, GY),
+            vmem(2, GX, BINS, GY), vmem(N_LEV, GX, BINS, GY), vmem(2, N_LEV, BINS, GY),
             vmem(2, GX, BINS, GY), vmem(N_LEV, GX, BINS, GY),
-            dma((2, GX)), dma((N_LEV,)), dma((N_LEV,)), dma((2, N_LEV)), dma((2, N_LEV)), dma((2,)), dma((2,)),
-            dma((3, N_LEV)), dma((3, N_LEV)),
+            dma((2, GX)), dma((2, 3, N_LEV)), dma((2, 3, N_LEV)), dma((2, N_LEV)), dma((2, N_LEV)), dma((2,)), dma((2,)),
         ],
         compiler_params=pltpu.CompilerParams(collective_id=1, has_side_effects=True, vmem_limit_bytes=LIMIT),
     )(blended, diffusivity, wind, p_high, p_low, p_col, e_col, factors)
@@ -684,7 +689,7 @@
         out_shape=shaped(ROWS, GX, GY),
         in_specs=whole(5),
         out_specs=pl.BlockSpec(memory_space=pltpu.HBM),
-        scratch_shapes=[vmem(GX, ROWS, GY), dma((GX,))],
+        scratch_shapes=[vmem(2, ROWS, GY), dma((GX,))],
         compiler_params=pltpu.CompilerParams(vmem_limit_bytes=LIMIT),
     )(second, down, upward, p_col, e_col)
     return result.reshape(BINS, LEV, GX, GY)

time: 47.2 us -> 43.3 us (0.917)
  Pallas kernels: 47 us -> 43.2 us
    pallas_call x1, Pallas kernels: 22 us -> 18.4 us  [shards(): pl.pallas_call(solve_kernel, name='solve', out_shape=[shaped(GX, ROWS, GY...]
    pallas_call x1, Pallas kernels: 5.85 us -> 5.16 us  [shards(): pl.pallas_call(deposit_kernel, name='deposit', out_shape=shaped(GX, ROWS,...]
    pallas_call x1, Pallas kernels: 17.7 us -> 18.2 us  [shards(): pl.pallas_call(route_kernel, name='route', out_shape=[shaped(GX, ROWS, GY...]
where the time goes in v3:
time: 43.3 us; the launch traced here: 43.2 us
  Pallas kernels  43.2 us (100%)
    pallas_call x1, Pallas kernels, shards(): pl.pallas_call(solve_kernel, name='solve', out_shape=[shaped(GX, ROWS, GY...  18.4 us
    pallas_call x1, Pallas kernels, shards(): pl.pallas_call(route_kernel, name='route', out_shape=[shaped(GX, ROWS, GY...  18.2 us
    pallas_call x1, Pallas kernels, shards(): pl.pallas_call(deposit_kernel, name='deposit', out_shape=shaped(GX, ROWS,...  5.16 us
    pallas_call x1, Pallas kernels, shards(): pl.pallas_call(finish_kernel, name='finish', out_shape=shaped(ROWS, GX, G...  1.38 us

profile of v3, /device:TPU:0, one launch (start us, length us, event | category | flops | bytes accessed | tf_op | source)
XLA Modules:
  0.0 43.2 jit_solution(1153163876152996379)
XLA Ops:
  0.0 18.2 %route.1 = (f32[8,256,256]{2,1,0:T(8,128)S(1)}, f32[32,8,256]{2,1,0:T(8,128)S(1)}, f32[32,256]{1,0:T(8,128)S(1)}, bf16[256,256]{1,0:T(8,128)(2,1)S(1)}, bf16[256...) custom-call(f32[256,8,256]{2,1,0:T(8,128)} %bitcast.4, ...), custom_call_target="tpu_custom_call" | custom-call | tf_op jit(solution)/shard_map/route/pallas_call | solution.py:636
  18.2 5.2 %deposit.1.blended = f32[8,256,256]{2,1,0:T(8,128)S(1)} custom-call(f32[32,8,256]{2,1,0:T(8,128)S(1)} %get-tuple-element.16.got_mass, f32[32,256]{1,0:T(8,128)S(1)} %get-tuple-element.17.got_code, f32[8,256,256]{2,1,0:T(8,128)S(1)} %get-tuple-element.18.first), custom_call_target="tpu_custom_call" | custom-call | tf_op jit(solution)/shard_map/deposit/pallas_call | solution.py:657
  23.4 18.4 %solve.1 = (f32[8,256,256]{2,1,0:T(8,128)S(1)}, f32[2,8,256]{2,1,0:T(8,128)S(1)}, f32[2,8,256]{2,1,0:T(8,128)S(1)}) custom-call(f32[8,256,256]{2,1,0:T(8,128)S(1)} %deposit.1.blended, f32[32,8,256]{2,1,0:T(8,128)} %diffusivity.3, f32[32,8,256]{2,1,0:T(8,128)} %wind.3, bf16[256,256]{1,0:T(8,128)(2,1)S(1)} %get-tuple-element.19.p_high, ...), custom_call_target="tpu_custom_call" | custom-call | tf_op jit(solution)/shard_map/solve/pallas_call | solution.py:671
  41.8 1.4 %finish.1 = f32[256,8,256]{2,1,0:T(8,128)} custom-call(f32[8,256,256]{2,1,0:T(8,128)S(1)} %get-tuple-element.24.second, f32[2,8,256]{2,1,0:T(8,128)S(1)} %get-tuple-element.25.down, f32[2,8,256]{2,1,0:T(8,128)S(1)} %get-tuple-element.26.upward, f32[256,128]{1,0:T(8,128)S(1)} %get-tuple-element.21.p_col, f32[256,128]{1,0:T(8,128)S(1)} %get-tuple-element.22.e_col), custom_call_target="tpu_custom_call" | custom-call | tf_op jit(solution)/shard_map/finish/pallas_call | solution.py:686

commit v4 on v3

--- a/solution.py
+++ b/solution.py
@@ -80,6 +80,22 @@
     return result.reshape(ROWS, GY)
 
 
+def at_edges(me, upward, downward, action):
+    @pl.when(me < N_XY - 1)
+    def _():
+        for copy in upward:
+            copy.start() if action == "start" else copy.wait_send()
+        for copy in downward if action == "wait" else []:
+            copy.wait_recv()
+
+    @pl.when(me > 0)
+    def _():
+        for copy in downward:
+            copy.start() if action == "start" else copy.wait_send()
+        for copy in upward if action == "wait" else []:
+            copy.wait_recv()
+
+
 def plane_copies(source, target, sems, at=0):
     return [pltpu.make_async_copy(source.at[:, x, :], target.at[at + x], sems.at[x]) for x in range(GX)]
 
@@ -90,7 +106,7 @@
     )
 
 
-def compose(inv, low, up, hi_ref, lo_ref, p_ref, e_ref):
+def compose(inv, low, up, triple, p_ref, e_ref):
     lane16 = lax.broadcasted_iota(I32, (16, ROWS), 1) % LEV
     row16 = lax.broadcasted_iota(I32, (16, ROWS), 0)
     own = lax.broadcasted_iota(I32, (BINS, 16, ROWS), 0) == (
@@ -121,8 +137,9 @@
     p1 = t1 + (l1 * m1_first) * tail0
     full = jnp.concatenate([p0, p1], axis=1).reshape(ROWS, ROWS)
     high = full.astype(BF16)
-    hi_ref[...] = high
-    lo_ref[...] = (full - high.astype(F32)).astype(BF16)
+    triple[:, 0:ROWS] = high
+    triple[:, ROWS : 2 * ROWS] = high
+    triple[:, 2 * ROWS :] = (full - high.astype(F32)).astype(BF16)
     passed = l1 * l0 * m0[:, 15:16, 0:1]
     c0 = l0 * m0_first + (u0 * m0_last) * (passed * m1[:, 0:1, 0:1])
     c1 = passed * m1_first
@@ -165,7 +182,7 @@
 
 def route_kernel(
     euler, mass, dest, cell, diffusivity, wind, inv, low, up,
-    first, got_mass, got_code, p_high, p_low, p_col, e_col, factors,
+    first, got_mass, got_code, order, triple, p_col, e_col, factors,
     ext, diff_s, wind_s, mass_s, dest_in, cell_in, inv_s, low_s, up_s,
     send_mass, send_code, spot_s, links,
     load_sem, small_sem, halo_send, halo_recv, mass_send, mass_recv, code_send, code_recv, link_send, link_recv,
@@ -193,18 +210,12 @@
     ]
     field = plane_copies(euler, ext, load_sem.at[0], 1)
     coefficients = plane_copies(diffusivity, diff_s, load_sem.at[1]) + plane_copies(wind, wind_s, load_sem.at[2])
-    for copy in small + field + coefficients:
+    for copy in small[:3] + [field[0], field[GX - 1]]:
         copy.start()
 
     above, below = lax.rem(me + 1, N_XY), lax.rem(me + N_XY - 1, N_XY)
     up_copy = remote(ext.at[GX], ext.at[0], halo_send.at[0], halo_recv.at[0], {"xy": above, "lev": level})
     down_copy = remote(ext.at[1], ext.at[GX + 1], halo_send.at[1], halo_recv.at[1], {"xy": below, "lev": level})
-    field[0].wait()
-    field[GX - 1].wait()
-    pl.semaphore_wait(barrier, N_XY - 1 + N_LEV - 1)
-    up_copy.start()
-    down_copy.start()
-
     def wide(ref):
         return lanes([ref[pl.ds(0, 16, stride=2), :], ref[pl.ds(1, 16, stride=2), :]])
 
@@ -222,6 +233,12 @@
     r, c = (lax.broadcasted_iota(I32, (512, 512), d) for d in (0, 1))
     lower = jnp.where((c < r) & (c // 16 == r // 16), 1.0, 0.0).astype(BF16)
     slot, unused_base = ranks(target, N_XY, lower)
+    for copy in small[3:] + field[1 : GX - 1] + coefficients:
+        copy.start()
+    field[0].wait()
+    field[GX - 1].wait()
+    pl.semaphore_wait(barrier, N_XY - 1 + N_LEV - 1)
+    at_edges(me, [up_copy], [down_copy], "start")
     spot_s[...] = one_hot(flat(slot))
     values = two_parts(mass_s[...])
     flat_target = flat(target)
@@ -259,7 +276,9 @@
 
     for copy in small[3:]:
         copy.wait()
-    compose(inv_s, low_s, up_s, p_high, p_low, p_col, e_col)
+    compose(inv_s, low_s, up_s, triple, p_col, e_col)
+    r, c = (lax.broadcasted_iota(I32, (N_XY * (BUCKETS + 1), N_XY * BUCKETS), d) for d in (0, 1))
+    order[...] = jnp.where((c < r) & (c % N_XY // SRC == r % N_XY // SRC), 1.0, 0.0).astype(BF16)
     links[level, 0] = p_col[pl.ds(LEV - 1, BINS, stride=LEV), :]
     links[level, 1] = e_col[pl.ds(0, BINS, stride=LEV), :]
     links[level, 2] = p_col[pl.ds(0, BINS, stride=LEV), :]
@@ -281,8 +300,7 @@
         return unused
 
     lax.fori_loop(1, GX - 1, step, 0)
-    up_copy.wait()
-    down_copy.wait()
+    at_edges(me, [up_copy], [down_copy], "wait")
 
     @pl.when(me == 0)
     def _():
@@ -309,8 +327,8 @@
 
 
 def deposit_kernel(
-    got_mass, got_code, first, blended,
-    rows_u, hl_u, col_u, hp_s, lp_s, hl_s, col_s, total, starts_v, starts_s, sem,
+    got_mass, got_code, order, total,
+    rows_u, hl_u, col_u, hp_s, lp_s, hl_s, col_s, starts_v, starts_s, sem,
 ):
     code = got_code[...].astype(I32)
     hl = code // 256
@@ -319,9 +337,7 @@
     key = jnp.where(valid, (hl - 1) // 16, -1).astype(F32)
     hl_s[...] = hl.astype(F32)
     col_s[...] = col.astype(F32)
-    r, c = (lax.broadcasted_iota(I32, (N_XY * (BUCKETS + 1), 512), d) for d in (0, 1))
-    lower = jnp.where((c < r) & ((c % N_XY) // SRC == (r % N_XY) // SRC), 1.0, 0.0).astype(BF16)
-    position, base = ranks(key, BUCKETS, lower)
+    position, base = ranks(key, BUCKETS, order[...])
     place = position.astype(I32)
     hp_s[...] = jnp.where(valid, place // BLK, -1).astype(F32)
     lp_s[...] = (place % BLK).astype(F32)
@@ -408,16 +424,6 @@
     def _():
         lax.fori_loop(0, BUCKETS, rest, 0)
 
-    def blend(x, unused):
-        counts = total[x, 8]
-        share = counts / (counts + 2.0)
-        old = first[x].reshape(BINS, LEV, GY)
-        mixed = (1.0 - share)[None] * old + share[None] * total[x, 0:8]
-        blended[x] = mixed.reshape(ROWS, GY)
-        return unused
-
-    lax.fori_loop(0, GX, blend, 0)
-
 
 def correction(values, down, upward, p_col, e_col):
     shape = (BINS, LEV, GY)
@@ -431,25 +437,27 @@
 
 
 def solve_kernel(
-    blended, diffusivity, wind, p_high, p_low, p_col, e_col, factors,
+    total, first, diffusivity, wind, triple, p_col, e_col, factors,
     second, down_out, up_out,
-    ext, fixed, triple, diff_s, wind_s, edge, seen, seen_halo, edge2, seen2,
+    ext, fixed, diff_s, wind_s, edge, seen, seen_halo, edge2, seen2,
     load_sem, lev_send, lev_recv, diag_send, diag_recv, halo_send, halo_recv,
 ):
     me, level = lax.axis_index("xy"), lax.axis_index("lev")
     above, below = lax.rem(me + 1, N_XY), lax.rem(me + N_XY - 1, N_XY)
     barrier = pltpu.get_barrier_semaphore()
-    for k in range(N_LEV):
-        peer = lax.rem(level + k, N_LEV)
-        for where in ([me] if k else []) + [above, below]:
-            pl.semaphore_signal(barrier, inc=1, device_id={"xy": where, "lev": peer}, device_id_type=MESH)
+
+    def greet(where, least):
+        for k in range(least, N_LEV):
+            device = {"xy": where, "lev": lax.rem(level + k, N_LEV)}
+            pl.semaphore_signal(barrier, inc=1, device_id=device, device_id_type=MESH)
+
+    greet(me, 1)
+    pl.when(me < N_XY - 1)(lambda: greet(above, 0))
+    pl.when(me > 0)(lambda: greet(below, 0))
+    sides = jnp.where(me < N_XY - 1, 1, 0) + jnp.where(me > 0, 1, 0)
     loads = plane_copies(diffusivity, diff_s, load_sem.at[0]) + plane_copies(wind, wind_s, load_sem.at[1])
     for copy in loads:
         copy.start()
-    triple[:, 0:ROWS] = p_high[...]
-    triple[:, ROWS : 2 * ROWS] = p_high[...]
-    triple[:, 2 * ROWS :] = p_low[...]
-
     def product(values):
         high = values.astype(BF16)
         low = (values - high.astype(F32)).astype(BF16)
@@ -513,7 +521,11 @@
             copy.wait()
 
     def solve_plane(x, place):
-        solved = product(blended[x])
+        counts = total[x, BINS]
+        share = counts / (counts + 2.0)
+        old = first[x].reshape(BINS, LEV, GY)
+        blended = (1.0 - share)[None] * old + share[None] * total[x, 0:BINS]
+        solved = product(blended.reshape(ROWS, GY))
         ext[x + 1] = solved
         edges(solved, edge, place)
 
@@ -526,12 +538,16 @@
 
     solve_plane(0, 0)
     solve_plane(GX - 1, 1)
-    pl.semaphore_wait(barrier, 3 * N_LEV - 1)
+    pl.semaphore_wait(barrier, N_LEV - 1 + N_LEV * sides)
     halos = [
         remote(ext.at[GX], ext.at[0], halo_send.at[0], halo_recv.at[0], {"xy": above, "lev": level}),
         remote(ext.at[1], ext.at[GX + 1], halo_send.at[1], halo_recv.at[1], {"xy": below, "lev": level}),
     ]
-    start(diag_copies(True) + lev_copies(0, 0, True) + halos)
+    sent = diag_copies(True)
+    seen_in = diag_copies(False)
+    at_edges(me, sent[: N_LEV - 1], sent[N_LEV - 1 :], "start")
+    start(lev_copies(0, 0, True))
+    at_edges(me, halos[:1], halos[1:], "start")
     some(solve_plane, 1, 3, 1)
     start(lev_copies(0, 1, True))
     some(solve_plane, 4, 3, 1)
@@ -567,9 +583,9 @@
     start(lev_copies(1, 1, True))
     some(second_plane, 4, 3, 1)
     start(lev_copies(1, 2, True))
-    wait(halos + diag_copies(False))
-    correct_halo(0, 0)
-    correct_halo(GX + 1, 1)
+    at_edges(me, seen_in[: N_LEV - 1] + halos[:1], seen_in[N_LEV - 1 :] + halos[1:], "wait")
+    pl.when(me > 0)(lambda: correct_halo(0, 0))
+    pl.when(me < N_XY - 1)(lambda: correct_halo(GX + 1, 1))
 
     @pl.when(me == 0)
     def _():
@@ -638,7 +654,7 @@
         name="route",
         out_shape=[
             shaped(GX, ROWS, GY), shaped(N_XY, BINS, CAP), shaped(N_XY, CAP),
-            shaped(ROWS, ROWS, dtype=BF16), shaped(ROWS, ROWS, dtype=BF16),
+            shaped(N_XY * (BUCKETS + 1), N_XY * BUCKETS, dtype=BF16), shaped(ROWS, 3 * ROWS, dtype=BF16),
             shaped(ROWS, 128), shaped(ROWS, 128), shaped(11, BINS, 128),
         ],
         in_specs=somewhere(9),
@@ -653,36 +669,35 @@
         ],
         compiler_params=pltpu.CompilerParams(collective_id=0, has_side_effects=True, vmem_limit_bytes=LIMIT),
     )(euler, mass, dest, cell, diffusivity, wind, inv, low, up)
-    first, got_mass, got_code, p_high, p_low, p_col, e_col, factors = routed
-    blended = pl.pallas_call(
+    first, got_mass, got_code, order, triple, p_col, e_col, factors = routed
+    total = pl.pallas_call(
         deposit_kernel,
         name="deposit",
-        out_shape=shaped(GX, ROWS, GY),
+        out_shape=shaped(GX, BINS + 1, LEV, GY),
         in_specs=whole(3),
         out_specs=pl.BlockSpec(memory_space=pltpu.VMEM),
         scratch_shapes=[
             vmem(SETS, UNITS + WIN, 16, 128), vmem(SETS, UNITS + 8, 128), vmem(SETS, UNITS + 8, 128),
             vmem(N_XY, BLK), vmem(N_XY, BLK), vmem(N_XY, BLK), vmem(N_XY, BLK),
-            vmem(GX, BINS + 1, LEV, GY), vmem(BUCKETS + 8, 128, dtype=I32),
-            pltpu.SMEM((BUCKETS + 8, 128), I32), dma,
+            vmem(BUCKETS + 8, 128, dtype=I32), pltpu.SMEM((BUCKETS + 8, 128), I32), dma,
         ],
         compiler_params=pltpu.CompilerParams(vmem_limit_bytes=LIMIT),
-    )(got_mass, got_code, first)
+    )(got_mass, got_code, order)
     second, down, upward = pl.pallas_call(
         solve_kernel,
         name="solve",
         out_shape=[shaped(GX, ROWS, GY), shaped(2, BINS, GY), shaped(2, BINS, GY)],
-        in_specs=whole(1) + somewhere(2) + whole(5),
+        in_specs=whole(2) + somewhere(2) + whole(4),
         out_specs=whole(3),
         scratch_shapes=[
-            vmem(GX + 2, ROWS, GY), vmem(GX + 2, ROWS, GY), vmem(ROWS, 3 * ROWS, dtype=BF16),
+            vmem(GX + 2, ROWS, GY), vmem(GX + 2, ROWS, GY),
             vmem(GX, LEV, GY), vmem(GX, LEV, GY),
             vmem(2, GX, BINS, GY), vmem(N_LEV, GX, BINS, GY), vmem(2, N_LEV, BINS, GY),
             vmem(2, GX, BINS, GY), vmem(N_LEV, GX, BINS, GY),
             dma((2, GX)), dma((2, 3, N_LEV)), dma((2, 3, N_LEV)), dma((2, N_LEV)), dma((2, N_LEV)), dma((2,)), dma((2,)),
         ],
         compiler_params=pltpu.CompilerParams(collective_id=1, has_side_effects=True, vmem_limit_bytes=LIMIT),
-    )(blended, diffusivity, wind, p_high, p_low, p_col, e_col, factors)
+    )(total, first, diffusivity, wind, triple, p_col, e_col, factors)
     result = pl.pallas_call(
         finish_kernel,
         name="finish",

time: 43.3 us -> 41.2 us (0.952)
  the two profiles are of different devices: /device:TPU:0 before, /device:TPU:1 now
where the time goes in v4:
time: 41.2 us; the launch traced here: 41 us
  Pallas kernels  41 us (100%)
    pallas_call x1, Pallas kernels, shards(): pl.pallas_call(route_kernel, name='route', out_shape=[shaped(GX, ROWS, GY...  18 us
    pallas_call x1, Pallas kernels, shards(): pl.pallas_call(solve_kernel, name='solve', out_shape=[shaped(GX, ROWS, GY...  16.8 us
    pallas_call x1, Pallas kernels, shards(): pl.pallas_call(deposit_kernel, name='deposit', out_shape=shaped(GX, BINS...  4.84 us
    pallas_call x1, Pallas kernels, shards(): pl.pallas_call(finish_kernel, name='finish', out_shape=shaped(ROWS, GX, G...  1.38 us

profile of v4, /device:TPU:1, one launch (start us, length us, event | category | flops | bytes accessed | tf_op | source)
XLA Modules:
  0.0 41.0 jit_solution(7901968962066635458)
XLA Ops:
  0.0 18.0 %route.1 = (f32[8,256,256]{2,1,0:T(8,128)S(1)}, f32[32,8,256]{2,1,0:T(8,128)S(1)}, f32[32,256]{1,0:T(8,128)S(1)}, bf16[544,512]{1,0:T(8,128)(2,1)S(1)}, bf16[256...) custom-call(f32[256,8,256]{2,1,0:T(8,128)} %bitcast.4, ...), custom_call_target="tpu_custom_call" | custom-call | tf_op jit(solution)/shard_map/route/pallas_call | solution.py:652
  18.0 4.8 %deposit.1.total = f32[8,9,32,256]{3,2,1,0:T(8,128)S(1)} custom-call(f32[32,8,256]{2,1,0:T(8,128)S(1)} %get-tuple-element.16.got_mass, f32[32,256]{1,0:T(8,128)S(1)} %get-tuple-element.17.got_code, bf16[544,512]{1,0:T(8,128)(2,1)S(1)} %get-tuple-element.18.order), custom_call_target="tpu_custom_call" | custom-call | tf_op jit(solution)/shard_map/deposit/pallas_call | solution.py:673
  22.9 16.8 %solve.1 = (f32[8,256,256]{2,1,0:T(8,128)S(1)}, f32[2,8,256]{2,1,0:T(8,128)S(1)}, f32[2,8,256]{2,1,0:T(8,128)S(1)}) custom-call(f32[8,9,32,256]{3,2,1,0:T(8,128)S(1)} %deposit.1.total, f32[8,256,256]{2,1,0:T(8,128)S(1)} %get-tuple-element.19.first, f32[32,8,256]{2,1,0:T(8,128)} %diffusivity.3, f32[32,8,256]{2,1,0:T(8,128)} %wind.3, ...), custom_call_target="tpu_custom_call" | custom-call | tf_op jit(solution)/shard_map/solve/pallas_call | solution.py:686
  39.7 1.4 %finish.1 = f32[256,8,256]{2,1,0:T(8,128)} custom-call(f32[8,256,256]{2,1,0:T(8,128)S(1)} %get-tuple-element.24.second, f32[2,8,256]{2,1,0:T(8,128)S(1)} %get-tuple-element.25.down, f32[2,8,256]{2,1,0:T(8,128)S(1)} %get-tuple-element.26.upward, f32[256,128]{1,0:T(8,128)S(1)} %get-tuple-element.21.p_col, f32[256,128]{1,0:T(8,128)S(1)} %get-tuple-element.22.e_col), custom_call_target="tpu_custom_call" | custom-call | tf_op jit(solution)/shard_map/finish/pallas_call | solution.py:701

commit v5 on v4

--- a/solution.py
+++ b/solution.py
@@ -210,12 +210,15 @@
     ]
     field = plane_copies(euler, ext, load_sem.at[0], 1)
     coefficients = plane_copies(diffusivity, diff_s, load_sem.at[1]) + plane_copies(wind, wind_s, load_sem.at[2])
-    for copy in small[:3] + [field[0], field[GX - 1]]:
+    for copy in small[:3]:
         copy.start()
 
     above, below = lax.rem(me + 1, N_XY), lax.rem(me + N_XY - 1, N_XY)
-    up_copy = remote(ext.at[GX], ext.at[0], halo_send.at[0], halo_recv.at[0], {"xy": above, "lev": level})
-    down_copy = remote(ext.at[1], ext.at[GX + 1], halo_send.at[1], halo_recv.at[1], {"xy": below, "lev": level})
+    up_copy = remote(euler.at[:, GX - 1, :], ext.at[0], halo_send.at[0], halo_recv.at[0], {"xy": above, "lev": level})
+    down_copy = remote(euler.at[:, 0, :], ext.at[GX + 1], halo_send.at[1], halo_recv.at[1], {"xy": below, "lev": level})
+    pl.semaphore_wait(barrier, N_XY - 1 + N_LEV - 1)
+    at_edges(me, [up_copy], [down_copy], "start")
+
     def wide(ref):
         return lanes([ref[pl.ds(0, 16, stride=2), :], ref[pl.ds(1, 16, stride=2), :]])
 
@@ -233,12 +236,8 @@
     r, c = (lax.broadcasted_iota(I32, (512, 512), d) for d in (0, 1))
     lower = jnp.where((c < r) & (c // 16 == r // 16), 1.0, 0.0).astype(BF16)
     slot, unused_base = ranks(target, N_XY, lower)
-    for copy in small[3:] + field[1 : GX - 1] + coefficients:
+    for copy in small[3:] + field + coefficients:
         copy.start()
-    field[0].wait()
-    field[GX - 1].wait()
-    pl.semaphore_wait(barrier, N_XY - 1 + N_LEV - 1)
-    at_edges(me, [up_copy], [down_copy], "start")
     spot_s[...] = one_hot(flat(slot))
     values = two_parts(mass_s[...])
     flat_target = flat(target)
@@ -292,7 +291,7 @@
     for k in range(1, N_LEV):
         link_copy(k, level).start()
 
-    for copy in field[1 : GX - 1] + coefficients:
+    for copy in field + coefficients:
         copy.wait()
 
     def step(x, unused):
@@ -433,14 +432,14 @@
     return result.reshape(ROWS, GY)
 
 
-PARTS = ((0, 2), (2, 3), (5, 3))
+PARTS = (((0, 2), (2, 3), (5, 3)), ((0, 3), (3, 3), (6, 2)))
 
 
 def solve_kernel(
     total, first, diffusivity, wind, triple, p_col, e_col, factors,
     second, down_out, up_out,
-    ext, fixed, diff_s, wind_s, edge, seen, seen_halo, edge2, seen2,
-    load_sem, lev_send, lev_recv, diag_send, diag_recv, halo_send, halo_recv,
+    ext, fixed, diff_s, wind_s, sum_s, beside, edge, seen, seen_halo, edge2, seen2, edge3, seen_halo2,
+    load_sem, lev_send, lev_recv, diag_send, diag_recv, halo_send, halo_recv, side_send, side_recv,
 ):
     me, level = lax.axis_index("xy"), lax.axis_index("lev")
     above, below = lax.rem(me + 1, N_XY), lax.rem(me + N_XY - 1, N_XY)
@@ -493,7 +492,7 @@
 
     def lev_copies(turn, part, own):
         source, target = ((edge, seen), (edge2, seen2))[turn]
-        span = pl.ds(*PARTS[part])
+        span = pl.ds(*PARTS[turn][part])
         return [
             remote(
                 source.at[kind(k), span], target.at[level if own else back(k), span],
@@ -502,11 +501,12 @@
             for k in range(1, N_LEV)
         ]
 
-    def diag_copies(own):
+    def diag_copies(turn, own):
+        source, target = ((edge, seen_halo), (edge3, seen_halo2))[turn]
         return [
             remote(
-                edge.at[kind(k), 1 - side], seen_halo.at[side, level if own else back(k)],
-                diag_send.at[side, k], diag_recv.at[side, k], {"xy": where, "lev": peer_of(k)},
+                source.at[kind(k), 1 - side], target.at[side, level if own else back(k)],
+                diag_send.at[turn, side, k], diag_recv.at[turn, side, k], {"xy": where, "lev": peer_of(k)},
             )
             for side, where in enumerate((above, below))
             for k in range(1, N_LEV)
@@ -538,15 +538,25 @@
 
     solve_plane(0, 0)
     solve_plane(GX - 1, 1)
+    wait(loads)
+    sum_s[...] = diff_s[0] + wind_s[0]
+    fixed[0] = jnp.zeros((ROWS, GY), F32)
+    fixed[GX + 1] = jnp.zeros((ROWS, GY), F32)
     pl.semaphore_wait(barrier, N_LEV - 1 + N_LEV * sides)
     halos = [
         remote(ext.at[GX], ext.at[0], halo_send.at[0], halo_recv.at[0], {"xy": above, "lev": level}),
         remote(ext.at[1], ext.at[GX + 1], halo_send.at[1], halo_recv.at[1], {"xy": below, "lev": level}),
     ]
-    sent = diag_copies(True)
-    seen_in = diag_copies(False)
-    at_edges(me, sent[: N_LEV - 1], sent[N_LEV - 1 :], "start")
+    weights = [
+        remote(diff_s.at[GX - 1], beside.at[0], side_send.at[0], side_recv.at[0], {"xy": above, "lev": level}),
+        remote(sum_s, beside.at[1], side_send.at[1], side_recv.at[1], {"xy": below, "lev": level}),
+    ]
+    sent, seen_in = diag_copies(0, True), diag_copies(0, False)
+    sent2, seen_in2 = diag_copies(1, True), diag_copies(1, False)
+    three = N_LEV - 1
+    at_edges(me, sent[:three], sent[three:], "start")
     start(lev_copies(0, 0, True))
+    at_edges(me, weights[:1], weights[1:], "start")
     at_edges(me, halos[:1], halos[1:], "start")
     some(solve_plane, 1, 3, 1)
     start(lev_copies(0, 1, True))
@@ -557,9 +567,8 @@
         down, upward = carries(ext[x + 1], lambda f: seen[f, place])
         fixed[x + 1] = correction(ext[x + 1], down, upward, p_col, e_col)
 
-    def correct_halo(at, side):
-        down, upward = carries(ext[at], lambda f: seen_halo[side, f])
-        fixed[at] = correction(ext[at], down, upward, p_col, e_col)
+    def scaled(plane, values):
+        return (plane[None] * values.reshape(BINS, LEV, GY)).reshape(ROWS, GY)
 
     def second_plane(x, place):
         stepped = stencil(fixed[x + 1], fixed[x], fixed[x + 2], diff_s[x], wind_s[x])
@@ -567,57 +576,76 @@
         second[x] = solved
         edges(solved, edge2, place)
 
-    def last_plane(x, place):
-        down, upward = carries(second[x], lambda f: seen2[f, place])
-        second[x] = correction(second[x], down, upward, p_col, e_col)
-
-    wait(loads)
+    def share_up():
+        edges(product(scaled(beside[1], fixed[GX])), edge3, 1)
+        start(sent2[:three])
+
+    def share_down():
+        edges(product(scaled(beside[0], fixed[1])), edge3, 0)
+        start(sent2[three:])
+
     wait(lev_copies(0, 0, False) + lev_copies(0, 1, False))
     correct_plane(0, 0)
     correct_plane(GX - 1, 1)
+    at_edges(me, weights[:1], weights[1:], "wait")
+    pl.when(me < N_XY - 1)(share_up)
+    pl.when(me > 0)(share_down)
     some(correct_plane, 1, 3, 1)
-    some(second_plane, 1, 2, 1)
+    some(second_plane, 0, 3, 0)
+    start(lev_copies(1, 0, True))
     wait(lev_copies(0, 2, False))
     some(correct_plane, 4, 3, 1)
-    second_plane(3, 4)
+    some(second_plane, 3, 3, 0)
     start(lev_copies(1, 1, True))
-    some(second_plane, 4, 3, 1)
+    some(second_plane, 6, 2, 0)
     start(lev_copies(1, 2, True))
-    at_edges(me, seen_in[: N_LEV - 1] + halos[:1], seen_in[N_LEV - 1 :] + halos[1:], "wait")
-    pl.when(me > 0)(lambda: correct_halo(0, 0))
-    pl.when(me < N_XY - 1)(lambda: correct_halo(GX + 1, 1))
-
-    @pl.when(me == 0)
-    def _():
-        fixed[0] = jnp.zeros((ROWS, GY), F32)
-
-    @pl.when(me == N_XY - 1)
-    def _():
-        fixed[GX + 1] = jnp.zeros((ROWS, GY), F32)
-
-    second_plane(0, 0)
-    second_plane(GX - 1, 1)
-    start(lev_copies(1, 0, True))
-    for part in (1, 2):
+
+    at_edges(me, seen_in[:three] + halos[:1], seen_in[three:] + halos[1:], "wait")
+
+    def add_halo(at, side, x, plane):
+        down, upward = carries(ext[at], lambda f: seen_halo[side, f])
+        halo = correction(ext[at], down, upward, p_col, e_col)
+        second[x] += product(scaled(plane, halo))
+
+    pl.when(me > 0)(lambda: add_halo(0, 0, 0, sum_s[...]))
+    pl.when(me < N_XY - 1)(lambda: add_halo(GX + 1, 1, GX - 1, diff_s[GX - 1]))
+    at_edges(me, seen_in2[:three], seen_in2[three:], "wait")
+
+    def no_share(side):
+        seen_halo2[side] = jnp.zeros((N_LEV, BINS, GY), F32)
+
+    pl.when(me == 0)(lambda: no_share(0))
+    pl.when(me == N_XY - 1)(lambda: no_share(1))
+
+    def seen_at(x):
+        if x == 0:
+            return lambda f: seen2[f, 0] + seen_halo2[0, f]
+        if x == GX - 1:
+            return lambda f: seen2[f, GX - 1] + seen_halo2[1, f]
+        return lambda f: seen2[f, x]
+
+    for part in range(2):
         wait(lev_copies(1, part, False))
-        some(last_plane, 3 * part - 2, 3, 1)
-    wait(lev_copies(1, 0, False))
-    for side in range(2):
-        down, upward = carries(second[side * (GX - 1)], lambda f: seen2[f, side])
-        down_out[side] = down
-        up_out[side] = upward
+        for x in range(3 * part, 3 * part + 3):
+            down, upward = carries(second[x], seen_at(x))
+            second[x] = correction(second[x], down, upward, p_col, e_col)
+    wait(lev_copies(1, 2, False))
+    for x in range(6, GX):
+        down, upward = carries(second[x], seen_at(x))
+        down_out[x - 6] = down
+        up_out[x - 6] = upward
 
 
 def finish_kernel(second, down, upward, p_col, e_col, out, outer, sem):
-    inner = [pltpu.make_async_copy(second.at[x], out.at[:, x, :], sem.at[x]) for x in range(1, GX - 1)]
+    inner = [pltpu.make_async_copy(second.at[x], out.at[:, x, :], sem.at[x]) for x in range(6)]
     for copy in inner:
         copy.start()
     last = []
-    for side in range(2):
-        x = side * (GX - 1)
-        outer[side] = correction(second[x], down[side], upward[side], p_col, e_col)
-        last.append(pltpu.make_async_copy(outer.at[side], out.at[:, x, :], sem.at[x]))
-        last[side].start()
+    for i in range(2):
+        x = 6 + i
+        outer[i] = correction(second[x], down[i], upward[i], p_col, e_col)
+        last.append(pltpu.make_async_copy(outer.at[i], out.at[:, x, :], sem.at[x]))
+        last[i].start()
     for copy in inner + last:
         copy.wait()
 
@@ -691,10 +719,11 @@
         out_specs=whole(3),
         scratch_shapes=[
             vmem(GX + 2, ROWS, GY), vmem(GX + 2, ROWS, GY),
-            vmem(GX, LEV, GY), vmem(GX, LEV, GY),
+            vmem(GX, LEV, GY), vmem(GX, LEV, GY), vmem(LEV, GY), vmem(2, LEV, GY),
             vmem(2, GX, BINS, GY), vmem(N_LEV, GX, BINS, GY), vmem(2, N_LEV, BINS, GY),
-            vmem(2, GX, BINS, GY), vmem(N_LEV, GX, BINS, GY),
-            dma((2, GX)), dma((2, 3, N_LEV)), dma((2, 3, N_LEV)), dma((2, N_LEV)), dma((2, N_LEV)), dma((2,)), dma((2,)),
+            vmem(2, GX, BINS, GY), vmem(N_LEV, GX, BINS, GY), vmem(2, 2, BINS, GY), vmem(2, N_LEV, BINS, GY),
+            dma((2, GX)), dma((2, 3, N_LEV)), dma((2, 3, N_LEV)), dma((2, 2, N_LEV)), dma((2, 2, N_LEV)),
+            dma((2,)), dma((2,)), dma((2,)), dma((2,)),
         ],
         compiler_params=pltpu.CompilerParams(collective_id=1, has_side_effects=True, vmem_limit_bytes=LIMIT),
     )(total, first, diffusivity, wind, triple, p_col, e_col, factors)

time: 41.2 us -> 41.6 us (level)
    pallas_call x1, Pallas kernels: 18 us -> 18.6 us  [shards(): pl.pallas_call(route_kernel, name='route', out_shape=[shaped(GX, ROWS, GY...]
where the time goes in v5:
time: 41.6 us; the launch traced here: 41.5 us
  Pallas kernels  41.4 us (100%)
    pallas_call x1, Pallas kernels, shards(): pl.pallas_call(route_kernel, name='route', out_shape=[shaped(GX, ROWS, GY...  18.6 us
    pallas_call x1, Pallas kernels, shards(): pl.pallas_call(solve_kernel, name='solve', out_shape=[shaped(GX, ROWS, GY...  16.7 us
    pallas_call x1, Pallas kernels, shards(): pl.pallas_call(deposit_kernel, name='deposit', out_shape=shaped(GX, BINS...  4.83 us
    pallas_call x1, Pallas kernels, shards(): pl.pallas_call(finish_kernel, name='finish', out_shape=shaped(ROWS, GX, G...  1.38 us

profile of v5, /device:TPU:1, one launch (start us, length us, event | category | flops | bytes accessed | tf_op | source)
XLA Modules:
  0.0 41.5 jit_solution(8101274803929139030)
XLA Ops:
  0.0 18.6 %route.1 = (f32[8,256,256]{2,1,0:T(8,128)S(1)}, f32[32,8,256]{2,1,0:T(8,128)S(1)}, f32[32,256]{1,0:T(8,128)S(1)}, bf16[544,512]{1,0:T(8,128)(2,1)S(1)}, bf16[256...) custom-call(f32[256,8,256]{2,1,0:T(8,128)} %bitcast.4, ...), custom_call_target="tpu_custom_call" | custom-call | tf_op jit(solution)/shard_map/route/pallas_call | solution.py:680
  18.6 4.8 %deposit.1.total = f32[8,9,32,256]{3,2,1,0:T(8,128)S(1)} custom-call(f32[32,8,256]{2,1,0:T(8,128)S(1)} %get-tuple-element.16.got_mass, f32[32,256]{1,0:T(8,128)S(1)} %get-tuple-element.17.got_code, bf16[544,512]{1,0:T(8,128)(2,1)S(1)} %get-tuple-element.18.order), custom_call_target="tpu_custom_call" | custom-call | tf_op jit(solution)/shard_map/deposit/pallas_call | solution.py:701
  23.4 16.7 %solve.1 = (f32[8,256,256]{2,1,0:T(8,128)S(1)}, f32[2,8,256]{2,1,0:T(8,128)S(1)}, f32[2,8,256]{2,1,0:T(8,128)S(1)}) custom-call(f32[8,9,32,256]{3,2,1,0:T(8,128)S(1)} %deposit.1.total, f32[8,256,256]{2,1,0:T(8,128)S(1)} %get-tuple-element.19.first, f32[32,8,256]{2,1,0:T(8,128)} %diffusivity.3, f32[32,8,256]{2,1,0:T(8,128)} %wind.3, ...), custom_call_target="tpu_custom_call" | custom-call | tf_op jit(solution)/shard_map/solve/pallas_call | solution.py:714
  40.1 1.4 %finish.1 = f32[256,8,256]{2,1,0:T(8,128)} custom-call(f32[8,256,256]{2,1,0:T(8,128)S(1)} %get-tuple-element.24.second, f32[2,8,256]{2,1,0:T(8,128)S(1)} %get-tuple-element.25.down, f32[2,8,256]{2,1,0:T(8,128)S(1)} %get-tuple-element.26.upward, f32[256,128]{1,0:T(8,128)S(1)} %get-tuple-element.21.p_col, f32[256,128]{1,0:T(8,128)S(1)} %get-tuple-element.22.e_col), custom_call_target="tpu_custom_call" | custom-call | tf_op jit(solution)/shard_map/finish/pallas_call | solution.py:730

commit v6 on v5

--- a/solution.py
+++ b/solution.py
@@ -147,6 +147,14 @@
     d1 = u1 * m1_last
     p_ref[...] = jnp.broadcast_to(jnp.concatenate([c0, c1], axis=1), (BINS, LEV, 128)).reshape(ROWS, 128)
     e_ref[...] = jnp.broadcast_to(jnp.concatenate([d0, d1], axis=1), (BINS, LEV, 128)).reshape(ROWS, 128)
+    blocks = full.reshape(BINS, LEV, ROWS)
+    eye = lax.broadcasted_iota(I32, (ROWS, ROWS), 0) == lax.broadcasted_iota(I32, (ROWS, ROWS), 1)
+    across = [jnp.sum(jnp.where(eye, lanes([ref[...], ref[...]]), 0.0), axis=0, keepdims=True) for ref in (p_ref, e_ref)]
+    rows = jnp.concatenate([blocks[:, at, :] * col for at in (LEV - 1, 0) for col in across], axis=0)
+    fold = (
+        lax.broadcasted_iota(I32, (ROWS, LEV), 0) % LEV == lax.broadcasted_iota(I32, (ROWS, LEV), 1)
+    ).astype(F32)
+    return jnp.dot(rows, fold, precision=lax.Precision.HIGHEST, preferred_element_type=F32)
 
 
 def carry_factors(level, all_ref, out_ref):
@@ -182,9 +190,9 @@
 
 def route_kernel(
     euler, mass, dest, cell, diffusivity, wind, inv, low, up,
-    first, got_mass, got_code, order, triple, p_col, e_col, factors,
+    first, got_mass, got_code, order, triple, p_col, e_col, factors, kept, turned,
     ext, diff_s, wind_s, mass_s, dest_in, cell_in, inv_s, low_s, up_s,
-    send_mass, send_code, spot_s, links,
+    send_mass, send_code, spare, spot_s, links,
     load_sem, small_sem, halo_send, halo_recv, mass_send, mass_recv, code_send, code_recv, link_send, link_recv,
 ):
     me, level = lax.axis_index("xy"), lax.axis_index("lev")
@@ -242,15 +250,13 @@
     values = two_parts(mass_s[...])
     flat_target = flat(target)
 
-    def copies(other, slot_id):
+    def mass_copy(other):
         device = {"xy": other, "lev": level}
-        return (
-            remote(send_mass.at[other], got_mass.at[slot_id], mass_send.at[other], mass_recv.at[slot_id], device),
-            remote(
-                send_code.at[pl.ds(other, 1)], got_code.at[pl.ds(slot_id, 1)],
-                code_send.at[other], code_recv.at[slot_id], device,
-            ),
-        )
+        return remote(send_mass.at[other], got_mass.at[me], mass_send, mass_recv, device)
+
+    def code_copy(other):
+        source, target = send_code.at[pl.ds(other, 1)], got_code.at[pl.ds(me, 1)]
+        return remote(source, target, code_send, code_recv, {"xy": other, "lev": level})
 
     half = N_XY // 2
     for begin in (0, half):
@@ -264,18 +270,19 @@
 
             @pl.when(other != me)
             def _():
-                for copy in copies(other, me):
-                    copy.start()
+                mass_copy(other).start()
+                code_copy(other).start()
 
             return unused
 
         lax.fori_loop(0, half, send, 0)
     got_mass[me] = send_mass[me]
-    got_code[pl.ds(me, 1), :] = send_code[pl.ds(me, 1), :]
+    pltpu.make_async_copy(send_code.at[pl.ds(me, 1)], got_code.at[pl.ds(me, 1)], code_recv).start()
+    pltpu.make_async_copy(send_code.at[pl.ds(me, 1)], spare, code_send).start()
 
     for copy in small[3:]:
         copy.wait()
-    compose(inv_s, low_s, up_s, triple, p_col, e_col)
+    edge_matrix = compose(inv_s, low_s, up_s, triple, p_col, e_col)
     r, c = (lax.broadcasted_iota(I32, (N_XY * (BUCKETS + 1), N_XY * BUCKETS), d) for d in (0, 1))
     order[...] = jnp.where((c < r) & (c % N_XY // SRC == r % N_XY // SRC), 1.0, 0.0).astype(BF16)
     links[level, 0] = p_col[pl.ds(LEV - 1, BINS, stride=LEV), :]
@@ -299,6 +306,21 @@
         return unused
 
     lax.fori_loop(1, GX - 1, step, 0)
+
+    kept[...] = jnp.broadcast_to(jnp.sum(edge_matrix, axis=1, keepdims=True), (4 * BINS, 128)).reshape(4, BINS, 128)
+    high = edge_matrix.astype(BF16)
+    low = (edge_matrix - high.astype(F32)).astype(BF16)
+    three_parts = lanes([high, high, low])
+
+    def turn(x, unused):
+        for i, ref in enumerate((diff_s, wind_s)):
+            top = ref[x].astype(BF16)
+            rest = (ref[x] - top.astype(F32)).astype(BF16)
+            result = jnp.dot(three_parts, jnp.concatenate([top, rest, top], axis=0), preferred_element_type=F32)
+            turned[i, x] = result.reshape(4, BINS, GY)
+        return unused
+
+    lax.fori_loop(0, GX, turn, 0, unroll=2)
     at_edges(me, [up_copy], [down_copy], "wait")
 
     @pl.when(me == 0)
@@ -315,14 +337,9 @@
         link_copy(k, lax.rem(level + N_LEV - k, N_LEV)).wait()
     carry_factors(level, links, factors)
 
-    def finish(k, unused):
-        for copy in copies(lax.rem(me + k, N_XY), me):
-            copy.wait_send()
-        for copy in copies(me, lax.rem(me + k, N_XY)):
-            copy.wait_recv()
-        return unused
-
-    lax.fori_loop(1, N_XY, finish, 0)
+    remote(send_code, got_code, code_send, code_recv, {"xy": above, "lev": level}).wait()
+    others = pl.ds(0, N_XY - 1)
+    remote(send_mass.at[others], got_mass.at[others], mass_send, mass_recv, {"xy": above, "lev": level}).wait()
 
 
 def deposit_kernel(
@@ -432,13 +449,13 @@
     return result.reshape(ROWS, GY)
 
 
-PARTS = (((0, 2), (2, 3), (5, 3)), ((0, 3), (3, 3), (6, 2)))
+PARTS = (((0, 2), (2, 3), (5, 3)), ((0, 4), (4, 4)))
 
 
 def solve_kernel(
-    total, first, diffusivity, wind, triple, p_col, e_col, factors,
+    total, first, diffusivity, wind, triple, p_col, e_col, factors, kept, turned,
     second, down_out, up_out,
-    ext, fixed, diff_s, wind_s, sum_s, beside, edge, seen, seen_halo, edge2, seen2, edge3, seen_halo2,
+    ext, fixed, diff_s, wind_s, sum_s, beside, edge, seen, seen_halo, edge_w, edge2, seen2, edge3, seen_halo2, carry,
     load_sem, lev_send, lev_recv, diag_send, diag_recv, halo_send, halo_recv, side_send, side_recv,
 ):
     me, level = lax.axis_index("xy"), lax.axis_index("lev")
@@ -471,15 +488,17 @@
         target[0, place] = last
         target[1, place] = start + both(10) * last
 
-    def carries(values, seen_at):
+    def carries(tail, seen_at):
         down = jnp.zeros((BINS, GY), F32)
         upward = jnp.zeros((BINS, GY), F32)
         for f in range(N_LEV):
             here = jnp.where(level == f, 0.0, seen_at(f))
             down += both(f) * here
             upward += both(N_LEV + f) * here
-        tail = values.reshape(BINS, LEV, GY)[:, LEV - 1, :]
         return down, upward + both(8) * tail + both(9) * down
+
+    def tail_of(values):
+        return values.reshape(BINS, LEV, GY)[:, LEV - 1, :]
 
     def peer_of(k):
         return lax.rem(level + k, N_LEV)
@@ -505,11 +524,11 @@
         source, target = ((edge, seen_halo), (edge3, seen_halo2))[turn]
         return [
             remote(
-                source.at[kind(k), 1 - side], target.at[side, level if own else back(k)],
+                source.at[kind(k) if k else 0, 1 - side], target.at[side, level if own else back(k)],
                 diag_send.at[turn, side, k], diag_recv.at[turn, side, k], {"xy": where, "lev": peer_of(k)},
             )
             for side, where in enumerate((above, below))
-            for k in range(1, N_LEV)
+            for k in range(turn, N_LEV)
         ]
 
     def start(copies):
@@ -540,8 +559,6 @@
     solve_plane(GX - 1, 1)
     wait(loads)
     sum_s[...] = diff_s[0] + wind_s[0]
-    fixed[0] = jnp.zeros((ROWS, GY), F32)
-    fixed[GX + 1] = jnp.zeros((ROWS, GY), F32)
     pl.semaphore_wait(barrier, N_LEV - 1 + N_LEV * sides)
     halos = [
         remote(ext.at[GX], ext.at[0], halo_send.at[0], halo_recv.at[0], {"xy": above, "lev": level}),
@@ -554,7 +571,7 @@
     sent, seen_in = diag_copies(0, True), diag_copies(0, False)
     sent2, seen_in2 = diag_copies(1, True), diag_copies(1, False)
     three = N_LEV - 1
-    at_edges(me, sent[:three], sent[three:], "start")
+    at_edges(me, sent[:N_LEV], sent[N_LEV:], "start")
     start(lev_copies(0, 0, True))
     at_edges(me, weights[:1], weights[1:], "start")
     at_edges(me, halos[:1], halos[1:], "start")
@@ -563,52 +580,93 @@
     some(solve_plane, 4, 3, 1)
     start(lev_copies(0, 2, True))
 
-    def correct_plane(x, place):
-        down, upward = carries(ext[x + 1], lambda f: seen[f, place])
-        fixed[x + 1] = correction(ext[x + 1], down, upward, p_col, e_col)
+    def early_plane(x, before, after):
+        edges(product(stencil(ext[x + 1], before, after, diff_s[x], wind_s[x])), edge_w, x)
+
+    nothing = jnp.zeros((ROWS, GY), F32)
+    early_plane(0, nothing, ext[2])
+    some(lambda x, place: early_plane(x, ext[x], ext[x + 2]), 1, 3, 0)
+    some(lambda x, place: early_plane(x, ext[x], ext[x + 2]), 4, 3, 0)
+    early_plane(GX - 1, ext[GX - 1], nothing)
 
     def scaled(plane, values):
         return (plane[None] * values.reshape(BINS, LEV, GY)).reshape(ROWS, GY)
 
-    def second_plane(x, place):
-        stepped = stencil(fixed[x + 1], fixed[x], fixed[x + 2], diff_s[x], wind_s[x])
-        solved = product(stepped)
-        second[x] = solved
-        edges(solved, edge2, place)
-
     def share_up():
-        edges(product(scaled(beside[1], fixed[GX])), edge3, 1)
+        edges(product(scaled(beside[1], ext[GX])), edge3, 1)
         start(sent2[:three])
 
     def share_down():
-        edges(product(scaled(beside[0], fixed[1])), edge3, 0)
+        edges(product(scaled(beside[0], ext[1])), edge3, 0)
         start(sent2[three:])
 
-    wait(lev_copies(0, 0, False) + lev_copies(0, 1, False))
-    correct_plane(0, 0)
-    correct_plane(GX - 1, 1)
     at_edges(me, weights[:1], weights[1:], "wait")
     pl.when(me < N_XY - 1)(share_up)
     pl.when(me > 0)(share_down)
-    some(correct_plane, 1, 3, 1)
-    some(second_plane, 0, 3, 0)
-    start(lev_copies(1, 0, True))
-    wait(lev_copies(0, 2, False))
-    some(correct_plane, 4, 3, 1)
-    some(second_plane, 3, 3, 0)
-    start(lev_copies(1, 1, True))
-    some(second_plane, 6, 2, 0)
-    start(lev_copies(1, 2, True))
-
-    at_edges(me, seen_in[:three] + halos[:1], seen_in[three:] + halos[1:], "wait")
-
-    def add_halo(at, side, x, plane):
-        down, upward = carries(ext[at], lambda f: seen_halo[side, f])
-        halo = correction(ext[at], down, upward, p_col, e_col)
-        second[x] += product(scaled(plane, halo))
-
-    pl.when(me > 0)(lambda: add_halo(0, 0, 0, sum_s[...]))
-    pl.when(me < N_XY - 1)(lambda: add_halo(GX + 1, 1, GX - 1, diff_s[GX - 1]))
+
+    for part in range(3):
+        wait(lev_copies(0, part, False))
+    at_edges(me, seen_in[:N_LEV], seen_in[N_LEV:], "wait")
+
+    def keep_carries(at, found):
+        carry[0, at] = found[0]
+        carry[1, at] = found[1]
+
+    def halo_carries(side):
+        keep_carries(side * (GX + 1), carries(seen_halo[side, level], lambda f: seen_halo[side, f]))
+
+    def no_carries(side):
+        keep_carries(side * (GX + 1), (jnp.zeros((BINS, GY), F32),) * 2)
+
+    pl.when(me > 0)(lambda: halo_carries(0))
+    pl.when(me < N_XY - 1)(lambda: halo_carries(1))
+    pl.when(me == 0)(lambda: no_carries(0))
+    pl.when(me == N_XY - 1)(lambda: no_carries(1))
+    for x in range(GX):
+        place = {0: 0, GX - 1: 1}.get(x, x + 1)
+        keep_carries(x + 1, carries(edge[0, place], lambda f: seen[f, place]))
+    lane = lax.broadcasted_iota(I32, (BINS, GY), 1)
+
+    def late_edges(x):
+        added = [jnp.zeros((BINS, GY), F32)] * 2
+        for v in range(2):
+            here, before = carry[v, x + 1], carry[v, x]
+            left = jnp.where(lane == 0, 0.0, pltpu.roll(here, 1, 1))
+            right = jnp.where(lane == GY - 1, 0.0, pltpu.roll(here, GY - 1, 1))
+            laplace = carry[v, x + 2] + before + right + left - 4.0 * here
+            drift = here - before
+            for end in range(2):
+                i = 2 * end + v
+                keep = lanes([kept[i], kept[i]])
+                added[end] += keep * here + turned[0, x, i] * laplace - turned[1, x, i] * drift
+        edge2[0, x] = edge_w[0, x] + added[0]
+        edge2[1, x] = edge_w[1, x] + added[1] + both(10) * added[0]
+
+    for part in range(2):
+        for x in range(4 * part, 4 * part + 4):
+            late_edges(x)
+        start(lev_copies(1, part, True))
+
+    def correct_plane(at, unused):
+        fixed[at] = correction(ext[at], carry[0, at], carry[1, at], p_col, e_col)
+
+    def second_plane(x, unused):
+        second[x] = product(stencil(fixed[x + 1], fixed[x], fixed[x + 2], diff_s[x], wind_s[x]))
+
+    def no_plane(at):
+        fixed[at] = nothing
+
+    some(correct_plane, 1, 4, 0)
+    some(correct_plane, 5, 4, 0)
+    some(second_plane, 1, 3, 0)
+    some(second_plane, 4, 3, 0)
+    at_edges(me, halos[:1], halos[1:], "wait")
+    pl.when(me > 0)(lambda: correct_plane(0, 0))
+    pl.when(me < N_XY - 1)(lambda: correct_plane(GX + 1, 0))
+    pl.when(me == 0)(lambda: no_plane(0))
+    pl.when(me == N_XY - 1)(lambda: no_plane(GX + 1))
+    second_plane(0, 0)
+    second_plane(GX - 1, 0)
     at_edges(me, seen_in2[:three], seen_in2[three:], "wait")
 
     def no_share(side):
@@ -624,25 +682,24 @@
             return lambda f: seen2[f, GX - 1] + seen_halo2[1, f]
         return lambda f: seen2[f, x]
 
-    for part in range(2):
-        wait(lev_copies(1, part, False))
-        for x in range(3 * part, 3 * part + 3):
-            down, upward = carries(second[x], seen_at(x))
-            second[x] = correction(second[x], down, upward, p_col, e_col)
-    wait(lev_copies(1, 2, False))
-    for x in range(6, GX):
-        down, upward = carries(second[x], seen_at(x))
-        down_out[x - 6] = down
-        up_out[x - 6] = upward
+    wait(lev_copies(1, 0, False))
+    for x in range(4):
+        down, upward = carries(tail_of(second[x]), seen_at(x))
+        second[x] = correction(second[x], down, upward, p_col, e_col)
+    wait(lev_copies(1, 1, False))
+    for x in range(4, GX):
+        down, upward = carries(tail_of(second[x]), seen_at(x))
+        down_out[x - 4] = down
+        up_out[x - 4] = upward
 
 
 def finish_kernel(second, down, upward, p_col, e_col, out, outer, sem):
-    inner = [pltpu.make_async_copy(second.at[x], out.at[:, x, :], sem.at[x]) for x in range(6)]
+    inner = [pltpu.make_async_copy(second.at[x], out.at[:, x, :], sem.at[x]) for x in range(4)]
     for copy in inner:
         copy.start()
     last = []
-    for i in range(2):
-        x = 6 + i
+    for i in range(4):
+        x = 4 + i
         outer[i] = correction(second[x], down[i], upward[i], p_col, e_col)
         last.append(pltpu.make_async_copy(outer.at[i], out.at[:, x, :], sem.at[x]))
         last[i].start()
@@ -684,20 +741,21 @@
             shaped(GX, ROWS, GY), shaped(N_XY, BINS, CAP), shaped(N_XY, CAP),
             shaped(N_XY * (BUCKETS + 1), N_XY * BUCKETS, dtype=BF16), shaped(ROWS, 3 * ROWS, dtype=BF16),
             shaped(ROWS, 128), shaped(ROWS, 128), shaped(11, BINS, 128),
+            shaped(4, BINS, 128), shaped(2, GX, 4, BINS, GY),
         ],
         in_specs=somewhere(9),
-        out_specs=whole(8),
+        out_specs=whole(10),
         scratch_shapes=[
             vmem(GX + 2, ROWS, GY), vmem(GX, LEV, GY), vmem(GX, LEV, GY),
             vmem(BINS, PARC), vmem(32, 128, dtype=I32), vmem(32, 128, dtype=I32),
             vmem(2, BINS, 16, 16), vmem(2, BINS), vmem(2, BINS),
-            vmem(N_XY, BINS, CAP), vmem(N_XY, CAP), vmem(CAP, PARC, dtype=BF16), vmem(N_LEV, 3, BINS, 128),
-            dma((3, GX)), dma((6,)), dma((2,)), dma((2,)), dma((N_XY,)), dma((N_XY,)), dma((N_XY,)), dma((N_XY,)),
+            vmem(N_XY, BINS, CAP), vmem(N_XY, CAP), vmem(1, CAP), vmem(CAP, PARC, dtype=BF16), vmem(N_LEV, 3, BINS, 128),
+            dma((3, GX)), dma((6,)), dma((2,)), dma((2,)), dma, dma, dma, dma,
             dma((N_LEV,)), dma((N_LEV,)),
         ],
         compiler_params=pltpu.CompilerParams(collective_id=0, has_side_effects=True, vmem_limit_bytes=LIMIT),
     )(euler, mass, dest, cell, diffusivity, wind, inv, low, up)
-    first, got_mass, got_code, order, triple, p_col, e_col, factors = routed
+    first, got_mass, got_code, order, triple, p_col, e_col, factors, kept, turned = routed
     total = pl.pallas_call(
         deposit_kernel,
         name="deposit",
@@ -714,26 +772,27 @@
     second, down, upward = pl.pallas_call(
         solve_kernel,
         name="solve",
-        out_shape=[shaped(GX, ROWS, GY), shaped(2, BINS, GY), shaped(2, BINS, GY)],
-        in_specs=whole(2) + somewhere(2) + whole(4),
+        out_shape=[shaped(GX, ROWS, GY), shaped(4, BINS, GY), shaped(4, BINS, GY)],
+        in_specs=whole(2) + somewhere(2) + whole(6),
         out_specs=whole(3),
         scratch_shapes=[
             vmem(GX + 2, ROWS, GY), vmem(GX + 2, ROWS, GY),
             vmem(GX, LEV, GY), vmem(GX, LEV, GY), vmem(LEV, GY), vmem(2, LEV, GY),
             vmem(2, GX, BINS, GY), vmem(N_LEV, GX, BINS, GY), vmem(2, N_LEV, BINS, GY),
-            vmem(2, GX, BINS, GY), vmem(N_LEV, GX, BINS, GY), vmem(2, 2, BINS, GY), vmem(2, N_LEV, BINS, GY),
+            vmem(2, GX, BINS, GY), vmem(2, GX, BINS, GY), vmem(N_LEV, GX, BINS, GY),
+            vmem(2, 2, BINS, GY), vmem(2, N_LEV, BINS, GY), vmem(2, GX + 2, BINS, GY),
             dma((2, GX)), dma((2, 3, N_LEV)), dma((2, 3, N_LEV)), dma((2, 2, N_LEV)), dma((2, 2, N_LEV)),
             dma((2,)), dma((2,)), dma((2,)), dma((2,)),
         ],
         compiler_params=pltpu.CompilerParams(collective_id=1, has_side_effects=True, vmem_limit_bytes=LIMIT),
-    )(total, first, diffusivity, wind, triple, p_col, e_col, factors)
+    )(total, first, diffusivity, wind, triple, p_col, e_col, factors, kept, turned)
     result = pl.pallas_call(
         finish_kernel,
         name="finish",
         out_shape=shaped(ROWS, GX, GY),
         in_specs=whole(5),
         out_specs=pl.BlockSpec(memory_space=pltpu.HBM),
-        scratch_shapes=[vmem(2, ROWS, GY), dma((GX,))],
+        scratch_shapes=[vmem(4, ROWS, GY), dma((GX,))],
         compiler_params=pltpu.CompilerParams(vmem_limit_bytes=LIMIT),
     )(second, down, upward, p_col, e_col)
     return result.reshape(BINS, LEV, GX, GY)

time: 41.6 us -> 39.6 us (0.952)
  the two profiles are of different devices: /device:TPU:1 before, /device:TPU:0 now
where the time goes in v6:
time: 39.6 us; the launch traced here: 39 us
  Pallas kernels  38.8 us (98%)
    pallas_call x1, Pallas kernels, shards(): pl.pallas_call(route_kernel, name='route', out_shape=[shaped(GX, ROWS, GY...  17 us
    pallas_call x1, Pallas kernels, shards(): pl.pallas_call(solve_kernel, name='solve', out_shape=[shaped(GX, ROWS, GY...  15.6 us
    pallas_call x1, Pallas kernels, shards(): pl.pallas_call(deposit_kernel, name='deposit', out_shape=shaped(GX, BINS...  4.84 us
    pallas_call x1, Pallas kernels, shards(): pl.pallas_call(finish_kernel, name='finish', out_shape=shaped(ROWS, GX, G...  1.38 us

profile of v6, /device:TPU:0, one launch (start us, length us, event | category | flops | bytes accessed | tf_op | source)
XLA Modules:
  0.0 39.0 jit_solution(7692308521969900933)
XLA Ops:
  0.0 17.0 %route.1 = (f32[8,256,256]{2,1,0:T(8,128)S(1)}, f32[32,8,256]{2,1,0:T(8,128)S(1)}, f32[32,256]{1,0:T(8,128)S(1)}, bf16[544,512]{1,0:T(8,128)(2,1)S(1)}, bf16[256...) custom-call(f32[256,8,256]{2,1,0:T(8,128)} %bitcast.4, ...), custom_call_target="tpu_custom_call" | custom-call | tf_op jit(solution)/shard_map/route/pallas_call | solution.py:737
  17.0 4.8 %deposit.1.total = f32[8,9,32,256]{3,2,1,0:T(8,128)S(1)} custom-call(f32[32,8,256]{2,1,0:T(8,128)S(1)} %get-tuple-element.18.got_mass, f32[32,256]{1,0:T(8,128)S(1)} %get-tuple-element.19.got_code, bf16[544,512]{1,0:T(8,128)(2,1)S(1)} %get-tuple-element.20.order), custom_call_target="tpu_custom_call" | custom-call | tf_op jit(solution)/shard_map/deposit/pallas_call | solution.py:759
  21.8 15.6 %solve.1 = (f32[8,256,256]{2,1,0:T(8,128)S(1)}, f32[4,8,256]{2,1,0:T(8,128)S(1)}, f32[4,8,256]{2,1,0:T(8,128)S(1)}) custom-call(f32[8,9,32,256]{3,2,1,0:T(8,128)S(1)} %deposit.1.total, f32[8,256,256]{2,1,0:T(8,128)S(1)} %get-tuple-element.21.first, f32[32,8,256]{2,1,0:T(8,128)} %diffusivity.3, f32[32,8,256]{2,1,0:T(8,128)} %wind.3, ...), custom_call_target="tpu_custom_call" | custom-call | tf_op jit(solution)/shard_map/solve/pallas_call | solution.py:772
  37.4 1.4 %finish.1 = f32[256,8,256]{2,1,0:T(8,128)} custom-call(f32[8,256,256]{2,1,0:T(8,128)S(1)} %get-tuple-element.28.second, f32[4,8,256]{2,1,0:T(8,128)S(1)} %get-tuple-element.29.down, f32[4,8,256]{2,1,0:T(8,128)S(1)} %get-tuple-element.30.upward, f32[256,128]{1,0:T(8,128)S(1)} %get-tuple-element.23.p_col, f32[256,128]{1,0:T(8,128)S(1)} %get-tuple-element.24.e_col), custom_call_target="tpu_custom_call" | custom-call | tf_op jit(solution)/shard_map/finish/pallas_call | solution.py:789

commit v7 on v6

--- a/solution.py
+++ b/solution.py
@@ -449,7 +449,8 @@
     return result.reshape(ROWS, GY)
 
 
-PARTS = (((0, 2), (2, 3), (5, 3)), ((0, 4), (4, 4)))
+PARTS = (((0, 3), (3, 2), (5, 3)), ((0, 2), (2, 3), (5, 3)))
+PLACE = (0, 2, 3, 4, 5, 6, 7, 1)
 
 
 def solve_kernel(
@@ -524,7 +525,7 @@
         source, target = ((edge, seen_halo), (edge3, seen_halo2))[turn]
         return [
             remote(
-                source.at[kind(k) if k else 0, 1 - side], target.at[side, level if own else back(k)],
+                source.at[kind(k) if k else 0, ((GX - 1, 0), (1, 0))[turn][side]], target.at[side, level if own else back(k)],
                 diag_send.at[turn, side, k], diag_recv.at[turn, side, k], {"xy": where, "lev": peer_of(k)},
             )
             for side, where in enumerate((above, below))
@@ -555,8 +556,9 @@
 
         lax.fori_loop(begin, begin + count, one, 0, unroll=count)
 
-    solve_plane(0, 0)
-    solve_plane(GX - 1, 1)
+    some(solve_plane, 0, 3, 0)
+    some(solve_plane, 3, 2, 0)
+    some(solve_plane, 5, 3, 0)
     wait(loads)
     sum_s[...] = diff_s[0] + wind_s[0]
     pl.semaphore_wait(barrier, N_LEV - 1 + N_LEV * sides)
@@ -571,14 +573,11 @@
     sent, seen_in = diag_copies(0, True), diag_copies(0, False)
     sent2, seen_in2 = diag_copies(1, True), diag_copies(1, False)
     three = N_LEV - 1
+    for part in range(3):
+        start(lev_copies(0, part, True))
     at_edges(me, sent[:N_LEV], sent[N_LEV:], "start")
-    start(lev_copies(0, 0, True))
     at_edges(me, weights[:1], weights[1:], "start")
     at_edges(me, halos[:1], halos[1:], "start")
-    some(solve_plane, 1, 3, 1)
-    start(lev_copies(0, 1, True))
-    some(solve_plane, 4, 3, 1)
-    start(lev_copies(0, 2, True))
 
     def early_plane(x, before, after):
         edges(product(stencil(ext[x + 1], before, after, diff_s[x], wind_s[x])), edge_w, x)
@@ -604,10 +603,6 @@
     pl.when(me < N_XY - 1)(share_up)
     pl.when(me > 0)(share_down)
 
-    for part in range(3):
-        wait(lev_copies(0, part, False))
-    at_edges(me, seen_in[:N_LEV], seen_in[N_LEV:], "wait")
-
     def keep_carries(at, found):
         carry[0, at] = found[0]
         carry[1, at] = found[1]
@@ -618,13 +613,10 @@
     def no_carries(side):
         keep_carries(side * (GX + 1), (jnp.zeros((BINS, GY), F32),) * 2)
 
-    pl.when(me > 0)(lambda: halo_carries(0))
-    pl.when(me < N_XY - 1)(lambda: halo_carries(1))
-    pl.when(me == 0)(lambda: no_carries(0))
-    pl.when(me == N_XY - 1)(lambda: no_carries(1))
-    for x in range(GX):
-        place = {0: 0, GX - 1: 1}.get(x, x + 1)
-        keep_carries(x + 1, carries(edge[0, place], lambda f: seen[f, place]))
+    def plane_carries(begin, end):
+        for x in range(begin, end):
+            keep_carries(x + 1, carries(edge[0, x], lambda f: seen[f, x]))
+
     lane = lax.broadcasted_iota(I32, (BINS, GY), 1)
 
     def late_edges(x):
@@ -639,13 +631,27 @@
                 i = 2 * end + v
                 keep = lanes([kept[i], kept[i]])
                 added[end] += keep * here + turned[0, x, i] * laplace - turned[1, x, i] * drift
-        edge2[0, x] = edge_w[0, x] + added[0]
-        edge2[1, x] = edge_w[1, x] + added[1] + both(10) * added[0]
-
-    for part in range(2):
-        for x in range(4 * part, 4 * part + 4):
-            late_edges(x)
-        start(lev_copies(1, part, True))
+        edge2[0, PLACE[x]] = edge_w[0, x] + added[0]
+        edge2[1, PLACE[x]] = edge_w[1, x] + added[1] + both(10) * added[0]
+
+    wait(lev_copies(0, 0, False) + lev_copies(0, 1, False))
+    plane_carries(0, 5)
+    for x in range(1, 4):
+        late_edges(x)
+    start(lev_copies(1, 1, True))
+    wait(lev_copies(0, 2, False))
+    plane_carries(5, GX)
+    for x in range(4, GX - 1):
+        late_edges(x)
+    start(lev_copies(1, 2, True))
+    at_edges(me, seen_in[:N_LEV], seen_in[N_LEV:], "wait")
+    pl.when(me > 0)(lambda: halo_carries(0))
+    pl.when(me < N_XY - 1)(lambda: halo_carries(1))
+    pl.when(me == 0)(lambda: no_carries(0))
+    pl.when(me == N_XY - 1)(lambda: no_carries(1))
+    late_edges(0)
+    late_edges(GX - 1)
+    start(lev_copies(1, 0, True))
 
     def correct_plane(at, unused):
         fixed[at] = correction(ext[at], carry[0, at], carry[1, at], p_col, e_col)
@@ -679,27 +685,29 @@
         if x == 0:
             return lambda f: seen2[f, 0] + seen_halo2[0, f]
         if x == GX - 1:
-            return lambda f: seen2[f, GX - 1] + seen_halo2[1, f]
-        return lambda f: seen2[f, x]
-
-    wait(lev_copies(1, 0, False))
-    for x in range(4):
+            return lambda f: seen2[f, 1] + seen_halo2[1, f]
+        return lambda f: seen2[f, PLACE[x]]
+
+    wait(lev_copies(1, 1, False))
+    for x in range(1, 4):
         down, upward = carries(tail_of(second[x]), seen_at(x))
         second[x] = correction(second[x], down, upward, p_col, e_col)
-    wait(lev_copies(1, 1, False))
-    for x in range(4, GX):
+    wait(lev_copies(1, 2, False) + lev_copies(1, 0, False))
+    for i, x in enumerate(LATE):
         down, upward = carries(tail_of(second[x]), seen_at(x))
-        down_out[x - 4] = down
-        up_out[x - 4] = upward
+        down_out[i] = down
+        up_out[i] = upward
+
+
+LATE = (4, 5, 6, 0, 7)
 
 
 def finish_kernel(second, down, upward, p_col, e_col, out, outer, sem):
-    inner = [pltpu.make_async_copy(second.at[x], out.at[:, x, :], sem.at[x]) for x in range(4)]
+    inner = [pltpu.make_async_copy(second.at[x], out.at[:, x, :], sem.at[x]) for x in range(1, 4)]
     for copy in inner:
         copy.start()
     last = []
-    for i in range(4):
-        x = 4 + i
+    for i, x in enumerate(LATE):
         outer[i] = correction(second[x], down[i], upward[i], p_col, e_col)
         last.append(pltpu.make_async_copy(outer.at[i], out.at[:, x, :], sem.at[x]))
         last[i].start()
@@ -772,7 +780,7 @@
     second, down, upward = pl.pallas_call(
         solve_kernel,
         name="solve",
-        out_shape=[shaped(GX, ROWS, GY), shaped(4, BINS, GY), shaped(4, BINS, GY)],
+        out_shape=[shaped(GX, ROWS, GY), shaped(len(LATE), BINS, GY), shaped(len(LATE), BINS, GY)],
         in_specs=whole(2) + somewhere(2) + whole(6),
         out_specs=whole(3),
         scratch_shapes=[
@@ -792,7 +800,7 @@
         out_shape=shaped(ROWS, GX, GY),
         in_specs=whole(5),
         out_specs=pl.BlockSpec(memory_space=pltpu.HBM),
-        scratch_shapes=[vmem(4, ROWS, GY), dma((GX,))],
+        scratch_shapes=[vmem(len(LATE), ROWS, GY), dma((GX,))],
         compiler_params=pltpu.CompilerParams(vmem_limit_bytes=LIMIT),
     )(second, down, upward, p_col, e_col)
     return result.reshape(BINS, LEV, GX, GY)

time: 39.6 us -> 38.7 us (0.977)
  the two profiles are of different devices: /device:TPU:0 before, /device:TPU:1 now
where the time goes in v7:
time: 38.7 us; the launch traced here: 38.6 us
  Pallas kernels  38.4 us (99%)
    pallas_call x1, Pallas kernels, shards(): pl.pallas_call(route_kernel, name='route', out_shape=[shaped(GX, ROWS, GY...  17.1 us
    pallas_call x1, Pallas kernels, shards(): pl.pallas_call(solve_kernel, name='solve', out_shape=[shaped(GX, ROWS, GY...  15 us
    pallas_call x1, Pallas kernels, shards(): pl.pallas_call(deposit_kernel, name='deposit', out_shape=shaped(GX, BINS...  4.84 us
    pallas_call x1, Pallas kernels, shards(): pl.pallas_call(finish_kernel, name='finish', out_shape=shaped(ROWS, GX, G...  1.38 us

profile of v7, /device:TPU:1, one launch (start us, length us, event | category | flops | bytes accessed | tf_op | source)
XLA Modules:
  0.0 38.6 jit_solution(9351034094703512029)
XLA Ops:
  0.0 17.1 %route.1 = (f32[8,256,256]{2,1,0:T(8,128)S(1)}, f32[32,8,256]{2,1,0:T(8,128)S(1)}, f32[32,256]{1,0:T(8,128)S(1)}, bf16[544,512]{1,0:T(8,128)(2,1)S(1)}, bf16[256...) custom-call(f32[256,8,256]{2,1,0:T(8,128)} %bitcast.4, ...), custom_call_target="tpu_custom_call" | custom-call | tf_op jit(solution)/shard_map/route/pallas_call | solution.py:745
  17.2 4.8 %deposit.1.total = f32[8,9,32,256]{3,2,1,0:T(8,128)S(1)} custom-call(f32[32,8,256]{2,1,0:T(8,128)S(1)} %get-tuple-element.18.got_mass, f32[32,256]{1,0:T(8,128)S(1)} %get-tuple-element.19.got_code, bf16[544,512]{1,0:T(8,128)(2,1)S(1)} %get-tuple-element.20.order), custom_call_target="tpu_custom_call" | custom-call | tf_op jit(solution)/shard_map/deposit/pallas_call | solution.py:767
  22.0 15.0 %solve.1 = (f32[8,256,256]{2,1,0:T(8,128)S(1)}, f32[5,8,256]{2,1,0:T(8,128)S(1)}, f32[5,8,256]{2,1,0:T(8,128)S(1)}) custom-call(f32[8,9,32,256]{3,2,1,0:T(8,128)S(1)} %deposit.1.total, f32[8,256,256]{2,1,0:T(8,128)S(1)} %get-tuple-element.21.first, f32[32,8,256]{2,1,0:T(8,128)} %diffusivity.3, f32[32,8,256]{2,1,0:T(8,128)} %wind.3, ...), custom_call_target="tpu_custom_call" | custom-call | tf_op jit(solution)/shard_map/solve/pallas_call | solution.py:780
  37.0 1.4 %finish.1 = f32[256,8,256]{2,1,0:T(8,128)} custom-call(f32[8,256,256]{2,1,0:T(8,128)S(1)} %get-tuple-element.28.second, f32[5,8,256]{2,1,0:T(8,128)S(1)} %get-tuple-element.29.down, f32[5,8,256]{2,1,0:T(8,128)S(1)} %get-tuple-element.30.upward, f32[256,128]{1,0:T(8,128)S(1)} %get-tuple-element.23.p_col, f32[256,128]{1,0:T(8,128)S(1)} %get-tuple-element.24.e_col), custom_call_target="tpu_custom_call" | custom-call | tf_op jit(solution)/shard_map/finish/pallas_call | solution.py:797

commit v8 on v7

--- a/solution.py
+++ b/solution.py
@@ -190,8 +190,8 @@
 
 def route_kernel(
     euler, mass, dest, cell, diffusivity, wind, inv, low, up,
-    first, got_mass, got_code, order, triple, p_col, e_col, factors, kept, turned,
-    ext, diff_s, wind_s, mass_s, dest_in, cell_in, inv_s, low_s, up_s,
+    first, rows_u, hl_u, col_u, starts_v, triple, p_col, e_col, factors, kept, turned,
+    got_mass, got_code, order, hp_s, lp_s, hl_s, col_s, ext, diff_s, wind_s, mass_s, dest_in, cell_in, inv_s, low_s, up_s,
     send_mass, send_code, spare, spot_s, links,
     load_sem, small_sem, halo_send, halo_recv, mass_send, mass_recv, code_send, code_recv, link_send, link_recv,
 ):
@@ -224,9 +224,6 @@
     above, below = lax.rem(me + 1, N_XY), lax.rem(me + N_XY - 1, N_XY)
     up_copy = remote(euler.at[:, GX - 1, :], ext.at[0], halo_send.at[0], halo_recv.at[0], {"xy": above, "lev": level})
     down_copy = remote(euler.at[:, 0, :], ext.at[GX + 1], halo_send.at[1], halo_recv.at[1], {"xy": below, "lev": level})
-    pl.semaphore_wait(barrier, N_XY - 1 + N_LEV - 1)
-    at_edges(me, [up_copy], [down_copy], "start")
-
     def wide(ref):
         return lanes([ref[pl.ds(0, 16, stride=2), :], ref[pl.ds(1, 16, stride=2), :]])
 
@@ -258,24 +255,20 @@
         source, target = send_code.at[pl.ds(other, 1)], got_code.at[pl.ds(me, 1)]
         return remote(source, target, code_send, code_recv, {"xy": other, "lev": level})
 
-    half = N_XY // 2
-    for begin in (0, half):
-        table = sort_slots(values, high_low, column, flat_target, spot_s[...], begin, half)
-        masses = table[: 16 * half].reshape(half, 16, CAP)
-        send_mass[begin : begin + half] = masses[:, :8] + masses[:, 8:]
-        send_code[begin : begin + half] = table[16 * half : 17 * half] * 256.0 + table[17 * half :]
-
-        def send(k, unused):
-            other = begin + lax.rem(me + k, half)
-
-            @pl.when(other != me)
-            def _():
-                mass_copy(other).start()
-                code_copy(other).start()
-
-            return unused
-
-        lax.fori_loop(0, half, send, 0)
+    table = sort_slots(values, high_low, column, flat_target, spot_s[...], 0, N_XY)
+    masses = table[: 16 * N_XY].reshape(N_XY, 16, CAP)
+    send_mass[...] = masses[:, :8] + masses[:, 8:]
+    send_code[...] = table[16 * N_XY : 17 * N_XY] * 256.0 + table[17 * N_XY :]
+    pl.semaphore_wait(barrier, N_XY - 1 + N_LEV - 1)
+
+    def send(k, unused):
+        other = lax.rem(me + k, N_XY)
+        mass_copy(other).start()
+        code_copy(other).start()
+        return unused
+
+    lax.fori_loop(1, N_XY, send, 0)
+    at_edges(me, [up_copy], [down_copy], "start")
     got_mass[me] = send_mass[me]
     pltpu.make_async_copy(send_code.at[pl.ds(me, 1)], got_code.at[pl.ds(me, 1)], code_recv).start()
     pltpu.make_async_copy(send_code.at[pl.ds(me, 1)], spare, code_send).start()
@@ -321,31 +314,11 @@
         return unused
 
     lax.fori_loop(0, GX, turn, 0, unroll=2)
-    at_edges(me, [up_copy], [down_copy], "wait")
-
-    @pl.when(me == 0)
-    def _():
-        ext[0] = jnp.zeros((ROWS, GY), F32)
-
-    @pl.when(me == N_XY - 1)
-    def _():
-        ext[GX + 1] = jnp.zeros((ROWS, GY), F32)
-
-    lax.fori_loop(0, 2, lambda i, u: step(i * (GX - 1), u), 0)
-
     for k in range(1, N_LEV):
         link_copy(k, lax.rem(level + N_LEV - k, N_LEV)).wait()
     carry_factors(level, links, factors)
 
     remote(send_code, got_code, code_send, code_recv, {"xy": above, "lev": level}).wait()
-    others = pl.ds(0, N_XY - 1)
-    remote(send_mass.at[others], got_mass.at[others], mass_send, mass_recv, {"xy": above, "lev": level}).wait()
-
-
-def deposit_kernel(
-    got_mass, got_code, order, total,
-    rows_u, hl_u, col_u, hp_s, lp_s, hl_s, col_s, starts_v, starts_s, sem,
-):
     code = got_code[...].astype(I32)
     hl = code // 256
     col = code % 256
@@ -371,8 +344,9 @@
             longest = jnp.maximum(longest, start - before // 128 * 128)
         before = start
     starts_v[BUCKETS + 1 : BUCKETS + 2, :] = longest
-    to_scalars = pltpu.make_async_copy(starts_v, starts_s, sem)
-    to_scalars.start()
+
+    others = pl.ds(0, N_XY - 1)
+    remote(send_mass.at[others], got_mass.at[others], mass_send, mass_recv, {"xy": above, "lev": level}).wait()
 
     def one_set(g, unused):
         take = lambda ref: lanes([ref[pl.ds(g * SRC + i, 1), :] for i in range(SRC)])
@@ -390,6 +364,22 @@
         return unused
 
     lax.fori_loop(0, SETS, one_set, 0)
+    at_edges(me, [up_copy], [down_copy], "wait")
+
+    @pl.when(me == 0)
+    def _():
+        ext[0] = jnp.zeros((ROWS, GY), F32)
+
+    @pl.when(me == N_XY - 1)
+    def _():
+        ext[GX + 1] = jnp.zeros((ROWS, GY), F32)
+
+    lax.fori_loop(0, 2, lambda i, u: step(i * (GX - 1), u), 0)
+
+
+def deposit_kernel(starts_v, rows_u, hl_u, col_u, total, starts_s, sem):
+    to_scalars = pltpu.make_async_copy(starts_v, starts_s, sem)
+    to_scalars.start()
     to_scalars.wait()
 
     def place_of(k):
@@ -746,14 +736,16 @@
         route_kernel,
         name="route",
         out_shape=[
-            shaped(GX, ROWS, GY), shaped(N_XY, BINS, CAP), shaped(N_XY, CAP),
-            shaped(N_XY * (BUCKETS + 1), N_XY * BUCKETS, dtype=BF16), shaped(ROWS, 3 * ROWS, dtype=BF16),
+            shaped(GX, ROWS, GY), shaped(SETS, UNITS + WIN, 16, 128), shaped(SETS, UNITS + 8, 128),
+            shaped(SETS, UNITS + 8, 128), shaped(BUCKETS + 8, 128, dtype=I32), shaped(ROWS, 3 * ROWS, dtype=BF16),
             shaped(ROWS, 128), shaped(ROWS, 128), shaped(11, BINS, 128),
             shaped(4, BINS, 128), shaped(2, GX, 4, BINS, GY),
         ],
         in_specs=somewhere(9),
-        out_specs=whole(10),
+        out_specs=whole(11),
         scratch_shapes=[
+            vmem(N_XY, BINS, CAP), vmem(N_XY, CAP), vmem(N_XY * (BUCKETS + 1), N_XY * BUCKETS, dtype=BF16),
+            vmem(N_XY, BLK), vmem(N_XY, BLK), vmem(N_XY, BLK), vmem(N_XY, BLK),
             vmem(GX + 2, ROWS, GY), vmem(GX, LEV, GY), vmem(GX, LEV, GY),
             vmem(BINS, PARC), vmem(32, 128, dtype=I32), vmem(32, 128, dtype=I32),
             vmem(2, BINS, 16, 16), vmem(2, BINS), vmem(2, BINS),
@@ -763,20 +755,16 @@
         ],
         compiler_params=pltpu.CompilerParams(collective_id=0, has_side_effects=True, vmem_limit_bytes=LIMIT),
     )(euler, mass, dest, cell, diffusivity, wind, inv, low, up)
-    first, got_mass, got_code, order, triple, p_col, e_col, factors, kept, turned = routed
+    first, rows_u, hl_u, col_u, starts, triple, p_col, e_col, factors, kept, turned = routed
     total = pl.pallas_call(
         deposit_kernel,
         name="deposit",
         out_shape=shaped(GX, BINS + 1, LEV, GY),
-        in_specs=whole(3),
+        in_specs=whole(4),
         out_specs=pl.BlockSpec(memory_space=pltpu.VMEM),
-        scratch_shapes=[
-            vmem(SETS, UNITS + WIN, 16, 128), vmem(SETS, UNITS + 8, 128), vmem(SETS, UNITS + 8, 128),
-            vmem(N_XY, BLK), vmem(N_XY, BLK), vmem(N_XY, BLK), vmem(N_XY, BLK),
-            vmem(BUCKETS + 8, 128, dtype=I32), pltpu.SMEM((BUCKETS + 8, 128), I32), dma,
-        ],
+        scratch_shapes=[pltpu.SMEM((BUCKETS + 8, 128), I32), dma],
         compiler_params=pltpu.CompilerParams(vmem_limit_bytes=LIMIT),
-    )(got_mass, got_code, order)
+    )(starts, rows_u, hl_u, col_u)
     second, down, upward = pl.pallas_call(
         solve_kernel,
         name="solve",

time: 38.7 us -> 36.3 us (0.938)
  the two profiles are of different devices: /device:TPU:1 before, /device:TPU:0 now
where the time goes in v8:
time: 36.3 us; the launch traced here: 36.1 us
  Pallas kernels  35.9 us (99%)
    pallas_call x1, Pallas kernels, shards(): pl.pallas_call(route_kernel, name='route', out_shape=[shaped(GX, ROWS, GY...  16.4 us
    pallas_call x1, Pallas kernels, shards(): pl.pallas_call(solve_kernel, name='solve', out_shape=[shaped(GX, ROWS, GY...  14.9 us
    pallas_call x1, Pallas kernels, shards(): pl.pallas_call(deposit_kernel, name='deposit', out_shape=shaped(GX, BINS...  3.26 us
    pallas_call x1, Pallas kernels, shards(): pl.pallas_call(finish_kernel, name='finish', out_shape=shaped(ROWS, GX, G...  1.38 us

profile of v8, /device:TPU:0, one launch (start us, length us, event | category | flops | bytes accessed | tf_op | source)
XLA Modules:
  0.0 36.1 jit_solution(6820021973127759752)
XLA Ops:
  0.0 16.4 %route.1 = (f32[8,256,256]{2,1,0:T(8,128)S(1)}, f32[2,36,16,128]{3,2,1,0:T(8,128)S(1)}, f32[2,40,128]{2,1,0:T(8,128)S(1)}, f32[2,40,128]{2,1,0:T(8,128)S(1)}, s3...) custom-call(f32[256,8,256]{2,1,0:T(8,128)} %bitcast.4, ...), custom_call_target="tpu_custom_call" | custom-call | tf_op jit(solution)/shard_map/route/pallas_call | solution.py:735
  16.4 3.3 %deposit.1.total = f32[8,9,32,256]{3,2,1,0:T(8,128)S(1)} custom-call(s32[24,128]{1,0:T(8,128)S(1)} %get-tuple-element.19.starts_v, f32[2,36,16,128]{3,2,1,0:T(8,128)S(1)} %get-tuple-element.20.rows_u, f32[2,40,128]{2,1,0:T(8,128)S(1)} %get-tuple-element.21.hl_u, f32[2,40,128]{2,1,0:T(8,128)S(1)} %get-tuple-element.22.col_u), custom_call_target="tpu_custom_call" | custom-call | tf_op jit(solution)/shard_map/deposit/pallas_call | solution.py:759
  19.7 14.9 %solve.1 = (f32[8,256,256]{2,1,0:T(8,128)S(1)}, f32[5,8,256]{2,1,0:T(8,128)S(1)}, f32[5,8,256]{2,1,0:T(8,128)S(1)}) custom-call(f32[8,9,32,256]{3,2,1,0:T(8,128)S(1)} %deposit.1.total, f32[8,256,256]{2,1,0:T(8,128)S(1)} %get-tuple-element.23.first, f32[32,8,256]{2,1,0:T(8,128)} %diffusivity.3, f32[32,8,256]{2,1,0:T(8,128)} %wind.3, ...), custom_call_target="tpu_custom_call" | custom-call | tf_op jit(solution)/shard_map/solve/pallas_call | solution.py:768
  34.5 1.4 %finish.1 = f32[256,8,256]{2,1,0:T(8,128)} custom-call(f32[8,256,256]{2,1,0:T(8,128)S(1)} %get-tuple-element.30.second, f32[5,8,256]{2,1,0:T(8,128)S(1)} %get-tuple-element.31.down, f32[5,8,256]{2,1,0:T(8,128)S(1)} %get-tuple-element.32.upward, f32[256,128]{1,0:T(8,128)S(1)} %get-tuple-element.25.p_col, f32[256,128]{1,0:T(8,128)S(1)} %get-tuple-element.26.e_col), custom_call_target="tpu_custom_call" | custom-call | tf_op jit(solution)/shard_map/finish/pallas_call | solution.py:785

commit v9 on v8

--- a/solution.py
+++ b/solution.py
@@ -299,6 +299,9 @@
         return unused
 
     lax.fori_loop(1, GX - 1, step, 0)
+    nothing = jnp.zeros((ROWS, GY), F32)
+    first[0] = stencil(ext[1], nothing, ext[2], diff_s[0], wind_s[0])
+    first[GX - 1] = stencil(ext[GX], ext[GX - 1], nothing, diff_s[GX - 1], wind_s[GX - 1])
 
     kept[...] = jnp.broadcast_to(jnp.sum(edge_matrix, axis=1, keepdims=True), (4 * BINS, 128)).reshape(4, BINS, 128)
     high = edge_matrix.astype(BF16)
@@ -366,15 +369,11 @@
     lax.fori_loop(0, SETS, one_set, 0)
     at_edges(me, [up_copy], [down_copy], "wait")
 
-    @pl.when(me == 0)
-    def _():
-        ext[0] = jnp.zeros((ROWS, GY), F32)
-
-    @pl.when(me == N_XY - 1)
-    def _():
-        ext[GX + 1] = jnp.zeros((ROWS, GY), F32)
-
-    lax.fori_loop(0, 2, lambda i, u: step(i * (GX - 1), u), 0)
+    def add_halo(x, at, weight):
+        first[x] += (weight[None] * ext[at].reshape(BINS, LEV, GY)).reshape(ROWS, GY)
+
+    pl.when(me > 0)(lambda: add_halo(0, 0, diff_s[0] + wind_s[0]))
+    pl.when(me < N_XY - 1)(lambda: add_halo(GX - 1, GX + 1, diff_s[GX - 1]))
 
 
 def deposit_kernel(starts_v, rows_u, hl_u, col_u, total, starts_s, sem):

time: 36.3 us -> 35.7 us (0.983)
  Pallas kernels: 35.9 us -> 35.4 us
    pallas_call x1, Pallas kernels: 16.4 us -> 15.9 us  [shards(): pl.pallas_call(route_kernel, name='route', out_shape=[shaped(GX, ROWS, GY...]
where the time goes in v9:
time: 35.7 us; the launch traced here: 35.5 us
  Pallas kernels  35.4 us (99%)
    pallas_call x1, Pallas kernels, shards(): pl.pallas_call(route_kernel, name='route', out_shape=[shaped(GX, ROWS, GY...  15.9 us
    pallas_call x1, Pallas kernels, shards(): pl.pallas_call(solve_kernel, name='solve', out_shape=[shaped(GX, ROWS, GY...  14.9 us
    pallas_call x1, Pallas kernels, shards(): pl.pallas_call(deposit_kernel, name='deposit', out_shape=shaped(GX, BINS...  3.26 us
    pallas_call x1, Pallas kernels, shards(): pl.pallas_call(finish_kernel, name='finish', out_shape=shaped(ROWS, GX, G...  1.38 us

profile of v9, /device:TPU:0, one launch (start us, length us, event | category | flops | bytes accessed | tf_op | source)
XLA Modules:
  0.0 35.5 jit_solution(3165602830556287911)
XLA Ops:
  0.0 15.9 %route.1 = (f32[8,256,256]{2,1,0:T(8,128)S(1)}, f32[2,36,16,128]{3,2,1,0:T(8,128)S(1)}, f32[2,40,128]{2,1,0:T(8,128)S(1)}, f32[2,40,128]{2,1,0:T(8,128)S(1)}, s3...) custom-call(f32[256,8,256]{2,1,0:T(8,128)} %bitcast.4, ...), custom_call_target="tpu_custom_call" | custom-call | tf_op jit(solution)/shard_map/route/pallas_call | solution.py:734
  15.9 3.3 %deposit.1.total = f32[8,9,32,256]{3,2,1,0:T(8,128)S(1)} custom-call(s32[24,128]{1,0:T(8,128)S(1)} %get-tuple-element.19.starts_v, f32[2,36,16,128]{3,2,1,0:T(8,128)S(1)} %get-tuple-element.20.rows_u, f32[2,40,128]{2,1,0:T(8,128)S(1)} %get-tuple-element.21.hl_u, f32[2,40,128]{2,1,0:T(8,128)S(1)} %get-tuple-element.22.col_u), custom_call_target="tpu_custom_call" | custom-call | tf_op jit(solution)/shard_map/deposit/pallas_call | solution.py:758
  19.1 14.9 %solve.1 = (f32[8,256,256]{2,1,0:T(8,128)S(1)}, f32[5,8,256]{2,1,0:T(8,128)S(1)}, f32[5,8,256]{2,1,0:T(8,128)S(1)}) custom-call(f32[8,9,32,256]{3,2,1,0:T(8,128)S(1)} %deposit.1.total, f32[8,256,256]{2,1,0:T(8,128)S(1)} %get-tuple-element.23.first, f32[32,8,256]{2,1,0:T(8,128)} %diffusivity.3, f32[32,8,256]{2,1,0:T(8,128)} %wind.3, ...), custom_call_target="tpu_custom_call" | custom-call | tf_op jit(solution)/shard_map/solve/pallas_call | solution.py:767
  34.0 1.4 %finish.1 = f32[256,8,256]{2,1,0:T(8,128)} custom-call(f32[8,256,256]{2,1,0:T(8,128)S(1)} %get-tuple-element.30.second, f32[5,8,256]{2,1,0:T(8,128)S(1)} %get-tuple-element.31.down, f32[5,8,256]{2,1,0:T(8,128)S(1)} %get-tuple-element.32.upward, f32[256,128]{1,0:T(8,128)S(1)} %get-tuple-element.25.p_col, f32[256,128]{1,0:T(8,128)S(1)} %get-tuple-element.26.e_col), custom_call_target="tpu_custom_call" | custom-call | tf_op jit(solution)/shard_map/finish/pallas_call | solution.py:784

commit v10 on v9

--- a/solution.py
+++ b/solution.py
@@ -262,11 +262,14 @@
     pl.semaphore_wait(barrier, N_XY - 1 + N_LEV - 1)
 
     def send(k, unused):
-        other = lax.rem(me + k, N_XY)
-        mass_copy(other).start()
-        code_copy(other).start()
+        mass_copy(lax.rem(me + k, N_XY)).start()
         return unused
 
+    def send_codes(k, unused):
+        code_copy(lax.rem(me + k, N_XY)).start()
+        return unused
+
+    lax.fori_loop(1, N_XY, send_codes, 0)
     lax.fori_loop(1, N_XY, send, 0)
     at_edges(me, [up_copy], [down_copy], "start")
     got_mass[me] = send_mass[me]

time: 35.7 us -> 35.7 us (level)
  Pallas kernels: 35.4 us -> 35 us
where the time goes in v10:
time: 35.7 us; the launch traced here: 35.2 us
  Pallas kernels  35 us (98%)
    pallas_call x1, Pallas kernels, shards(): pl.pallas_call(route_kernel, name='route', out_shape=[shaped(GX, ROWS, GY...  15.7 us
    pallas_call x1, Pallas kernels, shards(): pl.pallas_call(solve_kernel, name='solve', out_shape=[shaped(GX, ROWS, GY...  14.7 us
    pallas_call x1, Pallas kernels, shards(): pl.pallas_call(deposit_kernel, name='deposit', out_shape=shaped(GX, BINS...  3.26 us
    pallas_call x1, Pallas kernels, shards(): pl.pallas_call(finish_kernel, name='finish', out_shape=shaped(ROWS, GX, G...  1.38 us

profile of v10, /device:TPU:0, one launch (start us, length us, event | category | flops | bytes accessed | tf_op | source)
XLA Modules:
  0.0 35.2 jit_solution(11910303536899374248)
XLA Ops:
  0.0 15.7 %route.1 = (f32[8,256,256]{2,1,0:T(8,128)S(1)}, f32[2,36,16,128]{3,2,1,0:T(8,128)S(1)}, f32[2,40,128]{2,1,0:T(8,128)S(1)}, f32[2,40,128]{2,1,0:T(8,128)S(1)}, s3...) custom-call(f32[256,8,256]{2,1,0:T(8,128)} %bitcast.4, ...), custom_call_target="tpu_custom_call" | custom-call | tf_op jit(solution)/shard_map/route/pallas_call | solution.py:737
  15.7 3.3 %deposit.1.total = f32[8,9,32,256]{3,2,1,0:T(8,128)S(1)} custom-call(s32[24,128]{1,0:T(8,128)S(1)} %get-tuple-element.19.starts_v, f32[2,36,16,128]{3,2,1,0:T(8,128)S(1)} %get-tuple-element.20.rows_u, f32[2,40,128]{2,1,0:T(8,128)S(1)} %get-tuple-element.21.hl_u, f32[2,40,128]{2,1,0:T(8,128)S(1)} %get-tuple-element.22.col_u), custom_call_target="tpu_custom_call" | custom-call | tf_op jit(solution)/shard_map/deposit/pallas_call | solution.py:761
  19.0 14.7 %solve.1 = (f32[8,256,256]{2,1,0:T(8,128)S(1)}, f32[5,8,256]{2,1,0:T(8,128)S(1)}, f32[5,8,256]{2,1,0:T(8,128)S(1)}) custom-call(f32[8,9,32,256]{3,2,1,0:T(8,128)S(1)} %deposit.1.total, f32[8,256,256]{2,1,0:T(8,128)S(1)} %get-tuple-element.23.first, f32[32,8,256]{2,1,0:T(8,128)} %diffusivity.3, f32[32,8,256]{2,1,0:T(8,128)} %wind.3, ...), custom_call_target="tpu_custom_call" | custom-call | tf_op jit(solution)/shard_map/solve/pallas_call | solution.py:770
  33.7 1.4 %finish.1 = f32[256,8,256]{2,1,0:T(8,128)} custom-call(f32[8,256,256]{2,1,0:T(8,128)S(1)} %get-tuple-element.30.second, f32[5,8,256]{2,1,0:T(8,128)S(1)} %get-tuple-element.31.down, f32[5,8,256]{2,1,0:T(8,128)S(1)} %get-tuple-element.32.upward, f32[256,128]{1,0:T(8,128)S(1)} %get-tuple-element.25.p_col, f32[256,128]{1,0:T(8,128)S(1)} %get-tuple-element.26.e_col), custom_call_target="tpu_custom_call" | custom-call | tf_op jit(solution)/shard_map/finish/pallas_call | solution.py:787
